TPU v7x, 32 devices: a whole 2x2x4 slice. The times are simulated.
32 devices in a mesh: section: 2 (over x), fsdp: 4 (over z), replica: 4 (over y, core).
Axes of the slice: x: 2, y: 2, z: 4, core: 2. Of those that a mesh axis runs over, the one named last changes fastest.
Arguments:
- ends: bfloat16 [2, 96, 160, 1152], P('section', ('fsdp', 'replica')), may hold values from -6 to 6
- first_gain: bfloat16 [2, 1152], P('section', 'fsdp'), may hold values from 0.5 to 1.5
- first_shift: bfloat16 [2, 1152], P('section', 'fsdp'), may hold values from -2 to 2
- qkv_weight: bfloat16 [2, 1152, 3456], P('section', 'fsdp'), may hold values from -0.1875 to 0.1875
- qv_bias: bfloat16 [2, 2, 1152], P('section', None, 'fsdp'), may hold values from -3 to 3
- out_weight: bfloat16 [2, 1152, 1152], P('section', 'fsdp'), may hold values from -0.5 to 0.5
- out_bias: bfloat16 [2, 1152], P('section', 'fsdp'), may hold values from -2 to 2
- second_gain: bfloat16 [2, 1152], P('section', 'fsdp'), may hold values from 0.5 to 1.5
- second_shift: bfloat16 [2, 1152], P('section', 'fsdp'), may hold values from -2 to 2
- up_weight: bfloat16 [2, 1152, 4304], P('section', 'fsdp'), may hold values from -0.1875 to 0.1875
- up_bias: bfloat16 [2, 4304], P('section', 'fsdp'), may hold values from -3 to 3
- down_weight: bfloat16 [2, 4304, 1152], P('section', None, 'fsdp'), may hold values from -0.09375 to 0.09375
- down_bias: bfloat16 [2, 1152], P('section', 'fsdp'), may hold values from -2 to 2
Outputs:
- result_ends: float32 [2, 96, 160, 1152], P('section', ('fsdp', 'replica'))
- grad_first_gain: float32 [2, 1152], P('section', 'fsdp')
- grad_first_shift: float32 [2, 1152], P('section', 'fsdp')
- grad_qkv_weight: float32 [2, 1152, 3456], P('section', 'fsdp')
- grad_qv_bias: float32 [2, 2, 1152], P('section', None, 'fsdp')
- grad_out_weight: float32 [2, 1152, 1152], P('section', 'fsdp')
- grad_out_bias: float32 [2, 1152], P('section', 'fsdp')
- grad_second_gain: float32 [2, 1152], P('section', 'fsdp')
- grad_second_shift: float32 [2, 1152], P('section', 'fsdp')
- grad_up_weight: float32 [2, 1152, 4304], P('section', 'fsdp')
- grad_up_bias: float32 [2, 4304], P('section', 'fsdp')
- grad_down_weight: float32 [2, 4304, 1152], P('section', None, 'fsdp')
- grad_down_bias: float32 [2, 1152], P('section', 'fsdp')
All inputs are finite; a program needn't handle non-finite values.
Results may differ from a plain program's by a relative error of at most 0.009.
Values may be sent and summed in bfloat16 or wider, within the bound.
A program may use at most 320 MiB of HBM per device.

v0:
```python
import math

import jax
import jax.numpy as jnp
from jax import lax
from jax.sharding import PartitionSpec as P

HEADS = 16
HEAD_DIM = 72
MICRO = 2


def shifted(value, axis, steps):
    count = lax.axis_size(axis)
    first, last = (max(0, -steps), min(count, count - steps))
    return lax.ppermute(value, axis, [(source, source + steps) for source in range(first, last)])


def gelu_tanh(signal):
    return (
        0.5
        * signal
        * (
            1.0
            + jnp.tanh(math.sqrt(2.0 / math.pi) * (signal + 0.044715 * signal * signal * signal))
        )
    )


def layer_norm(signal, gain, shift):
    center = signal - jnp.mean(signal, axis=-1, keepdims=True)
    spread = jnp.mean(center * center, axis=-1, keepdims=True)
    return center * lax.rsqrt(spread + 1e-06) * gain + shift


def fetch_forward(shards):
    (
        gain_one,
        shift_one,
        weight_qkv,
        bias_qv,
        weight_out,
        bias_out,
        gain_two,
        shift_two,
        weight_up,
        bias_up,
        weight_down,
        bias_down,
    ) = shards
    return (
        lax.all_gather(gain_one, "fsdp", axis=0, tiled=True),
        lax.all_gather(shift_one, "fsdp", axis=0, tiled=True),
        lax.all_gather(weight_qkv, "fsdp", axis=0, tiled=True),
        lax.all_gather(bias_qv, "fsdp", axis=1, tiled=True),
        lax.all_gather(weight_out, "fsdp", axis=0, tiled=True),
        lax.all_gather(bias_out, "fsdp", axis=0, tiled=True),
        lax.all_gather(gain_two, "fsdp", axis=0, tiled=True),
        lax.all_gather(shift_two, "fsdp", axis=0, tiled=True),
        lax.all_gather(weight_up, "fsdp", axis=0, tiled=True),
        lax.all_gather(bias_up, "fsdp", axis=0, tiled=True),
        lax.all_gather(weight_down, "fsdp", axis=1, tiled=True),
        lax.all_gather(bias_down, "fsdp", axis=0, tiled=True),
    )


def fetch_backward(shards):
    (
        gain_one,
        shift_one,
        weight_qkv,
        bias_qv,
        weight_out,
        bias_out,
        gain_two,
        shift_two,
        weight_up,
        bias_up,
        weight_down,
        bias_down,
    ) = shards
    return (
        lax.all_gather(gain_one, "fsdp", axis=0, tiled=True),
        lax.all_gather(shift_one, "fsdp", axis=0, tiled=True),
        lax.all_gather(weight_qkv, "fsdp", axis=0, tiled=True),
        lax.all_gather(bias_qv, "fsdp", axis=1, tiled=True),
        lax.all_gather(weight_out, "fsdp", axis=0, tiled=True),
        lax.all_gather(bias_out, "fsdp", axis=0, tiled=True),
        lax.all_gather(gain_two, "fsdp", axis=0, tiled=True),
        lax.all_gather(shift_two, "fsdp", axis=0, tiled=True),
        lax.all_gather(weight_up, "fsdp", axis=0, tiled=True),
        lax.all_gather(bias_up, "fsdp", axis=0, tiled=True),
        lax.all_gather(weight_down, "fsdp", axis=1, tiled=True),
        lax.all_gather(bias_down, "fsdp", axis=0, tiled=True),
    )


def reduce_shares(grads):
    (
        gain_one,
        shift_one,
        weight_qkv,
        bias_qv,
        weight_out,
        bias_out,
        gain_two,
        shift_two,
        weight_up,
        bias_up,
        weight_down,
        bias_down,
    ) = grads
    return (
        lax.psum_scatter(gain_one, "fsdp", scatter_dimension=0, tiled=True),
        lax.psum_scatter(shift_one, "fsdp", scatter_dimension=0, tiled=True),
        lax.psum_scatter(weight_qkv, "fsdp", scatter_dimension=0, tiled=True),
        lax.psum_scatter(bias_qv, "fsdp", scatter_dimension=1, tiled=True),
        lax.psum_scatter(weight_out, "fsdp", scatter_dimension=0, tiled=True),
        lax.psum_scatter(bias_out, "fsdp", scatter_dimension=0, tiled=True),
        lax.psum_scatter(gain_two, "fsdp", scatter_dimension=0, tiled=True),
        lax.psum_scatter(shift_two, "fsdp", scatter_dimension=0, tiled=True),
        lax.psum_scatter(weight_up, "fsdp", scatter_dimension=0, tiled=True),
        lax.psum_scatter(bias_up, "fsdp", scatter_dimension=0, tiled=True),
        lax.psum_scatter(weight_down, "fsdp", scatter_dimension=1, tiled=True),
        lax.psum_scatter(bias_down, "fsdp", scatter_dimension=0, tiled=True),
    )


def sum_replicas(shares):
    (
        gain_one,
        shift_one,
        weight_qkv,
        bias_qv,
        weight_out,
        bias_out,
        gain_two,
        shift_two,
        weight_up,
        bias_up,
        weight_down,
        bias_down,
    ) = shares
    return lax.psum(
        (
            gain_one,
            shift_one,
            weight_qkv,
            bias_qv,
            weight_out,
            bias_out,
            gain_two,
            shift_two,
            weight_up,
            bias_up,
            weight_down,
            bias_down,
        ),
        "replica",
    )


def attention_scores(queries, key_rows):
    raw_scores = jnp.einsum(
        "bqhc,bkhc->bhqk", queries, key_rows, preferred_element_type=jnp.float32
    )
    return raw_scores * HEAD_DIM ** (-0.5)


def layer_forward(inputs, weights):
    (
        gain_one,
        shift_one,
        weight_qkv,
        bias_qv,
        weight_out,
        bias_out,
        gain_two,
        shift_two,
        weight_up,
        bias_up,
        weight_down,
        bias_down,
    ) = weights
    batches, seq_len, model_width = inputs.shape
    normed = layer_norm(inputs, gain_one.astype(jnp.float32), shift_one.astype(jnp.float32)).astype(
        jnp.bfloat16
    )
    joined = jnp.einsum("bsd,de->bse", normed, weight_qkv, preferred_element_type=jnp.float32)
    queries = (joined[..., :model_width] + bias_qv[0].astype(jnp.float32)).astype(jnp.bfloat16)
    key_rows = joined[..., model_width : 2 * model_width].astype(jnp.bfloat16)
    values = (joined[..., 2 * model_width :] + bias_qv[1].astype(jnp.float32)).astype(jnp.bfloat16)
    heads_q = queries.reshape(batches, seq_len, HEADS, HEAD_DIM)
    heads_k = key_rows.reshape(batches, seq_len, HEADS, HEAD_DIM)
    heads_v = values.reshape(batches, seq_len, HEADS, HEAD_DIM)
    scores = attention_scores(heads_q, heads_k)
    row_top = jnp.max(scores, axis=-1, keepdims=True)
    logsum = row_top + jnp.log(jnp.sum(jnp.exp(scores - row_top), axis=-1, keepdims=True))
    attn_probs = jnp.exp(scores - logsum).astype(jnp.bfloat16)
    context = jnp.einsum("bhqk,bkhc->bqhc", attn_probs, heads_v, preferred_element_type=jnp.float32)
    context = context.reshape(batches, seq_len, model_width).astype(jnp.bfloat16)
    attn_out = jnp.einsum(
        "bsd,de->bse", context, weight_out, preferred_element_type=jnp.float32
    ) + bias_out.astype(jnp.float32)
    mixed_rows = inputs + attn_out
    normed_two = layer_norm(
        mixed_rows, gain_two.astype(jnp.float32), shift_two.astype(jnp.float32)
    ).astype(jnp.bfloat16)
    pre_act = jnp.einsum(
        "bsd,df->bsf", normed_two, weight_up, preferred_element_type=jnp.float32
    ) + bias_up.astype(jnp.float32)
    activated = gelu_tanh(pre_act).astype(jnp.bfloat16)
    branch = jnp.einsum(
        "bsf,fd->bsd", activated, weight_down, preferred_element_type=jnp.float32
    ) + bias_down.astype(jnp.float32)
    result = mixed_rows + branch
    saved_acts = (
        inputs,
        normed,
        queries,
        key_rows,
        values,
        logsum,
        context,
        mixed_rows,
        normed_two,
        pre_act,
        activated,
    )
    return (result, saved_acts)


def layer_backward(grad_out, saved_acts, weights):
    (
        gain_one,
        shift_one,
        weight_qkv,
        bias_qv,
        weight_out,
        bias_out,
        gain_two,
        shift_two,
        weight_up,
        bias_up,
        weight_down,
        bias_down,
    ) = weights
    (
        inputs,
        normed,
        queries,
        key_rows,
        values,
        logsum,
        context,
        mixed_rows,
        normed_two,
        pre_act,
        activated,
    ) = saved_acts
    batches, seq_len, model_width = inputs.shape
    sum_axes = (0, 1)
    grad_branch = grad_out.astype(jnp.bfloat16)
    g_down_weight = jnp.einsum(
        "bsf,bsd->fd", activated, grad_branch, preferred_element_type=jnp.float32
    )
    g_down_bias = jnp.sum(grad_branch.astype(jnp.float32), axis=sum_axes)
    grad_act = jnp.einsum(
        "bsd,fd->bsf", grad_branch, weight_down, preferred_element_type=jnp.float32
    )
    gelu_pull = jax.vjp(gelu_tanh, pre_act)[1]
    grad_pre = gelu_pull(grad_act)[0].astype(jnp.bfloat16)
    g_up_weight = jnp.einsum(
        "bsd,bsf->df", normed_two, grad_pre, preferred_element_type=jnp.float32
    )
    g_up_bias = jnp.sum(grad_pre.astype(jnp.float32), axis=sum_axes)
    grad_normed_two = jnp.einsum(
        "bsf,df->bsd", grad_pre, weight_up, preferred_element_type=jnp.float32
    )
    norm_pull = jax.vjp(
        layer_norm, mixed_rows, gain_two.astype(jnp.float32), shift_two.astype(jnp.float32)
    )[1]
    grad_mix_part, g_second_gain, g_second_shift = norm_pull(grad_normed_two)
    grad_mixed = grad_out + grad_mix_part
    grad_attn = grad_mixed.astype(jnp.bfloat16)
    g_out_weight = jnp.einsum("bsd,bse->de", context, grad_attn, preferred_element_type=jnp.float32)
    g_out_bias = jnp.sum(grad_attn.astype(jnp.float32), axis=sum_axes)
    grad_context = jnp.einsum(
        "bse,de->bsd", grad_attn, weight_out, preferred_element_type=jnp.float32
    ).astype(jnp.bfloat16)
    heads_q = queries.reshape(batches, seq_len, HEADS, HEAD_DIM)
    heads_k = key_rows.reshape(batches, seq_len, HEADS, HEAD_DIM)
    heads_v = values.reshape(batches, seq_len, HEADS, HEAD_DIM)
    grad_heads = grad_context.reshape(batches, seq_len, HEADS, HEAD_DIM)
    probs_full = jnp.exp(attention_scores(heads_q, heads_k) - logsum)
    probs_low = probs_full.astype(jnp.bfloat16)
    grad_probs = jnp.einsum(
        "bqhc,bkhc->bhqk", grad_heads, heads_v, preferred_element_type=jnp.float32
    )
    grad_values = jnp.einsum(
        "bhqk,bqhc->bkhc", probs_low, grad_heads, preferred_element_type=jnp.float32
    )
    row_total = jnp.sum(probs_full * grad_probs, axis=-1, keepdims=True)
    grad_scores = (probs_full * (grad_probs - row_total)).astype(jnp.bfloat16)
    score_scale = HEAD_DIM ** (-0.5)
    grad_queries = (
        jnp.einsum("bhqk,bkhc->bqhc", grad_scores, heads_k, preferred_element_type=jnp.float32)
        * score_scale
    )
    grad_keys = (
        jnp.einsum("bhqk,bqhc->bkhc", grad_scores, heads_q, preferred_element_type=jnp.float32)
        * score_scale
    )
    grad_joined = jnp.concatenate(
        [
            grad_queries.reshape(batches, seq_len, model_width),
            grad_keys.reshape(batches, seq_len, model_width),
            grad_values.reshape(batches, seq_len, model_width),
        ],
        axis=-1,
    ).astype(jnp.bfloat16)
    joined_wide = grad_joined.astype(jnp.float32)
    g_qv_bias = jnp.stack(
        [
            jnp.sum(joined_wide[..., :model_width], axis=sum_axes),
            jnp.sum(joined_wide[..., 2 * model_width :], axis=sum_axes),
        ]
    )
    g_qkv_weight = jnp.einsum(
        "bsd,bse->de", normed, grad_joined, preferred_element_type=jnp.float32
    )
    grad_normed = jnp.einsum(
        "bse,de->bsd", grad_joined, weight_qkv, preferred_element_type=jnp.float32
    )
    first_pull = jax.vjp(
        layer_norm, inputs, gain_one.astype(jnp.float32), shift_one.astype(jnp.float32)
    )[1]
    grad_in_part, g_first_gain, g_first_shift = first_pull(grad_normed)
    grad_inputs = grad_mixed + grad_in_part
    grads = (
        g_first_gain,
        g_first_shift,
        g_qkv_weight,
        g_qv_bias,
        g_out_weight,
        g_out_bias,
        g_second_gain,
        g_second_shift,
        g_up_weight,
        g_up_bias,
        g_down_weight,
        g_down_bias,
    )
    return (grad_inputs, grads)


def on_device(
    ends,
    first_gain,
    first_shift,
    qkv_weight,
    qv_bias,
    out_weight,
    out_bias,
    second_gain,
    second_shift,
    up_weight,
    up_bias,
    down_weight,
    down_bias,
):
    shards = tuple(
        (
            item[0]
            for item in (
                first_gain,
                first_shift,
                qkv_weight,
                qv_bias,
                out_weight,
                out_bias,
                second_gain,
                second_shift,
                up_weight,
                up_bias,
                down_weight,
                down_bias,
            )
        )
    )
    section_idx = lax.axis_index("section")
    at_first = section_idx == 0
    boundary = ends[0].astype(jnp.float32)
    images = boundary.shape[0]
    per_micro = images // MICRO
    pieces = [
        boundary[micro_index * per_micro : (micro_index + 1) * per_micro]
        for micro_index in range(MICRO)
    ]
    received = jnp.zeros_like(pieces[0])
    saved_steps = []
    outputs = []
    for moment in range(MICRO + 1):
        weights = fetch_forward(shards)
        source = pieces[min(moment, MICRO - 1)]
        inputs = jnp.where(at_first, source, received)
        result, saved_acts = layer_forward(inputs, weights)
        saved_steps.append(saved_acts)
        outputs.append(result)
        if moment < MICRO:
            received = shifted(result.astype(jnp.bfloat16), "section", 1).astype(jnp.float32)
    stacked = tuple((jnp.stack(items) for items in zip(*saved_steps)))
    back_received = jnp.zeros_like(pieces[0])
    totals = None
    shares = None
    in_grads = []
    for moment in range(MICRO + 1):
        weights = fetch_backward(shards)
        slot_index = jnp.clip(moment - 1 + 2 * section_idx, 0, MICRO)
        saved_acts = tuple(
            (lax.dynamic_index_in_dim(item, slot_index, 0, keepdims=False) for item in stacked)
        )
        micro_index = moment - 1 + section_idx
        live_mask = ((micro_index >= 0) & (micro_index < MICRO)).astype(jnp.float32)
        grad_out = jnp.where(at_first, back_received, pieces[min(moment, MICRO - 1)]) * live_mask
        grad_inputs, grads = layer_backward(grad_out, saved_acts, weights)
        in_grads.append(grad_inputs)
        if moment < MICRO:
            back_received = shifted(grad_inputs.astype(jnp.bfloat16), "section", -1).astype(
                jnp.float32
            )
        totals = (
            grads if totals is None else tuple((left + right for left, right in zip(totals, grads)))
        )
    shares = reduce_shares(totals)
    summed = sum_replicas(shares)
    grad_rows = jnp.concatenate(in_grads[1:], axis=0)
    out_rows = jnp.concatenate(outputs[1:], axis=0)
    result_ends = jnp.where(at_first, grad_rows, out_rows)[None]
    (
        g_first_gain,
        g_first_shift,
        g_qkv_weight,
        g_qv_bias,
        g_out_weight,
        g_out_bias,
        g_second_gain,
        g_second_shift,
        g_up_weight,
        g_up_bias,
        g_down_weight,
        g_down_bias,
    ) = summed
    return (
        result_ends,
        g_first_gain[None],
        g_first_shift[None],
        g_qkv_weight[None],
        g_qv_bias[None],
        g_out_weight[None],
        g_out_bias[None],
        g_second_gain[None],
        g_second_shift[None],
        g_up_weight[None],
        g_up_bias[None],
        g_down_weight[None],
        g_down_bias[None],
    )


def solution(mesh):
    placed = (
        P("section", ("fsdp", "replica"), None, None),
        P("section", "fsdp"),
        P("section", "fsdp"),
        P("section", "fsdp", None),
        P("section", None, "fsdp"),
        P("section", "fsdp", None),
        P("section", "fsdp"),
        P("section", "fsdp"),
        P("section", "fsdp"),
        P("section", "fsdp", None),
        P("section", "fsdp"),
        P("section", None, "fsdp"),
        P("section", "fsdp"),
    )
    return jax.shard_map(
        on_device,
        mesh=mesh,
        in_specs=placed,
        out_specs=(
            P("section", ("fsdp", "replica"), None, None),
            P("section", "fsdp"),
            P("section", "fsdp"),
            P("section", "fsdp", None),
            P("section", None, "fsdp"),
            P("section", "fsdp", None),
            P("section", "fsdp"),
            P("section", "fsdp"),
            P("section", "fsdp"),
            P("section", "fsdp", None),
            P("section", "fsdp"),
            P("section", None, "fsdp"),
            P("section", "fsdp"),
        ),
        check_vma=False,
    )
```

profile of v0, /device:TPU:1, one launch (start us, length us, event | category | flops | bytes accessed | tf_op | source)
XLA Modules:
  0.0 2406.2 jit_solution(11743479714890755642)
XLA Ops:
  13.9 17.5 all-reduce.17
  34.1 28.1 %all-gather.3 = bf16[1,2,1152]{1,0,2:T(2,128)(2,1)S(1)} all-gather(bf16[1,2,288]{1,0,2:T(2,128)(2,1)S(1)} %copy.189), channel_id=5, replica_groups=mesh['section'=2,'fsdp'=4,'replica'=4] {'fsdp'}, dimensions={2}, use_global_device_ids=true | all-gather | bytes 5760 | tf_op jit(solution)/shard_map/all_gather | solution.py:55
  64.6 18.6 fusion.207
  83.2 81.5 %all-gather.17.cloned.1.call-done = bf16[1,1152,3456]{2,1,0:T(8,128)(2,1)} async-done(((bf16[1,288,3456]{2,1,0:T(8,128)(2,1)}), bf16[1,1152,3456]{2,1,0:T(8,128)(2,1)}) %all-gather.17.cloned.1.call-update) | async-done | bytes 7962640 | tf_op jit(solution)/shard_map/all_gather | solution.py:54
  194.0 25.8 %all-gather.19.cloned.1.call-done = bf16[1,1152,1152]{2,1,0:T(8,128)(2,1)} async-done(((bf16[1,288,1152]{2,1,0:T(8,128)(2,1)}), bf16[1,1152,1152]{2,1,0:T(8,128)(2,1)}) %all-gather.19.cloned.1.call-update) | async-done | bytes 2654224 | tf_op jit(solution)/shard_map/all_gather | solution.py:56
  225.9 171.0 %all-gather.21.cloned.1.call-done = bf16[1,1152,4304]{2,1,0:T(8,128)(2,1)} async-done(((bf16[1,288,4304]{2,1,0:T(8,128)(2,1)}), bf16[1,1152,4304]{2,1,0:T(8,128)(2,1)}) %all-gather.21.cloned.1.call-update) | async-done | bytes 9916432 | tf_op jit(solution)/shard_map/all_gather | solution.py:60
  409.1 163.8 %all-gather.23.cloned.1.call-done = bf16[1,4304,1152]{1,2,0:T(8,128)(2,1)} async-done(((bf16[1,4304,288]{1,2,0:T(8,128)(2,1)}), bf16[1,4304,1152]{1,2,0:T(8,128)(2,1)}) %all-gather.23.cloned.1.call-update) | async-done | bytes 9916432 | tf_op jit(solution)/shard_map/all_gather | solution.py:62
  588.3 23.5 collective-permute-done
  677.9 16.8 collective-permute-done.1
  747.3 16.8 pad_maximum_fusion
  764.1 15.8 convert_reduce_fusion.2
  906.8 14.9 convert_reduce_fusion.1
  993.9 16.5 collective-permute-done.3
  1011.4 14.6 convert_reduce_fusion
  1151.3 13.9 fusion.3
  1165.2 18.3 fusion.2
  1212.3 18.4 fusion.1
  1230.7 18.3 fusion
  1257.7 163.6 %reduce-scatter.8.cloned.1.call-done = f32[288,3456]{1,0:T(8,128)} async-done(((f32[1152,3456]{1,0:T(8,128)}), f32[288,3456]{1,0:T(8,128)}) %reduce-scatter.8.cloned.1.call-update) | async-done | bytes 3981328 | tf_op jit(solution)/shard_map/reduce_scatter | solution.py:116
  1421.3 335.6 %reduce-scatter.12.cloned.1.call-done = f32[288,4304]{1,0:T(8,128)} async-done(((f32[1152,4304]{1,0:T(8,128)}), f32[288,4304]{1,0:T(8,128)}) %reduce-scatter.12.cloned.1.call-update) | async-done | bytes 4958224 | tf_op jit(solution)/shard_map/reduce_scatter | solution.py:122
  1756.9 336.3 %reduce-scatter.14.cloned.1.call-done = f32[4304,288]{0,1:T(8,128)} async-done(((f32[4304,1152]{0,1:T(8,128)}), f32[4304,288]{0,1:T(8,128)}) %reduce-scatter.14.cloned.1.call-update) | async-done | bytes 4958224 | tf_op jit(solution)/shard_map/reduce_scatter | solution.py:124
  2107.8 18.2 all-reduce.16
  2134.7 14.2 all-reduce.14
  2148.9 238.8 %all-reduce.20.cloned.1.call-done = (f32[1,288,3456]{2,1,0:T(8,128)}, f32[1,288,1152]{2,1,0:T(8,128)}, f32[1,288,4304]{2,1,0:T(8,128)}, f32[1,4304,288]{1,2,0:T(8,128)}) async-done(((f32[1,288,3456]{2,1,0:T(8,128)}, f32[1,288,1152]{2,1,0:T(8,128)}, f32[1,288,4304]{2,1,0:T(8,128)}, f32[1,4304,288]{1,2,0:T(8,128)}), (f32[1,288,3456]{2,1,0:T(8,128)}, f32[1,288,1152]{2,1,0:T(8,128)}, f32[1,288,4304]{2,1,0:T(8,128)}, ...) | async-done | bytes 15224848 | tf_op jit(solution)/shard_map/psum | solution.py:144
  (701 shorter events, 585.6 us)
Async XLA Ops:
  7.2 157.6 %all-gather.17.cloned.1.call-start = ((), (), s32[]{:S(2)}) async-start(), calls=%async_computation.9 | async-start | bytes 9953280 | tf_op jit(solution)/shard_map/all_gather | solution.py:54
  7.9 211.9 %all-gather.19.cloned.1.call-start = ((), (), s32[]{:S(2)}) async-start(), calls=%async_computation.10 | async-start | bytes 3317760 | tf_op jit(solution)/shard_map/all_gather | solution.py:56
  8.8 388.1 %all-gather.21.cloned.1.call-start = ((), (), s32[]{:S(2)}) async-start(), calls=%async_computation.11 | async-start | bytes 12533760 | tf_op jit(solution)/shard_map/all_gather | solution.py:60
  9.5 563.4 %all-gather.23.cloned.1.call-start = ((), (), s32[]{:S(2)}) async-start(), calls=%async_computation.12 | async-start | bytes 12533760 | tf_op jit(solution)/shard_map/all_gather | solution.py:62
  10.1 1247.6 %reduce-scatter.10.cloned.1.call-start = ((), (), s32[]{:S(2)}) async-start(), calls=%async_computation.6 | async-start | bytes 6635520 | tf_op jit(solution)/shard_map/reduce_scatter | solution.py:118
  31.4 665.8 %copy-start.123 = (f32[1152]{0:T(1024)}, f32[1152]{0:T(1024)S(1)}, u32[]{:S(2)}) copy-start(f32[1152]{0:T(1024)S(1)} %convert_element_type.407) | copy-start | bytes 13828
  31.5 665.8 %copy-start.101 = (f32[1152]{0:T(1024)}, f32[1152]{0:T(1024)S(1)}, u32[]{:S(2)}) copy-start(f32[1152]{0:T(1024)S(1)} %convert_element_type.406) | copy-start | bytes 13828
  34.1 621.5 %copy-start.149 = (f32[1152]{0:T(1024)}, f32[1152]{0:T(1024)S(1)}, u32[]{:S(2)}) copy-start(f32[1152]{0:T(1024)S(1)} %convert_element_type.412) | copy-start | bytes 13828
  64.1 155.7 %copy-start.5 = (f32[1,3,160,1152]{3,2,1,0:T(8,128)}, f32[1,3,160,1152]{3,2,1,0:T(8,128)S(1)}, u32[]{:S(2)}) copy-start(f32[1,3,160,1152]{3,2,1,0:T(8,128)S(1)} %get-tuple-element.101) | copy-start | bytes 6635524
  64.1 108.1 %copy-start.108 = (f32[3,160]{1,0:T(4,128)}, f32[3,160]{1,0:T(4,128)S(1)}, u32[]{:S(2)}) copy-start(f32[3,160]{1,0:T(4,128)S(1)} %broadcast_multiply_fusion.11) | copy-start | bytes 5764
  64.6 107.7 %copy-start.138 = (f32[3,160]{1,0:T(4,128)}, f32[3,160]{1,0:T(4,128)S(1)}, u32[]{:S(2)}) copy-start(f32[3,160]{1,0:T(4,128)S(1)} %add_rsqrt_fusion.5) | copy-start | bytes 5764
  224.1 185.0 %copy-start.115 = (f32[3,160]{1,0:T(4,128)}, f32[3,160]{1,0:T(4,128)S(1)}, u32[]{:S(2)}) copy-start(f32[3,160]{1,0:T(4,128)S(1)} %broadcast_multiply_fusion.10) | copy-start | bytes 5764
  225.8 183.2 %copy-start.144 = (f32[3,160]{1,0:T(4,128)}, f32[3,160]{1,0:T(4,128)S(1)}, u32[]{:S(2)}) copy-start(f32[3,160]{1,0:T(4,128)S(1)} %add_rsqrt_fusion.4) | copy-start | bytes 5764
  225.9 347.1 %copy-start.17 = (f32[3,160,1152]{2,1,0:T(8,128)S(1)}, f32[3,160,1152]{2,1,0:T(8,128)}, u32[]{:S(2)}) copy-start(f32[3,160,1152]{2,1,0:T(8,128)} %copy-done.16) | copy-start | bytes 6635524
  585.2 26.7 %collective-permute-start = (bf16[3,160,1152]{2,1,0:T(8,128)(2,1)}, bf16[3,160,1152]{2,1,0:T(8,128)(2,1)S(1)}, u32[]{:S(2)}, u32[]{:S(2)}) collective-permute-start(bf16[3,160,1152]{2,1,0:T(8,128)(2,1)} %fusion.158), channel_id=1, source_target_pairs={{0,16},{1,17},{2,18},{3,19},{4,20},{5,21},{6,22},{7,23},{8,24},{9,... | collective-permute-start | bytes 3317768 | tf_op jit(solution)/shard_map/ppermute | solution.py:16
  613.8 114.6 %copy-start.3 = (f32[3,160,1152]{2,1,0:T(8,128)}, f32[3,160,1152]{2,1,0:T(8,128)S(1)}, u32[]{:S(2)}) copy-start(f32[3,160,1152]{2,1,0:T(8,128)S(1)} %get-tuple-element.99) | copy-start | bytes 6635524
  668.4 26.4 %collective-permute-start.1 = (bf16[3,160,1152]{2,1,0:T(8,128)(2,1)S(1)}, bf16[3,160,1152]{2,1,0:T(8,128)(2,1)S(1)}, u32[]{:S(2)}, u32[]{:S(2)}) collective-permute-start(bf16[3,160,1152]{2,1,0:T(8,128)(2,1)S(1)} %get-tuple-element.151), channel_id=1, source_target_pairs={{0,16},{1,17},{2,18},{3,19},{4,20},{5,21},{6,22},{7,23},{8,24},{9,... | collective-permute-start | bytes 3317768 | tf_op jit(solution)/shard_map/ppermute | solution.py:16
  871.9 31.8 %collective-permute-start.2 = (bf16[3,160,1152]{2,1,0:T(8,128)(2,1)}, bf16[3,160,1152]{2,1,0:T(8,128)(2,1)}, u32[]{:S(2)}, u32[]{:S(2)}) collective-permute-start(bf16[3,160,1152]{2,1,0:T(8,128)(2,1)} %add_convert_fusion), channel_id=1, source_target_pairs={{16,0},{17,1},{18,2},{19,3},{20,4},{21,5},{22,6},{23,7},{24,8},{25... | collective-permute-start | bytes 3317768 | tf_op jit(solution)/shard_map/ppermute | solution.py:16
  983.3 27.1 %collective-permute-start.3 = (bf16[3,160,1152]{2,1,0:T(8,128)(2,1)S(1)}, bf16[3,160,1152]{2,1,0:T(8,128)(2,1)S(1)}, u32[]{:S(2)}, u32[]{:S(2)}) collective-permute-start(bf16[3,160,1152]{2,1,0:T(8,128)(2,1)S(1)} %get-tuple-element.109), channel_id=1, source_target_pairs={{16,0},{17,1},{18,2},{19,3},{20,4},{21,5},{22,6},{23,7},{24,8},{25... | collective-permute-start | bytes 3317768 | tf_op jit(solution)/shard_map/ppermute | solution.py:16
  1056.7 364.6 %reduce-scatter.8.cloned.1.call-start = ((), (), s32[]{:S(2)}) async-start(), calls=%async_computation.5 | async-start | bytes 19906560 | tf_op jit(solution)/shard_map/reduce_scatter | solution.py:116
  1137.0 619.9 %reduce-scatter.12.cloned.1.call-start = ((), (), s32[]{:S(2)}) async-start(), calls=%async_computation.7 | async-start | bytes 25067520 | tf_op jit(solution)/shard_map/reduce_scatter | solution.py:122
  1183.5 909.6 %reduce-scatter.14.cloned.1.call-start = ((), (), s32[]{:S(2)}) async-start(), calls=%async_computation.8 | async-start | bytes 25067520 | tf_op jit(solution)/shard_map/reduce_scatter | solution.py:124
  1249.1 884.6 %reduce-scatter.16.cloned.1.call-start = ((), (), s32[]{:S(2)}) async-start(), calls=%async_computation.13 | async-start | bytes 737280
  1257.6 1130.0 %all-reduce.20.cloned.1.call-start = ((), (), s32[]{:S(2)}) async-start(), calls=%async_computation.14 | async-start | bytes 30670848 | tf_op jit(solution)/shard_map/psum | solution.py:144
  (198 other events, 1518.6 us)
Sparse Core Ops, SparseCore 0:
  9.6 155.1 all-gather.16
  166.3 53.4 all-gather.18
  221.4 175.4 all-gather.20
  398.3 174.6 all-gather.22
  1056.8 94.3 reduce-scatter.9
  1153.5 267.6 reduce-scatter.7
  1423.7 333.1 reduce-scatter.11
  1759.3 333.8 reduce-scatter.13
  2096.0 21.7 reduce-scatter.15
  2120.4 267.2 all-reduce.19
where the time goes:
time: 2410 us
  waiting for transfers between devices  1580 us (66%)
  matrix products  426 us (18%)
  local copies, waits for them, and re-layouts  152 us (6%)
  other arithmetic  144 us (6%)
  blocking collectives  78 us (3%)
    reduce_scatter x1, waiting for transfers between devices, reduce_shares(): lax.psum_scatter(weight_down, 'fsdp', scatter_dimension=1, tiled=True)  336 us
    reduce_scatter x1, waiting for transfers between devices, reduce_shares(): lax.psum_scatter(weight_up, 'fsdp', scatter_dimension=0, tiled=True)  336 us
    psum x1, waiting for transfers between devices, sum_replicas(): lax.psum((gain_one, shift_one, weight_qkv, bias_qv, weight_out, bias_out,...  239 us
    all_gather x1, waiting for transfers between devices, fetch_forward(): lax.all_gather(weight_up, 'fsdp', axis=0, tiled=True)  171 us
    all_gather x1, waiting for transfers between devices, fetch_forward(): lax.all_gather(weight_down, 'fsdp', axis=1, tiled=True)  164 us
    reduce_scatter x1, waiting for transfers between devices, reduce_shares(): lax.psum_scatter(weight_qkv, 'fsdp', scatter_dimension=0, tiled=True)  164 us
    all_gather x1, waiting for transfers between devices, fetch_forward(): lax.all_gather(weight_qkv, 'fsdp', axis=0, tiled=True)  81.5 us
    ppermute x4, waiting for transfers between devices, shifted(): lax.ppermute(value, axis, [(source, source + steps) for source in range(f...  56.8 us
  transfers between devices with their start and end apart: 14, of which 11 were waited for; matrix products, arithmetic and copies ran while one was open for 13% of the time, Pallas kernels for 0%

commit v1 on v0

--- a/solution.py
+++ b/solution.py
@@ -1,13 +1,443 @@
+import functools
 import math
 
 import jax
 import jax.numpy as jnp
 from jax import lax
+from jax.experimental import pallas as pl
+from jax.experimental.pallas import tpu as pltpu
 from jax.sharding import PartitionSpec as P
 
+MESH = pl.DeviceIdType.MESH
 HEADS = 16
 HEAD_DIM = 72
 MICRO = 2
+
+
+def powers(count):
+    bits = []
+    bit = count // 2
+    while bit:
+        bits.append(bit)
+        bit //= 2
+    return bits
+
+def gather_kernel(n, R, qkv, out, up, down, small, G, S, stage, stage_small, lsem, ssem, rsem, small_send, small_recv):
+    z = lax.axis_index("fsdp")
+    r = lax.axis_index("replica")
+    rows, wide = up.shape
+    part = wide // R
+    bits = powers(R)
+    barrier = pltpu.get_barrier_semaphore()
+    for hop in range(1, n):
+        pl.semaphore_signal(barrier, inc=1, device_id={"fsdp": lax.rem(z + hop, n)}, device_id_type=MESH)
+    for bit in bits:
+        pl.semaphore_signal(barrier, inc=1, device_id={"replica": r ^ bit}, device_id_type=MESH)
+    mine = pl.ds(pl.multiple_of(z * rows, 16), rows)
+    first = qkv.shape[1]
+    local = [
+        pltpu.make_async_copy(qkv, stage.at[0, :, pl.ds(0, first)], lsem.at[0]),
+        pltpu.make_async_copy(out, stage.at[0, :, pl.ds(first, out.shape[1])], lsem.at[1]),
+        pltpu.make_async_copy(up, stage.at[1], lsem.at[2]),
+        pltpu.make_async_copy(down, stage.at[2], lsem.at[3]),
+        pltpu.make_async_copy(small, stage_small, lsem.at[4]),
+    ]
+    for copy in local:
+        copy.start()
+    keep = [pltpu.make_async_copy(stage.at[group], G.at[group, mine], lsem.at[5 + group]) for group in range(3)]
+    keep.append(pltpu.make_async_copy(stage_small, S.at[z], lsem.at[8]))
+    pl.semaphore_wait(barrier, n - 1 + len(bits))
+
+    def piece(group, source, column):
+        return G.at[group, pl.ds(pl.multiple_of(source * rows, 16), rows),
+                    pl.ds(pl.multiple_of(column * part, 128), part)]
+
+    def send(group, source, column, kind, target, origin=None):
+        return pltpu.make_async_remote_copy(
+            src_ref=piece(group, source, column) if origin is None else origin, dst_ref=piece(group, source, column),
+            send_sem=ssem.at[group, source, column, kind], recv_sem=rsem.at[group, source, column],
+            device_id=target, device_id_type=MESH)
+
+    def to_right(group, source, origin=None):
+        return send(group, source, r, 0, {"fsdp": z + 1}, origin)
+
+    def to_left(group, source, origin=None):
+        return send(group, source, r, 1, {"fsdp": z - 1}, origin)
+
+    def own(group):
+        return stage.at[group, :, pl.ds(pl.multiple_of(r * part, 128), part)]
+
+    def share(group, source, column, level):
+        return send(group, source, column, 2 + level, {"replica": r ^ bits[level]})
+
+    def arrived(group, source, column):
+        send(group, source, column, 0, {"replica": r ^ bits[0]}).wait_recv()
+
+    def small_to(hop):
+        return pltpu.make_async_remote_copy(
+            src_ref=small, dst_ref=S.at[z], send_sem=small_send.at[hop],
+            recv_sem=small_recv.at[z], device_id={"fsdp": lax.rem(z + hop, n)}, device_id_type=MESH)
+    for hop in range(1, n):
+        small_to(hop).start()
+    for group in range(3):
+        if group == 0:
+            local[0].wait()
+            local[1].wait()
+        else:
+            local[1 + group].wait()
+        @pl.when(z + 1 < n)
+        def _():
+            to_right(group, z, own(group)).start()
+        @pl.when(z > 0)
+        def _():
+            to_left(group, z, own(group)).start()
+        keep[group].start()
+    local[4].wait()
+    keep[3].start()
+    columns = {}
+    for level, bit in enumerate(bits):
+        masks = [0]
+        for upper in bits[:level]:
+            masks = masks + [m | upper for m in masks]
+        columns[level] = [bit | m for m in masks]
+    steps = [(hop, group) for hop in range(1, n) for group in range(3)]
+    for turn in range(len(steps) + len(bits)):
+        for level in range(-1, len(bits)):
+            place = turn - 1 - level
+            if place < 0 or place >= len(steps):
+                continue
+            hop, group = steps[place]
+            for sign in (-1, 1):
+                source = z + sign * hop
+                @pl.when((source >= 0) & (source < n))
+                def _():
+                    if level < 0:
+                        arrived(group, source, r)
+                        for lower in range(len(bits)):
+                            share(group, source, r, lower).start()
+                        if sign < 0:
+                            @pl.when(z + 1 < n)
+                            def _():
+                                to_right(group, source).start()
+                        else:
+                            @pl.when(z > 0)
+                            def _():
+                                to_left(group, source).start()
+                    else:
+                        for mask in columns[level]:
+                            arrived(group, source, r ^ mask)
+                            for lower in range(level + 1, len(bits)):
+                                share(group, source, r ^ mask, lower).start()
+    for copy in keep:
+        copy.wait()
+    for hop in range(1, n):
+        pltpu.make_async_remote_copy(
+            src_ref=small, dst_ref=S.at[lax.rem(z + hop, n)], send_sem=small_send.at[hop],
+            recv_sem=small_recv.at[lax.rem(z + hop, n)], device_id={"fsdp": lax.rem(z + hop, n)}, device_id_type=MESH).wait_recv()
+        small_to(hop).wait_send()
+    for group in range(3):
+        for source in range(n):
+            @pl.when((source <= z) & (z + 1 < n))
+            def _():
+                to_right(group, source).wait_send()
+            @pl.when((source >= z) & (z > 0))
+            def _():
+                to_left(group, source).wait_send()
+            @pl.when(source != z)
+            def _():
+                for level in range(len(bits)):
+                    share(group, source, r, level).wait_send()
+                for level in range(len(bits)):
+                    for mask in columns[level]:
+                        for lower in range(level + 1, len(bits)):
+                            share(group, source, r ^ mask, lower).wait_send()
+
+def gather_weights(n, R, qkv, out, up, down, small):
+    rows, wide = up.shape
+    kinds = 2 + len(powers(R))
+    return pl.pallas_call(
+        functools.partial(gather_kernel, n, R),
+        out_shape=(jax.ShapeDtypeStruct((3, n * rows, wide), qkv.dtype),
+                   jax.ShapeDtypeStruct((n,) + small.shape, small.dtype)),
+        in_specs=[pl.BlockSpec(memory_space=pl.ANY)] * 5,
+        out_specs=(pl.BlockSpec(memory_space=pl.ANY),) * 2,
+        scratch_shapes=[
+            pltpu.VMEM((3, rows, wide), qkv.dtype),
+            pltpu.VMEM(small.shape, small.dtype),
+            pltpu.SemaphoreType.DMA((9,)),
+            pltpu.SemaphoreType.DMA((3, n, R, kinds)),
+            pltpu.SemaphoreType.DMA((3, n, R)),
+            pltpu.SemaphoreType.DMA((n,)),
+            pltpu.SemaphoreType.DMA((n,)),
+        ],
+        compiler_params=pltpu.CompilerParams(collective_id=0, has_side_effects=True, vmem_limit_bytes=32 * 1024 * 1024),
+    )(qkv, out, up, down, small)
+
+
+def reduce_kernel(n, R, sub, small_in, a_in, u_in, d_in, F, small_out, *scratch):
+    bits = []
+    while (1 << len(bits)) < R:
+        bits.append(1 << len(bits))
+    L = len(bits)
+    held = scratch[:L]
+    (xv, flow, small_z, small_r, small_sum, xsem, send_sem, recv_sem, zsend, zrecv, fsend, frecv, fkeep,
+     ss_z, sr_z, ss_r, sr_r, ss_l) = scratch[L:]
+    z = lax.axis_index("fsdp")
+    r = lax.axis_index("replica")
+    inputs = (a_in, u_in, d_in)
+    full = a_in.shape[0]
+    rows = full // n
+    wide = a_in.shape[1]
+    part = wide // R
+    subs = part // sub
+    K = 3 * subs
+    barrier = pltpu.get_barrier_semaphore()
+    for hop in range(1, n):
+        pl.semaphore_signal(barrier, inc=1, device_id={"fsdp": lax.rem(z + hop, n)}, device_id_type=MESH)
+    for hop in range(1, R):
+        pl.semaphore_signal(barrier, inc=1, device_id={"replica": lax.rem(r + hop, R)}, device_id_type=MESH)
+
+    def columns(k, p):
+        return pl.ds(pl.multiple_of(p * part + (k % subs) * sub, 128), sub)
+
+    def block(t):
+        return pl.ds(pl.multiple_of(t * rows, 16), rows)
+
+    def low(level):
+        return r & ((1 << level) - 1)
+
+    def kept(level, j):
+        return low(level + 1) | (j << (level + 1))
+
+    def load(k, j):
+        return pltpu.make_async_copy(inputs[k // subs].at[:, columns(k, kept(0, j))], xv.at[k % 2, j], xsem.at[k % 2, j])
+
+    def give(level, k, j):
+        if level == 0:
+            source = inputs[k // subs].at[:, columns(k, (r ^ 1) & 1 | (j << 1))]
+        else:
+            source = held[level - 1].at[k, 2 * j + (((r >> level) & 1) ^ 1)]
+        return pltpu.make_async_remote_copy(
+            src_ref=source, dst_ref=held[level].at[k, j], send_sem=send_sem.at[level, k, j],
+            recv_sem=recv_sem.at[level, k, j], device_id={"replica": r ^ bits[level]}, device_id_type=MESH)
+
+    STEP = 96 if full % 96 == 0 else 16
+
+    def start(k):
+        for j in range(R // 2):
+            give(0, k, j).start()
+            load(k, j).start()
+
+    def merge(level, k):
+        for j in range(R >> (level + 1)):
+            give(level, k, j).wait_recv()
+            if level == 0:
+                load(k, j).wait()
+            mine = held[level].at[k, j]
+            other = xv.at[k % 2, j] if level == 0 else held[level - 1].at[k, 2 * j + ((r >> level) & 1)]
+            def body(i, c):
+                at = pl.ds(pl.multiple_of(i * STEP, 16), STEP)
+                mine[at, :] = (mine[at, :].astype(jnp.float32) + other[at, :].astype(jnp.float32)).astype(mine.dtype)
+                return c
+            lax.fori_loop(0, full // STEP, body, 0)
+        if level + 1 < L:
+            for j in range(R >> (level + 2)):
+                give(level + 1, k, j).start()
+
+    def pass_on(k, t, side, source):
+        return pltpu.make_async_remote_copy(
+            src_ref=source, dst_ref=flow.at[k, side, t], send_sem=zsend.at[k, side, t], recv_sem=zrecv.at[k, side, t],
+            device_id={"fsdp": z + 1 if side == 0 else z - 1}, device_id_type=MESH)
+
+    def launch(k):
+        total = held[L - 1].at[k, 0]
+        @pl.when(z == 0)
+        def _():
+            for t in range(n - 1, 0, -1):
+                pass_on(k, t, 0, total.at[block(t)]).start()
+        @pl.when(z == n - 1)
+        def _():
+            for t in range(n - 1):
+                pass_on(k, t, 1, total.at[block(t)]).start()
+
+    RSTEP = 96 if rows % 96 == 0 else 16
+
+    def add_block(target, other, at_other):
+        def body(i, c):
+            at = pl.ds(pl.multiple_of(i * RSTEP, 16), RSTEP)
+            there = pl.ds(pl.multiple_of(at_other + i * RSTEP, 16), RSTEP)
+            target[at, :] = (target[at, :].astype(jnp.float32) + other[there, :].astype(jnp.float32)).astype(target.dtype)
+            return c
+        lax.fori_loop(0, rows // RSTEP, body, 0)
+
+    def flows(k):
+        total = held[L - 1].at[k, 0]
+        for step in range(n):
+            t0, t1 = n - 1 - step, step
+            @pl.when((z > 0) & (t0 >= z))
+            def _():
+                pass_on(k, t0, 0, flow.at[k, 0, t0]).wait_recv()
+                add_block(flow.at[k, 0, t0], total, t0 * rows)
+                @pl.when(t0 > z)
+                def _():
+                    pass_on(k, t0, 0, flow.at[k, 0, t0]).start()
+            @pl.when((z < n - 1) & (t1 <= z))
+            def _():
+                pass_on(k, t1, 1, flow.at[k, 1, t1]).wait_recv()
+                @pl.when(t1 < z)
+                def _():
+                    add_block(flow.at[k, 1, t1], total, t1 * rows)
+                    pass_on(k, t1, 1, flow.at[k, 1, t1]).start()
+        @pl.when(z == 0)
+        def _():
+            add_block(flow.at[k, 1, 0], total, 0)
+        @pl.when((z > 0) & (z < n - 1))
+        def _():
+            add_block(flow.at[k, 1, z], flow.at[k, 0, z], 0)
+
+    def finished(k, p):
+        return F.at[k // subs, :, columns(k, p)]
+
+    def share(k, p, level, source=None):
+        return pltpu.make_async_remote_copy(
+            src_ref=finished(k, p) if source is None else source, dst_ref=finished(k, p),
+            send_sem=fsend.at[k, p, level], recv_sem=frecv.at[k, p], device_id={"replica": r ^ bits[level]}, device_id_type=MESH)
+
+    def keep(k, side):
+        return pltpu.make_async_copy(flow.at[k, side, z], finished(k, r), fkeep.at[k])
+
+    def publish(k):
+        @pl.when(z < n - 1)
+        def _():
+            for level in reversed(range(L)):
+                share(k, r, level, flow.at[k, 1, z]).start()
+            keep(k, 1).start()
+        @pl.when(z == n - 1)
+        def _():
+            for level in reversed(range(L)):
+                share(k, r, level, flow.at[k, 0, z]).start()
+            keep(k, 0).start()
+
+    def masks(level):
+        found = [0]
+        for upper in range(level + 1, L):
+            found = found + [m | bits[upper] for m in found]
+        return [m | bits[level] for m in found]
+
+    def collect(level, k):
+        for mask in masks(level):
+            p = r ^ mask
+            share(k, p, level).wait_recv()
+            for lower in reversed(range(level)):
+                share(k, p, lower).start()
+
+    def small_to_z(t):
+        return pltpu.make_async_remote_copy(
+            src_ref=small_in.at[t], dst_ref=small_z.at[z], send_sem=ss_z.at[t], recv_sem=sr_z.at[z],
+            device_id={"fsdp": t}, device_id_type=MESH)
+
+    def small_to_r(p):
+        return pltpu.make_async_remote_copy(
+            src_ref=small_sum, dst_ref=small_r.at[r], send_sem=ss_r.at[p], recv_sem=sr_r.at[r],
+            device_id={"replica": p}, device_id_type=MESH)
+
+    pl.semaphore_wait(barrier, n - 1 + R - 1)
+    own_small = pltpu.make_async_copy(small_in.at[z], small_z.at[z], ss_l)
+    own_small.start()
+    start(0)
+    for hop in range(1, n):
+        small_to_z(lax.rem(z + hop, n)).start()
+    stages = 1 + L + 1 + L
+    for turn in range(K + stages - 1):
+        for stage in range(stages):
+            k = turn - stage
+            if k < 0 or k >= K:
+                continue
+            if stage == 0:
+                if k > 0:
+                    start(k)
+            elif stage <= L:
+                merge(stage - 1, k)
+                if stage == L:
+                    launch(k)
+            elif stage == L + 1:
+                flows(k)
+                publish(k)
+            else:
+                collect(L - 1 - (stage - L - 2), k)
+        if turn == 1:
+            own_small.wait()
+            for hop in range(1, n):
+                source = lax.rem(z + hop, n)
+                pltpu.make_async_remote_copy(
+                    src_ref=small_in.at[source], dst_ref=small_z.at[source], send_sem=ss_z.at[source],
+                    recv_sem=sr_z.at[source], device_id={"fsdp": source}, device_id_type=MESH).wait_recv()
+            together = small_z[0]
+            for t in range(1, n):
+                together = together + small_z[t]
+            small_sum[...] = together
+            small_r[r] = together
+            for hop in range(1, R):
+                small_to_r(lax.rem(r + hop, R)).start()
+    for hop in range(1, R):
+        p = lax.rem(r + hop, R)
+        pltpu.make_async_remote_copy(
+            src_ref=small_sum, dst_ref=small_r.at[p], send_sem=ss_r.at[p], recv_sem=sr_r.at[p],
+            device_id={"replica": p}, device_id_type=MESH).wait_recv()
+    together = small_r[0]
+    for p in range(1, R):
+        together = together + small_r[p]
+    small_out[...] = together
+    for hop in range(1, R):
+        small_to_r(lax.rem(r + hop, R)).wait_send()
+    for hop in range(1, n):
+        small_to_z(lax.rem(z + hop, n)).wait_send()
+    for k in range(K):
+        for level in range(L):
+            for j in range(R >> (level + 1)):
+                give(level, k, j).wait_send()
+        for t in range(n):
+            @pl.when((t > z))
+            def _():
+                pass_on(k, t, 0, flow.at[k, 0, t]).wait_send()
+            @pl.when((t < z))
+            def _():
+                pass_on(k, t, 1, flow.at[k, 1, t]).wait_send()
+        keep(k, 0).wait()
+        for level in range(L):
+            share(k, r, level).wait_send()
+            for mask in masks(level):
+                for lower in range(level):
+                    share(k, r ^ mask, lower).wait_send()
+
+def reduce_grads(n, R, small, a, u, d):
+    full, wide = a.shape
+    rows = full // n
+    part = wide // R
+    sub = next(s for s in (384, 256, 128) if part % s == 0)
+    K = 3 * (part // sub)
+    L = R.bit_length() - 1
+    dma = pltpu.SemaphoreType.DMA
+    return pl.pallas_call(
+        functools.partial(reduce_kernel, n, R, sub),
+        out_shape=(jax.ShapeDtypeStruct((3, rows, wide), a.dtype),
+                   jax.ShapeDtypeStruct(small.shape[1:], small.dtype)),
+        in_specs=[pl.BlockSpec(memory_space=pltpu.VMEM)] + [pl.BlockSpec(memory_space=pl.ANY)] * 3,
+        out_specs=(pl.BlockSpec(memory_space=pl.ANY), pl.BlockSpec(memory_space=pltpu.VMEM)),
+        scratch_shapes=[pltpu.VMEM((K, R >> (level + 1), full, sub), a.dtype) for level in range(L)] + [
+            pltpu.VMEM((2, R // 2, full, sub), a.dtype),
+            pltpu.VMEM((K, 2, n, rows, sub), a.dtype),
+            pltpu.VMEM((n,) + small.shape[1:], small.dtype),
+            pltpu.VMEM((R,) + small.shape[1:], small.dtype),
+            pltpu.VMEM(small.shape[1:], small.dtype),
+            dma((2, R // 2)),
+            dma((L, K, R // 2)), dma((L, K, R // 2)),
+            dma((K, 2, n)), dma((K, 2, n)),
+            dma((K, R, L)), dma((K, R)), dma((K,)),
+            dma((n,)), dma((n,)), dma((R,)), dma((R,)), dma(()),
+        ],
+        compiler_params=pltpu.CompilerParams(collective_id=1, has_side_effects=True, vmem_limit_bytes=60 * 1024 * 1024),
+    )(small, a, u, d)
 
 
 def shifted(value, axis, steps):
@@ -33,131 +463,55 @@
     return center * lax.rsqrt(spread + 1e-06) * gain + shift
 
 
-def fetch_forward(shards):
-    (
-        gain_one,
-        shift_one,
-        weight_qkv,
-        bias_qv,
-        weight_out,
-        bias_out,
-        gain_two,
-        shift_two,
-        weight_up,
-        bias_up,
-        weight_down,
-        bias_down,
-    ) = shards
-    return (
-        lax.all_gather(gain_one, "fsdp", axis=0, tiled=True),
-        lax.all_gather(shift_one, "fsdp", axis=0, tiled=True),
-        lax.all_gather(weight_qkv, "fsdp", axis=0, tiled=True),
-        lax.all_gather(bias_qv, "fsdp", axis=1, tiled=True),
-        lax.all_gather(weight_out, "fsdp", axis=0, tiled=True),
-        lax.all_gather(bias_out, "fsdp", axis=0, tiled=True),
-        lax.all_gather(gain_two, "fsdp", axis=0, tiled=True),
-        lax.all_gather(shift_two, "fsdp", axis=0, tiled=True),
-        lax.all_gather(weight_up, "fsdp", axis=0, tiled=True),
-        lax.all_gather(bias_up, "fsdp", axis=0, tiled=True),
-        lax.all_gather(weight_down, "fsdp", axis=1, tiled=True),
-        lax.all_gather(bias_down, "fsdp", axis=0, tiled=True),
-    )
-
-
-def fetch_backward(shards):
-    (
-        gain_one,
-        shift_one,
-        weight_qkv,
-        bias_qv,
-        weight_out,
-        bias_out,
-        gain_two,
-        shift_two,
-        weight_up,
-        bias_up,
-        weight_down,
-        bias_down,
-    ) = shards
-    return (
-        lax.all_gather(gain_one, "fsdp", axis=0, tiled=True),
-        lax.all_gather(shift_one, "fsdp", axis=0, tiled=True),
-        lax.all_gather(weight_qkv, "fsdp", axis=0, tiled=True),
-        lax.all_gather(bias_qv, "fsdp", axis=1, tiled=True),
-        lax.all_gather(weight_out, "fsdp", axis=0, tiled=True),
-        lax.all_gather(bias_out, "fsdp", axis=0, tiled=True),
-        lax.all_gather(gain_two, "fsdp", axis=0, tiled=True),
-        lax.all_gather(shift_two, "fsdp", axis=0, tiled=True),
-        lax.all_gather(weight_up, "fsdp", axis=0, tiled=True),
-        lax.all_gather(bias_up, "fsdp", axis=0, tiled=True),
-        lax.all_gather(weight_down, "fsdp", axis=1, tiled=True),
-        lax.all_gather(bias_down, "fsdp", axis=0, tiled=True),
-    )
-
-
-def reduce_shares(grads):
-    (
-        gain_one,
-        shift_one,
-        weight_qkv,
-        bias_qv,
-        weight_out,
-        bias_out,
-        gain_two,
-        shift_two,
-        weight_up,
-        bias_up,
-        weight_down,
-        bias_down,
-    ) = grads
-    return (
-        lax.psum_scatter(gain_one, "fsdp", scatter_dimension=0, tiled=True),
-        lax.psum_scatter(shift_one, "fsdp", scatter_dimension=0, tiled=True),
-        lax.psum_scatter(weight_qkv, "fsdp", scatter_dimension=0, tiled=True),
-        lax.psum_scatter(bias_qv, "fsdp", scatter_dimension=1, tiled=True),
-        lax.psum_scatter(weight_out, "fsdp", scatter_dimension=0, tiled=True),
-        lax.psum_scatter(bias_out, "fsdp", scatter_dimension=0, tiled=True),
-        lax.psum_scatter(gain_two, "fsdp", scatter_dimension=0, tiled=True),
-        lax.psum_scatter(shift_two, "fsdp", scatter_dimension=0, tiled=True),
-        lax.psum_scatter(weight_up, "fsdp", scatter_dimension=0, tiled=True),
-        lax.psum_scatter(bias_up, "fsdp", scatter_dimension=0, tiled=True),
-        lax.psum_scatter(weight_down, "fsdp", scatter_dimension=1, tiled=True),
-        lax.psum_scatter(bias_down, "fsdp", scatter_dimension=0, tiled=True),
-    )
-
-
-def sum_replicas(shares):
-    (
-        gain_one,
-        shift_one,
-        weight_qkv,
-        bias_qv,
-        weight_out,
-        bias_out,
-        gain_two,
-        shift_two,
-        weight_up,
-        bias_up,
-        weight_down,
-        bias_down,
-    ) = shares
-    return lax.psum(
-        (
-            gain_one,
-            shift_one,
-            weight_qkv,
-            bias_qv,
-            weight_out,
-            bias_out,
-            gain_two,
-            shift_two,
-            weight_up,
-            bias_up,
-            weight_down,
-            bias_down,
-        ),
-        "replica",
-    )
+def pad_columns(value, wide):
+    return jnp.pad(value, ((0, 0), (0, wide - value.shape[1])))
+
+
+def packed_width(widths, count):
+    unit = 128 * count
+    return max(-(-width // unit) * unit for width in widths)
+
+
+def gather_layer(shards, n, R):
+    (gain_one, shift_one, weight_qkv, bias_qv, weight_out, bias_out, gain_two, shift_two,
+     weight_up, bias_up, weight_down, bias_down) = shards
+    model = gain_one.shape[0] * n
+    hidden = weight_up.shape[1]
+    wide = packed_width((weight_qkv.shape[1] + weight_out.shape[1], hidden), R)
+    vector = jnp.concatenate([gain_one, shift_one, bias_qv[0], bias_qv[1], bias_out, gain_two, shift_two, bias_down, bias_up])
+    lanes = -(-vector.shape[0] // (16 * 128)) * 128
+    small = jnp.pad(vector, (0, 16 * lanes - vector.shape[0])).reshape(16, lanes)
+    G, S = gather_weights(n, R, weight_qkv, weight_out, pad_columns(weight_up, wide), pad_columns(weight_down.T, wide), small)
+    S = S.reshape(n, -1)
+    piece = model // n
+    vectors = S[:, : 8 * piece].reshape(n, 8, piece).transpose(1, 0, 2).reshape(8, model)
+    up_bias = S[:, 8 * piece : 8 * piece + hidden // n].reshape(hidden)
+    return (vectors[0], vectors[1], G[0][:, : 3 * model], vectors[2:4], G[0][:, 3 * model : 4 * model], vectors[4],
+            vectors[5], vectors[6], G[1][:, :hidden], up_bias, G[2][:, :hidden].T, vectors[7])
+
+
+def reduce_layer(grads, n, R):
+    (gain_one, shift_one, weight_qkv, bias_qv, weight_out, bias_out, gain_two, shift_two,
+     weight_up, bias_up, weight_down, bias_down) = grads
+    model = gain_one.shape[0]
+    hidden = weight_up.shape[1]
+    wide = packed_width((4 * model, hidden), R)
+    half = jnp.bfloat16
+    a = pad_columns(jnp.concatenate([weight_qkv.astype(half), weight_out.astype(half)], axis=1), wide)
+    u = pad_columns(weight_up.astype(half), wide)
+    d = pad_columns(weight_down.astype(half), wide)
+    piece = model // n
+    vectors = jnp.stack([gain_one, shift_one, bias_qv[0], bias_qv[1], bias_out, gain_two, shift_two, bias_down])
+    vectors = vectors.reshape(8, n, piece).transpose(1, 0, 2).reshape(n, 8 * piece)
+    vectors = jnp.concatenate([vectors, bias_up.reshape(n, hidden // n)], axis=1)
+    lanes = -(-vectors.shape[1] // (16 * 128)) * 128
+    small = jnp.pad(vectors, ((0, 0), (0, 16 * lanes - vectors.shape[1]))).reshape(n, 16, lanes)
+    F, s = reduce_grads(n, R, small, a, u, d)
+    s = s.reshape(-1)
+    v = s[: 8 * piece].reshape(8, piece)
+    F = F.astype(jnp.float32)
+    return (v[0], v[1], F[0][:, : 3 * model], v[2:4], F[0][:, 3 * model : 4 * model], v[4], v[5], v[6],
+            F[1][:, :hidden], s[8 * piece : 8 * piece + hidden // n], F[2][:, :hidden].T, v[7])
 
 
 def attention_scores(queries, key_rows):
@@ -262,7 +616,7 @@
     sum_axes = (0, 1)
     grad_branch = grad_out.astype(jnp.bfloat16)
     g_down_weight = jnp.einsum(
-        "bsf,bsd->fd", activated, grad_branch, preferred_element_type=jnp.float32
+        "bsd,bsf->df", grad_branch, activated, preferred_element_type=jnp.float32
     )
     g_down_bias = jnp.sum(grad_branch.astype(jnp.float32), axis=sum_axes)
     grad_act = jnp.einsum(
@@ -397,11 +751,12 @@
         boundary[micro_index * per_micro : (micro_index + 1) * per_micro]
         for micro_index in range(MICRO)
     ]
+    n, R = lax.axis_size("fsdp"), lax.axis_size("replica")
+    weights = gather_layer(shards, n, R)
     received = jnp.zeros_like(pieces[0])
     saved_steps = []
     outputs = []
     for moment in range(MICRO + 1):
-        weights = fetch_forward(shards)
         source = pieces[min(moment, MICRO - 1)]
         inputs = jnp.where(at_first, source, received)
         result, saved_acts = layer_forward(inputs, weights)
@@ -412,10 +767,8 @@
     stacked = tuple((jnp.stack(items) for items in zip(*saved_steps)))
     back_received = jnp.zeros_like(pieces[0])
     totals = None
-    shares = None
     in_grads = []
     for moment in range(MICRO + 1):
-        weights = fetch_backward(shards)
         slot_index = jnp.clip(moment - 1 + 2 * section_idx, 0, MICRO)
         saved_acts = tuple(
             (lax.dynamic_index_in_dim(item, slot_index, 0, keepdims=False) for item in stacked)
@@ -432,8 +785,7 @@
         totals = (
             grads if totals is None else tuple((left + right for left, right in zip(totals, grads)))
         )
-    shares = reduce_shares(totals)
-    summed = sum_replicas(shares)
+    summed = reduce_layer(totals, n, R)
     grad_rows = jnp.concatenate(in_grads[1:], axis=0)
     out_rows = jnp.concatenate(outputs[1:], axis=0)
     result_ends = jnp.where(at_first, grad_rows, out_rows)[None]

time: 2410 us -> 1340 us (0.56)
  waiting for transfers between devices: 1580 us -> 41.2 us
  Pallas kernels: 0 us -> 417 us
  local copies, waits for them, and re-layouts: 152 us -> 243 us
  blocking collectives: 78 us -> 0 us
  other arithmetic: 144 us -> 169 us
    reduce_scatter x4 -> x0, waiting for transfers between devices: 835 us -> none  [the longest x1 336 us: reduce_shares(): lax.psum_scatter(weight_down, 'fsdp', scatter_dimension=1, tiled=True)]
    all_gather x4 -> x0, waiting for transfers between devices: 442 us -> none  [the longest x1 171 us: fetch_forward(): lax.all_gather(weight_up, 'fsdp', axis=0, tiled=True)]
    pallas_call x0 -> x2, Pallas kernels: none -> 417 us  [the longest x1 262 us: reduce_grads(): pl.pallas_call(functools.partial(reduce_kernel, n, R, sub), out_shape=(ja...]
    psum x1 -> x0, waiting for transfers between devices: 239 us -> none  [sum_replicas(): lax.psum((gain_one, shift_one, weight_qkv, bias_qv, weight_out, bias_out,...]
    add x0 -> x9, local copies, waits for them, and re-layouts: none -> 43.7 us  [on_device(): left + right]
    unnamed x2 -> x0, blocking collectives: 35.7 us -> none
    squeeze x0 -> x2, local copies, waits for them, and re-layouts: none -> 28.8 us  [the longest x1 22.5 us: gather_layer(): G[1][:, :hidden]]
    all_gather x1 -> x0, blocking collectives: 28.1 us -> none  [fetch_forward(): lax.all_gather(bias_qv, 'fsdp', axis=1, tiled=True)]
  transfers between devices with their start and end apart: 14 -> 4, of which waited for: 11 -> 2; matrix products, arithmetic and copies ran while one was open for 13% -> 12% of each run, Pallas kernels for 0% -> 0%
where the time goes in v1:
time: 1340 us; the launch traced here: 1330 us
  matrix products  444 us (33%)
  Pallas kernels  417 us (31%)
  local copies, waits for them, and re-layouts  243 us (18%)
  other arithmetic  169 us (13%)
  waiting for transfers between devices  41.2 us (3%)
    pallas_call x1, Pallas kernels, reduce_grads(): pl.pallas_call(functools.partial(reduce_kernel, n, R, sub), out_shape=(ja...  262 us
    pallas_call x1, Pallas kernels, gather_weights(): pl.pallas_call(functools.partial(gather_kernel, n, R), out_shape=(jax.Sha...  155 us
    another operation x14, other arithmetic, on_device(): stacked = tuple((jnp.stack(items) for items in zip(*saved_steps)))  64.3 us
    dot_general x3, matrix products, layer_backward(): jnp.einsum('bsd,fd->bsf', grad_branch, weight_down, preferred_element_typ...  48.6 us
    dot_general x3, matrix products, layer_backward(): jnp.einsum('bsd,bsf->df', grad_branch, activated, preferred_element_type=...  45.5 us
    add x9, local copies, waits for them, and re-layouts, on_device(): left + right  43.7 us
    dot_general x3, matrix products, layer_backward(): jnp.einsum('bsd,bsf->df', normed_two, grad_pre, preferred_element_type=jn...  42 us
    dot_general x3, matrix products, layer_forward(): jnp.einsum('bsf,fd->bsd', activated, weight_down, preferred_element_type=...  41.7 us
  transfers between devices with their start and end apart: 4, of which 2 were waited for; matrix products, arithmetic and copies ran while one was open for 12% of the time, Pallas kernels for 0%

profile of v1, /device:TPU:1, one launch (start us, length us, event | category | flops | bytes accessed | tf_op | source)
XLA Modules:
  0.0 1327.4 jit_solution(9801379494179116350)
XLA Ops:
  8.6 155.0 %shard_map.228 = (bf16[3,1152,4608]{2,1,0:T(8,128)(2,1)}, bf16[4,16,256]{2,1,0:T(8,128)(2,1)S(1)}) custom-call(bf16[288,3456]{1,0:T(8,128)(2,1)S(1)} %bitcast.564, bf16[288,1152]{1,0:T(8,128)(2,1)S(1)} %bitcast.565, bf16[288,4608]{1,0:T(8,128)(2,1)S(1)} %pad.22.up, bf16[288,4608]{1,0:T(8,128)(2,1)S(1)} %copy-done, bf16[16,256]{1,0:T(8,128)(2,1)S(1)} %reshape.900.small), custom_call_target="tpu_custom_call" | custom-call | tf_op jit(solution)/shard_map/pallas_call | solution.py:158
  170.5 22.5 %slice_bitcast_fusion.1 = (bf16[1152,4608]{1,0:T(8,128)(2,1)}, bf16[1152,4608]{1,0:T(8,128)(2,1)}, bf16[1152,4608]{1,0:T(8,128)(2,1)}) fusion(bf16[3,1152,4608]{2,1,0:T(8,128)(2,1)} %get-tuple-element.18), kind=kLoop, calls=%fused_computation.37 | loop fusion | bytes 63700992 | tf_op jit(solution)/shard_map/squeeze | solution.py:490
  231.9 12.8 fusion.143
  244.7 13.4 %fusion.94 = bf16[3,160,1152]{2,1,0:T(8,128)(2,1)} fusion(f32[3,160,1152]{2,1,0:T(8,128)S(1)} %copy-done.16, f32[1152]{0:T(1024)S(1)} %reshape.945, bf16[1152,4608]{1,0:T(8,128)(2,1)} %get-tuple-element.93, f32[3,160,4304]{2,1,0:T(8,128)} %fusion.143, f32[4304]{0:T(1024)S(1)} %reshape.944), kind=kOutput, calls=%fused_computation.196 | convolution fusion | flops 4782197760 | bytes 21722432 | tf_op jit(solution)/shard_map/bsf,fd->bsd/dot_general | solution.py:567
  261.3 23.9 %collective-permute-done = bf16[3,160,1152]{2,1,0:T(8,128)(2,1)S(1)} collective-permute-done((bf16[3,160,1152]{2,1,0:T(8,128)(2,1)}, bf16[3,160,1152]{2,1,0:T(8,128)(2,1)S(1)}, u32[]{:S(2)}, u32[]{:S(2)}) %collective-permute-start) | collective-permute-done | bytes 1105952 | tf_op jit(solution)/shard_map/ppermute | solution.py:446
  331.3 14.4 %fusion.215 = (bf16[3,160,1152]{2,1,0:T(8,128)(2,1)S(1)}, f32[3,160,1152]{2,1,0:T(8,128)}) fusion(f32[3,160,1152]{2,1,0:T(8,128)} %copy-done.23, f32[1152]{0:T(1024)S(1)} %reshape.945, bf16[1152,4608]{1,0:T(8,128)(2,1)} %get-tuple-element.93, f32[3,160,4304]{2,1,0:T(8,128)} %fusion.147, f32[4304]{0:T(1024)S(1)} %reshape.944), kind=kOutput, calls=%fused_computation.463 | convolution fusion | flops 4782197760 | bytes 23934272 | tf_op jit(solution)/shard_map/bsf,fd->bsd/dot_general | solution.py:567
  355.3 17.2 %collective-permute-done.1 = bf16[3,160,1152]{2,1,0:T(8,128)(2,1)S(1)} collective-permute-done((bf16[3,160,1152]{2,1,0:T(8,128)(2,1)S(1)}, bf16[3,160,1152]{2,1,0:T(8,128)(2,1)S(1)}, u32[]{:S(2)}, u32[]{:S(2)}) %collective-permute-start.1) | collective-permute-done | bytes 1105952 | tf_op jit(solution)/shard_map/ppermute | solution.py:446
  432.6 22.3 %fusion.202 = (bf16[1,3,160,4304]{3,2,1,0:T(8,128)(2,1)}, f32[1,3,160,4304]{3,2,1,0:T(8,128)}, f32[1,3,160,4304]{3,2,1,0:T(8,128)}, bf16[1,3,160,4304]{3,2,1,0:T...) fusion(f32[3,160,4304]{2,1,0:T(8,128)} %fusion.143, f32[4304]{0:T(1024)S(1)} %reshape.944, ...), kind=kLoop, calls=%fused_computation.454 | loop fusion | flops 61977600 | bytes 61994816 | tf_op jit(solution)/shard_map/stack | solution.py:767
  455.0 18.6 %pad_maximum_fusion = f32[3,3,160,4304]{3,2,1,0:T(8,128)} fusion(f32[1,3,160,4304]{3,2,1,0:T(8,128)} %get-tuple-element.128, f32[1,3,160,4304]{3,2,1,0:T(8,128)} %get-tuple-element.126, f32[1,3,160,4304]{3,2,1,0:T(8,128)} %get-tuple-element.99), kind=kLoop, calls=%fused_computation | loop fusion | flops 12395520 | bytes 49582080 | tf_op jit(solution)/shard_map/stack | solution.py:767
  473.6 15.9 %convert_reduce_fusion.2 = (f32[4304]{0:T(1024)}, bf16[3,160,4304]{2,1,0:T(8,128)(2,1)}) fusion(bf16[3,160,1152]{2,1,0:T(8,128)(2,1)S(1)} %copy-done.93, bf16[1152,4608]{1,0:T(8,128)(2,1)} %get-tuple-element.93, f32[3,3,160,4304]{3,2,1,0:T(8,128)} %pad_maximum_fusion, s32[]{:T(128)S(6)} %min.10), kind=kOutput, calls=%fused_computation.102 | convolution fusion | flops 4813589504 | bytes 23637828 | tf_op jit(solution)/shard_map/bsd,fd->bsf/dot_general | solution.py:622
  489.5 13.5 %multiply_reduce_fusion.8 = (f32[1152]{0:T(1024)}, f32[3,160]{1,0:T(4,128)S(1)}, f32[1152]{0:T(1024)}, f32[3,160,1152]{2,1,0:T(8,128)}) fusion(f32[3,3,160,1152]{3,2,1,0:T(8,128)} %copy-done.3, s32[]{:T(128)S(6)} %min.10, f32[3,160]{1,0:T(4,128)S(1)} %fusion.173, f32[3,160]{1,0:T(4,128)S(1)} %broadcast_multiply_fusion.5, f32[1152]{0:T(1024)S(1)} %reshape.942, ...), kind=kOutput, calls=%fused_computation.237 | convolution fusion | flops 4764300800 | bytes 18648196 | tf_op jit(solution)/shard_map/bsf,df->bsd/dot_general | solution.py:631
  553.9 13.9 %fusion.93 = f32[1,3,160,1152]{3,2,1,0:T(8,128)} fusion(f32[3,160,1152]{2,1,0:T(8,128)S(1)} %copy-done.20, f32[1152]{0:T(1024)S(1)} %copy-done.158, bf16[1152,4608]{1,0:T(8,128)(2,1)} %get-tuple-element.93, f32[3,160,4304]{2,1,0:T(8,128)} %fusion.151, f32[4304]{0:T(1024)S(1)} %copy-done.110), kind=kOutput, calls=%fused_computation.195 | convolution fusion | flops 4781644800 | bytes 22828352 | tf_op jit(solution)/shard_map/bsf,fd->bsd/dot_general | solution.py:567
  652.2 13.2 convolution_bitcast_fusion.5
  667.7 16.4 %convert_reduce_fusion.1 = (f32[4304]{0:T(1024)}, bf16[3,160,4304]{2,1,0:T(8,128)(2,1)}) fusion(bf16[3,160,1152]{2,1,0:T(8,128)(2,1)S(1)} %get-tuple-element.71, bf16[1152,4608]{1,0:T(8,128)(2,1)} %get-tuple-element.93, f32[3,3,160,4304]{3,2,1,0:T(8,128)} %pad_maximum_fusion, s32[]{:T(128)S(6)} %min.11), kind=kOutput, calls=%fused_computation.101 | convolution fusion | flops 4813589504 | bytes 23637828 | tf_op jit(solution)/shard_map/bsd,fd->bsf/dot_general | solution.py:622
  748.7 15.3 %fusion.3 = f32[1152,4304]{0,1:T(8,128)} fusion(f32[1152,4304]{0,1:T(8,128)} %convolution_bitcast_fusion.5, bf16[3,160,4304]{2,1,0:T(8,128)(2,1)} %get-tuple-element.184, bf16[3,3,160,1152]{3,2,1,0:T(8,128)(2,1)} %copy-done.67, s32[]{:T(128)S(6)} %min.11), kind=kOutput, calls=%fused_computation.9 | convolution fusion | flops 4764837888 | bytes 44949508 | tf_op jit(solution)/shard_map/bsd,bsf->df/dot_general | solution.py:627
  764.0 19.6 %fusion.1 = f32[1152,4304]{0,1:T(8,128)} fusion(f32[1152,4304]{0,1:T(8,128)} %convolution_bitcast_fusion.2, bf16[3,160,1152]{2,1,0:T(8,128)(2,1)S(1)} %copy-done.70, bf16[3,3,160,4304]{3,2,1,0:T(8,128)(2,1)} %copy-done.14, s32[]{:T(128)S(6)} %min.11), kind=kOutput, calls=%fused_computation.4 | convolution fusion | flops 4764837888 | bytes 44949508 | tf_op jit(solution)/shard_map/bsd,bsf->df/dot_general | solution.py:618
  786.9 21.6 %copy.239 = f32[1152,4304]{1,0:T(8,128)} copy(f32[1152,4304]{0,1:T(8,128)} %fusion.3) | data formatting | bytes 39665664 | tf_op jit(solution)/shard_map/add | solution.py:786
  808.5 21.6 %copy.241 = f32[1152,4304]{1,0:T(8,128)} copy(f32[1152,4304]{0,1:T(8,128)} %fusion.1) | data formatting | bytes 39665664 | tf_op jit(solution)/shard_map/add | solution.py:786
  840.2 16.3 %convert_reduce_fusion = (f32[4304]{0:T(1024)}, bf16[3,160,4304]{2,1,0:T(8,128)(2,1)}) fusion(bf16[3,160,1152]{2,1,0:T(8,128)(2,1)S(1)} %get-tuple-element.75, bf16[1152,4608]{1,0:T(8,128)(2,1)} %get-tuple-element.93, f32[3,3,160,4304]{3,2,1,0:T(8,128)} %pad_maximum_fusion, s32[]{:T(128)S(6)} %min.12), kind=kOutput, calls=%fused_computation.100 | convolution fusion | flops 4813589504 | bytes 23637828 | tf_op jit(solution)/shard_map/bsd,fd->bsf/dot_general | solution.py:622
  856.6 12.0 multiply_reduce_fusion.15
  962.8 13.9 %fusion.8 = bf16[1152,3456]{1,0:T(8,128)(2,1)} fusion(f32[1152,3456]{1,0:T(8,128)} %fusion.7, bf16[3,3,160,1152]{3,2,1,0:T(8,128)(2,1)S(1)} %pad_maximum_fusion.12, s32[]{:T(128)S(6)} %min.12, bf16[3,160,1152]{2,1,0:T(8,128)(2,1)S(1)} %copy-done.85, bf16[3,160,1152]{2,1,0:T(8,128)(2,1)} %copy.230, bf16[3,160,1152]{2,1,0:T(8,128)(2,1)} %copy.229), kind=kOutput, calls=%fused_computation.18 | convolution fusion | flops 3839975424 | bytes 28311556 | tf_op jit(solution)/shard_map/bsd,bse->de/dot_general | solution.py:683
  976.7 13.5 %fusion.4 = bf16[1152,4304]{1,0:T(8,128)(2,1)} fusion(f32[1152,4304]{1,0:T(8,128)} %copy.239, bf16[3,160,4304]{2,1,0:T(8,128)(2,1)} %get-tuple-element.180, bf16[3,3,160,1152]{3,2,1,0:T(8,128)(2,1)} %copy-done.67, s32[]{:T(128)S(6)} %min.12), kind=kOutput, calls=%fused_computation.11 | convolution fusion | flops 4769796096 | bytes 35254276 | tf_op jit(solution)/shard_map/bsd,bsf->df/dot_general | solution.py:627
  999.0 15.0 %fusion.5 = bf16[1152,4304]{1,0:T(8,128)(2,1)} fusion(f32[1152,4304]{1,0:T(8,128)} %copy.241, bf16[3,160,1152]{2,1,0:T(8,128)(2,1)S(1)} %copy-done.96, bf16[3,3,160,4304]{3,2,1,0:T(8,128)(2,1)} %copy-done.14, s32[]{:T(128)S(6)} %min.12), kind=kOutput, calls=%fused_computation.12 | convolution fusion | flops 4769796096 | bytes 35254276 | tf_op jit(solution)/shard_map/bsd,bsf->df/dot_general | solution.py:618
  1031.4 261.9 %shard_map.229 = (bf16[3,288,4608]{2,1,0:T(8,128)(2,1)}, f32[16,256]{1,0:T(8,128)}) custom-call(f32[4,16,256]{2,1,0:T(8,128)} %bitcast.649, bf16[1152,4608]{1,0:T(8,128)(2,1)} %pad_maximum_fusion.2.a_in, bf16[1152,4608]{1,0:T(8,128)(2,1)} %pad.26.u_in, bf16[1152,4608]{1,0:T(8,128)(2,1)} %pad.27.d_in), custom_call_target="tpu_custom_call" | custom-call | tf_op jit(solution)/shard_map/pallas_call | solution.py:421
  (635 shorter events, 540.3 us)
Async XLA Ops:
  164.0 213.3 %copy-start.128 = (f32[1152]{0:T(1024)}, f32[1152]{0:T(1024)S(1)}, u32[]{:S(2)}) copy-start(f32[1152]{0:T(1024)S(1)} %reshape.938) | copy-start | bytes 13828
  164.1 213.2 %copy-start.107 = (f32[1152]{0:T(1024)}, f32[1152]{0:T(1024)S(1)}, u32[]{:S(2)}) copy-start(f32[1152]{0:T(1024)S(1)} %reshape.937) | copy-start | bytes 13828
  170.0 55.7 %copy-start.8 = (f32[1,3,160,1152]{3,2,1,0:T(8,128)}, f32[1,3,160,1152]{3,2,1,0:T(8,128)S(1)}, u32[]{:S(2)}) copy-start(f32[1,3,160,1152]{3,2,1,0:T(8,128)S(1)} %get-tuple-element.91) | copy-start | bytes 6635524
  170.0 23.2 %copy-start.112 = (f32[3,160]{1,0:T(4,128)}, f32[3,160]{1,0:T(4,128)S(1)}, u32[]{:S(2)}) copy-start(f32[3,160]{1,0:T(4,128)S(1)} %broadcast_multiply_fusion.11) | copy-start | bytes 5764
  170.4 22.8 %copy-start.145 = (f32[3,160]{1,0:T(4,128)}, f32[3,160]{1,0:T(4,128)S(1)}, u32[]{:S(2)}) copy-start(f32[3,160]{1,0:T(4,128)S(1)} %add_rsqrt_fusion.5) | copy-start | bytes 5764
  220.1 111.3 %copy-start.157 = (f32[1152]{0:T(1024)}, f32[1152]{0:T(1024)S(1)}, u32[]{:S(2)}) copy-start(f32[1152]{0:T(1024)S(1)} %reshape.945) | copy-start | bytes 13828
  220.2 282.8 %copy-start.105 = (f32[1152]{0:T(1024)}, f32[1152]{0:T(1024)S(1)}, u32[]{:S(2)}) copy-start(f32[1152]{0:T(1024)S(1)} %reshape.942) | copy-start | bytes 13828
  231.9 200.7 %copy-start.109 = (f32[4304]{0:T(1024)}, f32[4304]{0:T(1024)S(1)}, u32[]{:S(2)}) copy-start(f32[4304]{0:T(1024)S(1)} %reshape.944) | copy-start | bytes 51652
  258.1 27.1 %collective-permute-start = (bf16[3,160,1152]{2,1,0:T(8,128)(2,1)}, bf16[3,160,1152]{2,1,0:T(8,128)(2,1)S(1)}, u32[]{:S(2)}, u32[]{:S(2)}) collective-permute-start(bf16[3,160,1152]{2,1,0:T(8,128)(2,1)} %fusion.94), channel_id=1, source_target_pairs={{0,16},{1,17},{2,18},{3,19},{4,20},{5,21},{6,22},{7,23},{8,24},{9,... | collective-permute-start | bytes 3317768 | tf_op jit(solution)/shard_map/ppermute | solution.py:446
  287.2 123.6 %copy-start.6 = (f32[3,160,1152]{2,1,0:T(8,128)}, f32[3,160,1152]{2,1,0:T(8,128)S(1)}, u32[]{:S(2)}) copy-start(f32[3,160,1152]{2,1,0:T(8,128)S(1)} %get-tuple-element.89) | copy-start | bytes 6635524
  345.7 26.8 %collective-permute-start.1 = (bf16[3,160,1152]{2,1,0:T(8,128)(2,1)S(1)}, bf16[3,160,1152]{2,1,0:T(8,128)(2,1)S(1)}, u32[]{:S(2)}, u32[]{:S(2)}) collective-permute-start(bf16[3,160,1152]{2,1,0:T(8,128)(2,1)S(1)} %get-tuple-element.161), channel_id=1, source_target_pairs={{0,16},{1,17},{2,18},{3,19},{4,20},{5,21},{6,22},{7,23},{8,24},{9,... | collective-permute-start | bytes 3317768 | tf_op jit(solution)/shard_map/ppermute | solution.py:446
  455.0 18.7 %copy-start.93 = (bf16[3,160,1152]{2,1,0:T(8,128)(2,1)S(1)}, bf16[3,160,1152]{2,1,0:T(8,128)(2,1)}, u32[]{:S(2)}) copy-start(bf16[3,160,1152]{2,1,0:T(8,128)(2,1)} %get-tuple-element.73) | copy-start | bytes 3317764
  455.0 55.0 %slice-start = ((s8[4423680]{0:T(1024)(128)(4,1)}), s8[4194304]{0:T(1024)(128)(4,1)S(1)}, s32[]{:S(2)}) async-start(s8[4423680]{0:T(1024)(128)(4,1)} %bitcast.567), calls=%async_computation | async-start | bytes 8388608
  473.6 36.3 %slice-start.1 = ((s8[4423680]{0:T(1024)(128)(4,1)}), s8[229376]{0:T(1024)(128)(4,1)S(1)}, s32[]{:S(2)}) async-start(s8[4423680]{0:T(1024)(128)(4,1)} %bitcast.567), calls=%async_computation.1 | async-start | bytes 458752
  594.1 71.3 %collective-permute-start.2 = (bf16[3,160,1152]{2,1,0:T(8,128)(2,1)}, bf16[3,160,1152]{2,1,0:T(8,128)(2,1)}, u32[]{:S(2)}, u32[]{:S(2)}) collective-permute-start(bf16[3,160,1152]{2,1,0:T(8,128)(2,1)} %add_convert_fusion), channel_id=1, source_target_pairs={{16,0},{17,1},{18,2},{19,3},{20,4},{21,5},{22,6},{23,7},{24,8},{25... | collective-permute-start | bytes 3317768 | tf_op jit(solution)/shard_map/ppermute | solution.py:446
  603.6 32.8 %copy-start.25 = (bf16[1,3,160,1152]{2,3,1,0:T(8,128)(2,1)}, bf16[1,3,160,1152]{2,3,1,0:T(8,128)(2,1)S(1)}, u32[]{:S(2)}) copy-start(bf16[1,3,160,1152]{2,3,1,0:T(8,128)(2,1)S(1)} %copy.311) | copy-start | bytes 3317764
  606.4 30.0 %copy-start.27 = (bf16[1,3,160,1152]{2,3,1,0:T(8,128)(2,1)}, bf16[1,3,160,1152]{2,3,1,0:T(8,128)(2,1)S(1)}, u32[]{:S(2)}) copy-start(bf16[1,3,160,1152]{2,3,1,0:T(8,128)(2,1)S(1)} %copy.310) | copy-start | bytes 3317764
  642.3 23.1 %slice-start.4 = ((s8[4423680]{0:T(1024)(128)(4,1)}), s8[229376]{0:T(1024)(128)(4,1)S(1)}, s32[]{:S(2)}) async-start(s8[4423680]{0:T(1024)(128)(4,1)} %bitcast.571), calls=%async_computation.4 | async-start | bytes 458752
  747.3 16.7 %copy-start.70 = (bf16[3,160,1152]{2,1,0:T(8,128)(2,1)S(1)}, bf16[3,160,1152]{2,1,0:T(8,128)(2,1)}, u32[]{:S(2)}) copy-start(bf16[3,160,1152]{2,1,0:T(8,128)(2,1)} %copy-done.69) | copy-start | bytes 3317764
  747.3 90.1 %collective-permute-start.3 = (bf16[3,160,1152]{2,1,0:T(8,128)(2,1)}, bf16[3,160,1152]{2,1,0:T(8,128)(2,1)}, u32[]{:S(2)}, u32[]{:S(2)}) collective-permute-start(bf16[3,160,1152]{2,1,0:T(8,128)(2,1)} %get-tuple-element.111), channel_id=1, source_target_pairs={{16,0},{17,1},{18,2},{19,3},{20,4},{21,5},{22,6},{23,7},{24,8},{25... | collective-permute-start | bytes 3317768 | tf_op jit(solution)/shard_map/ppermute | solution.py:446
  764.0 19.6 %copy-start.79 = (bf16[3,160,1152]{2,1,0:T(8,128)(2,1)S(1)}, bf16[3,160,1152]{2,1,0:T(8,128)(2,1)}, u32[]{:S(2)}) copy-start(bf16[3,160,1152]{2,1,0:T(8,128)(2,1)} %copy.216) | copy-start | bytes 3317764
  764.0 19.6 %copy-start.81 = (bf16[3,160,1152]{2,1,0:T(8,128)(2,1)S(1)}, bf16[3,160,1152]{2,1,0:T(8,128)(2,1)}, u32[]{:S(2)}) copy-start(bf16[3,160,1152]{2,1,0:T(8,128)(2,1)} %copy.215) | copy-start | bytes 3317764
  830.1 41.8 %slice-start.6 = ((s8[4423680]{0:T(1024)(128)(4,1)}), s8[4194304]{0:T(1024)(128)(4,1)S(1)}, s32[]{:S(2)}) async-start(s8[4423680]{0:T(1024)(128)(4,1)} %bitcast.573), calls=%async_computation.6 | async-start | bytes 8388608
  840.2 31.7 %slice-start.7 = ((s8[4423680]{0:T(1024)(128)(4,1)}), s8[229376]{0:T(1024)(128)(4,1)S(1)}, s32[]{:S(2)}) async-start(s8[4423680]{0:T(1024)(128)(4,1)} %bitcast.573), calls=%async_computation.7 | async-start | bytes 458752
  (172 other events, 912.3 us)

commit v2 on v1

v2 whole, which is shorter than its diff:
```python
import functools
import math

import jax
import jax.numpy as jnp
from jax import lax
from jax.experimental import pallas as pl
from jax.experimental.pallas import tpu as pltpu
from jax.sharding import PartitionSpec as P

MESH = pl.DeviceIdType.MESH
HEADS = 16
HEAD_DIM = 72
MICRO = 3
F32 = jnp.float32
HALF = jnp.bfloat16
EPS = 1e-06
ANY = pl.BlockSpec(memory_space=pl.ANY)
NN = (((1,), (0,)), ((), ()))
NT = (((1,), (1,)), ((), ()))
TN = (((0,), (0,)), ((), ()))


def mul(left, right, dims=NN):
    return lax.dot_general(left, right, dims, preferred_element_type=F32)


def row_loop(count, step, body):
    def run(i, carry):
        body(pl.ds(pl.multiple_of(i * step, step), step))
        return carry
    lax.fori_loop(0, count // step, run, 0)


def normal(value):
    center = value - jnp.mean(value, axis=-1, keepdims=True)
    scale = lax.rsqrt(jnp.mean(center * center, axis=-1, keepdims=True) + EPS)
    return center * scale, scale


def fold(value):
    return value.reshape(value.shape[0] // 8, 8, value.shape[1]).sum(axis=0)


def norm_back(value, grad, gain):
    hat, scale = normal(value)
    d = grad * gain
    low = d - jnp.mean(d, axis=-1, keepdims=True) - hat * jnp.mean(d * hat, axis=-1, keepdims=True)
    return low * scale, hat


def params(limit=56, **kw):
    return pltpu.CompilerParams(vmem_limit_bytes=limit * 1024 * 1024, **kw)


def shape(rows, columns, dtype):
    return jax.ShapeDtypeStruct((rows, columns), dtype)


def spans(h):
    a, b = h * HEAD_DIM, (h + 1) * HEAD_DIM
    lo = a // 128 * 128
    hi = -(-b // 128) * 128
    return a, b, lo, hi

def head_mask(h, rows):
    a, b, lo, hi = spans(h)
    lane = lax.broadcasted_iota(jnp.int32, (rows, hi - lo), 1) + lo
    return (lane >= a) & (lane < b)

def attn_image(qkv, P, c, D, tok, factor):
    for h in range(HEADS):
        a, b, lo, hi = spans(h)
        mask = head_mask(h, tok)
        q = jnp.where(mask, qkv[:, lo:hi], 0)
        k = qkv[:, D + lo:D + hi]
        v = qkv[:, 2 * D + lo:2 * D + hi]
        s = mul(k, q, NT)
        e = jnp.exp2((s - jnp.max(s, axis=0, keepdims=True)) * factor)
        p = (e * (1.0 / jnp.sum(e, axis=0, keepdims=True))).astype(HALF)
        P[h] = p
        o = mul(p, v, TN).astype(HALF)
        if a > lo:
            c[:, lo:hi] = jnp.where(mask, o, c[:, lo:hi])
        else:
            c[:, lo:hi] = o

def attn_back_image(qkv, P, dc, out, D, tok, factor):
    for h in range(HEADS):
        a, b, lo, hi = spans(h)
        mask = head_mask(h, tok)
        q = qkv[:, lo:hi]
        k = qkv[:, D + lo:D + hi]
        v = qkv[:, 2 * D + lo:2 * D + hi]
        d = dc[:, lo:hi]
        p = P[h]
        dv = mul(p, d).astype(HALF)
        wide = p.astype(F32)
        dp = mul(v, jnp.where(mask, d, 0), NT)
        ds = (wide * (dp - jnp.sum(wide * dp, axis=0, keepdims=True))).astype(HALF)
        dk = (mul(ds, q) * factor).astype(HALF)
        dq = (mul(ds, k, TN) * factor).astype(HALF)
        for base, value in ((0, dq), (D, dk), (2 * D, dv)):
            if a > lo:
                out[:, base + lo:base + hi] = jnp.where(mask, value, out[:, base + lo:base + hi])
            else:
                out[:, base + lo:base + hi] = value


TILE = 512
LANES = 256


def pieces(width, step):
    return [(a, min(step, width - a)) for a in range(0, width, step)]


def tiles(width, step, body):
    whole = width // step
    def run(i, carry):
        body(pl.multiple_of(i * step, step), step)
        return carry
    lax.fori_loop(0, whole, run, 0)
    if width % step:
        body(whole * step, width % step)


def f_layer(slots, total, wide, x, vec, qb, ub, G, tok, kept):
    T, D = x.shape
    hidden = ub.shape[1]
    images = T // tok
    factor = HEAD_DIM ** (-0.5) * math.log2(math.e)
    root = math.sqrt(2.0 / math.pi)
    cut = pieces(4 * D, 768)
    plain, spare = 5, sum(b is not None for b in kept)
    chunk = T // 2 if T % 32 == 0 else T

    def kernel(slot, *refs):
        @pl.when(slot[1] == 1)
        def _():
            work(slot, *refs)

    def work(slot, *refs):
        x, vec, qb, ub, G = refs[:plain]
        (n1o, qkvo, Po, co, r1o, n2o, go, gpo, reso, y,
         wa, wb, n1, qkv, P, c, r1, n2, g, gp, res, wsem, psem, gsem, osem) = refs[plain + spare:]
        save = pl.ds(pl.multiple_of(slot[0] * T, 16), T)

        def weight(j):
            a, w = cut[j]
            return pltpu.make_async_copy(G.at[0, :, pl.ds(a, w)], wa.at[:, pl.ds(a, w)], wsem.at[j])
        up = pltpu.make_async_copy(G.at[1, :, pl.ds(0, hidden)], wb, wsem.at[len(cut)])
        down = pltpu.make_async_copy(G.at[2, :, pl.ds(0, hidden)], wa.at[:, pl.ds(0, hidden)], wsem.at[len(cut) + 1])
        for j in range(len(cut)):
            weight(j).start()
        up.start()

        def out(source, target, at, k):
            return pltpu.make_async_copy(source, target.at[at], osem.at[k])
        outs = [out(n1, n1o, save, 0), out(qkv, qkvo, save, 1), out(c, co, save, 2), out(r1, r1o, save, 3),
                out(n2, n2o, save, 4), out(g, go, (save, pl.ds(0, hidden)), 5), out(res, reso, save, 6)]

        def first(at):
            n1[at, :] = (normal(x[at, :].astype(F32))[0] * vec[0:1, :] + vec[1:2, :]).astype(HALF)
        row_loop(T, tok, first)
        outs[0].start()
        for j, (a, w) in enumerate(cut):
            weight(j).wait()
            if a < 3 * D:
                b = min(a + w, 3 * D)
                qkv[:, a:b] = (mul(n1[...], wa[:, a:b]) + qb[:, a:b]).astype(HALF)
        outs[1].start()

        def probs(i):
            return pltpu.make_async_copy(P.at[i % 2], Po.at[slot[0] * images + i], psem.at[i % 2])

        def image(i, carry):
            @pl.when(i >= 2)
            def _():
                probs(i - 2).wait()
            rows = pl.ds(pl.multiple_of(i * tok, 16), tok)
            attn_image(qkv.at[rows], P.at[i % 2], c.at[rows], D, tok, factor)
            probs(i).start()
            return carry
        lax.fori_loop(0, images, image, 0)
        outs[2].start()
        r1[...] = mul(c[...], wa[:, 3 * D:4 * D])
        down.start()

        def second(at):
            value = r1[at, :] + vec[4:5, :] + x[at, :].astype(F32)
            r1[at, :] = value
            n2[at, :] = (normal(value)[0] * vec[5:6, :] + vec[6:7, :]).astype(HALF)
        row_loop(T, tok, second)
        outs[3].start()
        outs[4].start()
        up.wait()

        def slope(i, size):
            return pltpu.make_async_copy(
                gp.at[lax.rem(i, 2), :, pl.ds(0, size)], gpo.at[save, pl.ds(pl.multiple_of(i * TILE, 128), size)],
                gsem.at[lax.rem(i, 2)])

        def rise(start, size):
            i = start // TILE
            @pl.when(i >= 2)
            def _():
                slope(i - 2, TILE).wait()
            at = pl.ds(start, size)
            for a in range(0, T, chunk):
                u = mul(n2[a:a + chunk, :], wb[:, at]) + ub[:, at]
                square = u * u
                t = jnp.tanh(u * (root + (root * 0.044715) * square))
                half = 0.5 + 0.5 * t
                g[a:a + chunk, at] = (u * half).astype(HALF)
                gp[lax.rem(i, 2), a:a + chunk, 0:size] = (
                    half + (0.5 * u) * (1.0 - t * t) * (root + (3.0 * root * 0.044715) * square)).astype(HALF)
            slope(i, size).start()
        tiles(hidden, TILE, rise)
        outs[5].start()
        down.wait()
        for a, w in pieces(D, LANES):
            at = slice(a, a + w)
            value = mul(g[...], wa[a:a + w, 0:hidden], NT) + (r1[:, at] + vec[7:8, at])
            res[:, at] = value
            y[:, at] = value.astype(HALF)
        outs[6].start()
        for copy in outs:
            copy.wait()
        for i in range(max(0, images - 2), images):
            probs(i).wait()
        count = -(-hidden // TILE)
        for i in range(max(0, count - 2), count):
            slope(i, min(TILE, hidden - i * TILE)).wait()

    aliases = {}
    ins = [x, vec, qb, ub, G]
    for index, buffer in enumerate(kept):
        if buffer is not None:
            aliases[1 + len(ins)] = index
            ins.append(buffer)
    dma = pltpu.SemaphoreType.DMA
    whole = pl.BlockSpec(memory_space=pltpu.VMEM)
    return pl.pallas_call(
        kernel,
        out_shape=(shape(total, D, HALF), shape(total, 3 * D, HALF),
                   jax.ShapeDtypeStruct((total // tok, HEADS, tok, tok), HALF), shape(total, D, HALF), shape(total, D, F32),
                   shape(total, D, HALF), shape(total, wide, HALF), shape(total, hidden, HALF), shape(total, D, F32),
                   shape(T, D, HALF)),
        grid_spec=pltpu.PrefetchScalarGridSpec(
            num_scalar_prefetch=1, grid=(1,), in_specs=[whole] * 4 + [ANY] * (1 + spare), out_specs=(ANY,) * 9 + (whole,),
            scratch_shapes=[
                pltpu.VMEM((D, 4 * D), HALF), pltpu.VMEM((D, hidden), HALF), pltpu.VMEM((T, D), HALF),
                pltpu.VMEM((T, 3 * D), HALF), pltpu.VMEM((2, HEADS, tok, tok), HALF), pltpu.VMEM((T, D), HALF),
                pltpu.VMEM((T, D), F32), pltpu.VMEM((T, D), HALF), pltpu.VMEM((T, hidden), HALF),
                pltpu.VMEM((2, T, TILE), HALF), pltpu.VMEM((T, D), F32),
                dma((len(cut) + 2,)), dma((2,)), dma((2,)), dma((7,))]),
        input_output_aliases=aliases,
        compiler_params=params(60),
        cost_estimate=pl.CostEstimate(flops=T * D, bytes_accessed=T * D, transcendentals=0),
    )(slots, *ins)


def d_layer(slots, total, wide, final, e, x, vec, G, GP, R1, QKV, PP, tok, kept):
    T, D = x.shape
    hidden = GP.shape[1]
    images = T // tok
    scale = HEAD_DIM ** (-0.5)
    plain, spare = 8, sum(b is not None for b in kept)
    chunk = T // 2 if T % 32 == 0 else T

    def kernel(slot, *refs):
        @pl.when(slot[1] == 1)
        def _():
            work(slot, *refs)

    def work(slot, *refs):
        e, x, vec, G, GP, R1, QKV, PP = refs[:plain]
        (duo, lowo, dqkvo, reso, dx, stats, sums,
         wa, wb, gp, r1, qkv, P, du, grad, dr1, low, dc, dqkv, wsem, psem, isem, osem) = refs[plain + spare:]
        save = pl.ds(pl.multiple_of(slot[0] * T, 16), T)
        cuts = pieces(hidden, 2 * TILE)
        down = [pltpu.make_async_copy(G.at[2, :, pl.ds(a, w)], wa.at[:, pl.ds(a, w)], wsem.at[2 + j]) for j, (a, w) in enumerate(cuts)]
        slope = [pltpu.make_async_copy(GP.at[save, pl.ds(a, w)], gp.at[:, pl.ds(a, w)], isem.at[2 + j]) for j, (a, w) in enumerate(cuts)]
        up = pltpu.make_async_copy(G.at[1, :, pl.ds(0, hidden)], wb, wsem.at[0])
        rest = pltpu.make_async_copy(G.at[0, :, pl.ds(0, 4 * D)], wa, wsem.at[1])
        loads = [pltpu.make_async_copy(R1.at[save], r1, isem.at[0]), pltpu.make_async_copy(QKV.at[save], qkv, isem.at[1])]
        for weight, factor in zip(down, slope):
            weight.start()
            factor.start()
        up.start()
        for copy in loads:
            copy.start()

        def out(source, target, at, k):
            return pltpu.make_async_copy(source, target.at[at], osem.at[k])
        outs = [out(du, duo, (save, pl.ds(0, hidden)), 0), out(low, lowo, save, 1), out(dqkv, dqkvo, save, 2)]
        if final:
            outs.append(out(dr1, reso, save, 3))

        def probs(i):
            return pltpu.make_async_copy(PP.at[slot[0] * images + i], P.at[i % 2], psem.at[i % 2])
        for i in range(min(2, images)):
            probs(i).start()
        stats[...] = jnp.zeros_like(stats)

        def fall(start, size):
            at = pl.ds(start, size)
            total = None
            for a in range(0, T, chunk):
                d = (mul(e[a:a + chunk, :], wa[:, at]) * gp[a:a + chunk, at].astype(F32)).astype(HALF)
                du[a:a + chunk, at] = d
                part = jnp.sum(d.astype(F32), axis=0, keepdims=True)
                total = part if total is None else total + part
            sums[:, at] = total
        for j, (a, w) in enumerate(cuts):
            down[j].wait()
            slope[j].wait()
            for b in range(a, a + w, TILE):
                fall(b, min(TILE, a + w - b))
        rest.start()
        outs[0].start()
        up.wait()
        for a, w in pieces(D, LANES):
            grad[:, a:a + w] = mul(du[...], wb[a:a + w, :], NT)
        loads[0].wait()

        def second(at):
            g = grad[at, :]
            part, hat = norm_back(r1[at, :], g, vec[5:6, :])
            eb = e[at, :].astype(F32)
            value = eb + part
            rounded = value.astype(HALF)
            dr1[at, :] = value
            low[at, :] = rounded
            stats[0] += fold(g * hat)
            stats[1] += fold(g)
            stats[2] += fold(rounded.astype(F32))
            stats[3] += fold(eb)
        row_loop(T, tok, second)
        outs[1].start()
        rest.wait()
        for a, w in pieces(D, LANES):
            dc[:, a:a + w] = mul(low[...], wa[a:a + w, 3 * D:4 * D], NT).astype(HALF)
        loads[1].wait()

        def image(i, carry):
            probs(i).wait()
            rows = pl.ds(pl.multiple_of(i * tok, 16), tok)
            attn_back_image(qkv.at[rows], P.at[i % 2], dc.at[rows], dqkv.at[rows], D, tok, scale)
            @pl.when(i + 2 < images)
            def _():
                probs(i + 2).start()
            return carry
        lax.fori_loop(0, images, image, 0)
        outs[2].start()
        for a, w in pieces(D, LANES):
            grad[:, a:a + w] = mul(dqkv[...], wa[a:a + w, 0:3 * D], NT)

        def first(at):
            g = grad[at, :]
            part, hat = norm_back(x[at, :].astype(F32), g, vec[0:1, :])
            value = dr1[at, :] + part
            dr1[at, :] = value
            dx[at, :] = value.astype(HALF)
            stats[4] += fold(g * hat)
            stats[5] += fold(g)
            stats[6] += fold(dqkv[at, 0:D].astype(F32))
            stats[7] += fold(dqkv[at, 2 * D:3 * D].astype(F32))
        row_loop(T, tok, first)
        if final:
            outs[3].start()
        for copy in outs:
            copy.wait()

    aliases = {}
    ins = [e, x, vec, G, GP, R1, QKV, PP]
    for index, buffer in enumerate(kept):
        if buffer is not None:
            aliases[1 + len(ins)] = index
            ins.append(buffer)
    dma = pltpu.SemaphoreType.DMA
    whole = pl.BlockSpec(memory_space=pltpu.VMEM)
    return pl.pallas_call(
        kernel,
        out_shape=(shape(total, wide, HALF), shape(total, D, HALF), shape(total, 3 * D, HALF), shape(total, D, F32),
                   shape(T, D, HALF), jax.ShapeDtypeStruct((8, 8, D), F32), shape(1, hidden, F32)),
        grid_spec=pltpu.PrefetchScalarGridSpec(
            num_scalar_prefetch=1, grid=(1,), in_specs=[whole] * 3 + [ANY] * (5 + spare), out_specs=(ANY,) * 4 + (whole,) * 3,
            scratch_shapes=[
                pltpu.VMEM((D, 4 * D), HALF), pltpu.VMEM((D, hidden), HALF), pltpu.VMEM((T, hidden), HALF),
                pltpu.VMEM((T, D), F32), pltpu.VMEM((T, 3 * D), HALF), pltpu.VMEM((2, HEADS, tok, tok), HALF),
                pltpu.VMEM((T, hidden), HALF), pltpu.VMEM((T, D), F32), pltpu.VMEM((T, D), F32), pltpu.VMEM((T, D), HALF),
                pltpu.VMEM((T, D), HALF), pltpu.VMEM((T, 3 * D), HALF),
                dma((2 + len(pieces(hidden, 2 * TILE)),)), dma((2,)), dma((2 + len(pieces(hidden, 2 * TILE)),)), dma((4,))]),
        input_output_aliases=aliases,
        compiler_params=params(60),
        cost_estimate=pl.CostEstimate(flops=T * D, bytes_accessed=T * D, transcendentals=0),
    )(slots, *ins)


def powers(count):
    bits = []
    bit = count // 2
    while bit:
        bits.append(bit)
        bit //= 2
    return bits

def gather_kernel(n, R, qkv, out, up, down, small, G, S, stage, stage_small, lsem, ssem, rsem, small_send, small_recv):
    z = lax.axis_index("fsdp")
    r = lax.axis_index("replica")
    rows, wide = up.shape
    part = wide // R
    bits = powers(R)
    barrier = pltpu.get_barrier_semaphore()
    for hop in range(1, n):
        pl.semaphore_signal(barrier, inc=1, device_id={"fsdp": lax.rem(z + hop, n)}, device_id_type=MESH)
    for bit in bits:
        pl.semaphore_signal(barrier, inc=1, device_id={"replica": r ^ bit}, device_id_type=MESH)
    mine = pl.ds(pl.multiple_of(z * rows, 16), rows)
    first = qkv.shape[1]
    local = [
        pltpu.make_async_copy(qkv, stage.at[0, :, pl.ds(0, first)], lsem.at[0]),
        pltpu.make_async_copy(out, stage.at[0, :, pl.ds(first, out.shape[1])], lsem.at[1]),
        pltpu.make_async_copy(up, stage.at[1], lsem.at[2]),
        pltpu.make_async_copy(down, stage.at[2], lsem.at[3]),
        pltpu.make_async_copy(small, stage_small, lsem.at[4]),
    ]
    for copy in local:
        copy.start()
    keep = [pltpu.make_async_copy(stage.at[group], G.at[group, mine], lsem.at[5 + group]) for group in range(3)]
    keep.append(pltpu.make_async_copy(stage_small, S.at[z], lsem.at[8]))
    pl.semaphore_wait(barrier, n - 1 + len(bits))

    def piece(group, source, column):
        return G.at[group, pl.ds(pl.multiple_of(source * rows, 16), rows),
                    pl.ds(pl.multiple_of(column * part, 128), part)]

    def send(group, source, column, kind, target, origin=None):
        return pltpu.make_async_remote_copy(
            src_ref=piece(group, source, column) if origin is None else origin, dst_ref=piece(group, source, column),
            send_sem=ssem.at[group, source, column, kind], recv_sem=rsem.at[group, source, column],
            device_id=target, device_id_type=MESH)

    def to_right(group, source, origin=None):
        return send(group, source, r, 0, {"fsdp": z + 1}, origin)

    def to_left(group, source, origin=None):
        return send(group, source, r, 1, {"fsdp": z - 1}, origin)

    def own(group):
        return stage.at[group, :, pl.ds(pl.multiple_of(r * part, 128), part)]

    def share(group, source, column, level):
        return send(group, source, column, 2 + level, {"replica": r ^ bits[level]})

    def arrived(group, source, column):
        send(group, source, column, 0, {"replica": r ^ bits[0]}).wait_recv()

    def small_to(hop):
        return pltpu.make_async_remote_copy(
            src_ref=small, dst_ref=S.at[z], send_sem=small_send.at[hop],
            recv_sem=small_recv.at[z], device_id={"fsdp": lax.rem(z + hop, n)}, device_id_type=MESH)
    for hop in range(1, n):
        small_to(hop).start()
    for group in range(3):
        if group == 0:
            local[0].wait()
            local[1].wait()
        else:
            local[1 + group].wait()
        @pl.when(z + 1 < n)
        def _():
            to_right(group, z, own(group)).start()
        @pl.when(z > 0)
        def _():
            to_left(group, z, own(group)).start()
        keep[group].start()
    local[4].wait()
    keep[3].start()
    columns = {}
    for level, bit in enumerate(bits):
        masks = [0]
        for upper in bits[:level]:
            masks = masks + [m | upper for m in masks]
        columns[level] = [bit | m for m in masks]
    steps = [(hop, group) for hop in range(1, n) for group in range(3)]
    for turn in range(len(steps) + len(bits)):
        for level in range(-1, len(bits)):
            place = turn - 1 - level
            if place < 0 or place >= len(steps):
                continue
            hop, group = steps[place]
            for sign in (-1, 1):
                source = z + sign * hop
                @pl.when((source >= 0) & (source < n))
                def _():
                    if level < 0:
                        arrived(group, source, r)
                        for lower in range(len(bits)):
                            share(group, source, r, lower).start()
                        if sign < 0:
                            @pl.when(z + 1 < n)
                            def _():
                                to_right(group, source).start()
                        else:
                            @pl.when(z > 0)
                            def _():
                                to_left(group, source).start()
                    else:
                        for mask in columns[level]:
                            arrived(group, source, r ^ mask)
                            for lower in range(level + 1, len(bits)):
                                share(group, source, r ^ mask, lower).start()
    for copy in keep:
        copy.wait()
    for hop in range(1, n):
        pltpu.make_async_remote_copy(
            src_ref=small, dst_ref=S.at[lax.rem(z + hop, n)], send_sem=small_send.at[hop],
            recv_sem=small_recv.at[lax.rem(z + hop, n)], device_id={"fsdp": lax.rem(z + hop, n)}, device_id_type=MESH).wait_recv()
        small_to(hop).wait_send()
    for group in range(3):
        for source in range(n):
            @pl.when((source <= z) & (z + 1 < n))
            def _():
                to_right(group, source).wait_send()
            @pl.when((source >= z) & (z > 0))
            def _():
                to_left(group, source).wait_send()
            @pl.when(source != z)
            def _():
                for level in range(len(bits)):
                    share(group, source, r, level).wait_send()
                for level in range(len(bits)):
                    for mask in columns[level]:
                        for lower in range(level + 1, len(bits)):
                            share(group, source, r ^ mask, lower).wait_send()

def gather_weights(n, R, qkv, out, up, down, small):
    rows, wide = up.shape
    kinds = 2 + len(powers(R))
    return pl.pallas_call(
        functools.partial(gather_kernel, n, R),
        out_shape=(jax.ShapeDtypeStruct((3, n * rows, wide), qkv.dtype),
                   jax.ShapeDtypeStruct((n,) + small.shape, small.dtype)),
        in_specs=[pl.BlockSpec(memory_space=pl.ANY)] * 5,
        out_specs=(pl.BlockSpec(memory_space=pl.ANY),) * 2,
        scratch_shapes=[
            pltpu.VMEM((3, rows, wide), qkv.dtype),
            pltpu.VMEM(small.shape, small.dtype),
            pltpu.SemaphoreType.DMA((9,)),
            pltpu.SemaphoreType.DMA((3, n, R, kinds)),
            pltpu.SemaphoreType.DMA((3, n, R)),
            pltpu.SemaphoreType.DMA((n,)),
            pltpu.SemaphoreType.DMA((n,)),
        ],
        compiler_params=pltpu.CompilerParams(collective_id=0, has_side_effects=True, vmem_limit_bytes=32 * 1024 * 1024),
    )(qkv, out, up, down, small)


ORDER = (2, 1, 0)


def plan(R, part, D):
    found = []
    for place in range(3):
        edges = (3 * D, 4 * D) if ORDER[place] == 0 else ()
        sizes, at = [], 0
        while at < part:
            size = min(max(12 // R, 1) * 128, part - at)
            while any(p * part + at < edge < p * part + at + size for p in range(R) for edge in edges):
                size -= 128
            sizes.append(size)
            at += size
        if place == 0 and sizes[0] == 384:
            sizes[:1] = [128, 256]
        if place == 2 and sizes[-1] > 128:
            sizes[-1:] = [sizes[-1] - 128, 128]
        at = 0
        for size in sizes:
            found.append((place, at, size))
            at += size
    return found


def ahead_of_pairs(k, L):
    return L >= 2 and k % 3 == 2


def places(chunks, L):
    every, kind, counts = [], [], [0, 0, 0]
    for k, (_, _, size) in enumerate(chunks):
        which = int(ahead_of_pairs(k, L))
        every.append(counts[2])
        kind.append(counts[which])
        counts[which] += size
        counts[2] += size
    return every, kind, counts


def reduce_kernel(n, R, chunks, small_in, n1, c, n2, eb, dqkv, low, du, g, F, small_out, *scratch):
    L = R.bit_length() - 1
    bits = [1 << level for level in range(L)]
    held = scratch[:L]
    (X, left, stage, right, flow, flow_two, pair, small_z, small_r, small_sum, rsem, lsem, send_sem, recv_sem, zsend, zrecv,
     psend, precv, fsend, frecv, fkeep, ss_z, sr_z, ss_r, sr_r, ss_l) = scratch[L:]
    z = lax.axis_index("fsdp")
    r = lax.axis_index("replica")
    tokens, D = n1.shape
    full = D
    rows = full // n
    wide = F.shape[2]
    part = wide // R
    K = len(chunks)
    every, kind, _ = places(chunks, L)
    barrier = pltpu.get_barrier_semaphore()
    for hop in range(1, n):
        pl.semaphore_signal(barrier, inc=1, device_id={"fsdp": lax.rem(z + hop, n)}, device_id_type=MESH)
    for hop in range(1, R):
        pl.semaphore_signal(barrier, inc=1, device_id={"replica": lax.rem(r + hop, R)}, device_id_type=MESH)

    def group(k):
        return ORDER[chunks[k][0]]

    def columns(k, p):
        return pl.ds(pl.multiple_of(p * part + chunks[k][1], 128), chunks[k][2])

    def part_lanes(k, p):
        return pl.ds(pl.multiple_of(p * chunks[k][2], 128), chunks[k][2])

    def block(t):
        return pl.ds(pl.multiple_of(t * rows, 16), rows)

    def kept(level, j):
        return (r & ((2 << level) - 1)) | (j << (level + 1))

    def factors(k, p):
        a, sub = p * part + chunks[k][1], chunks[k][2]
        if group(k) == 2:
            return 0, g.at[:, pl.ds(a, sub)]
        if group(k) == 1:
            return 1, du.at[:, pl.ds(a, sub)]
        if a < 3 * D:
            return 0, dqkv.at[:, pl.ds(a, sub)]
        if a < 4 * D:
            return 1, low.at[:, pl.ds(a - 3 * D, sub)]
        return None, None

    def fetch(k, p):
        return pltpu.make_async_copy(factors(k, p)[1], right.at[:, pl.ds(p * chunks[k][2], chunks[k][2])], rsem.at[p])

    def fetch_all(k):
        for p in range(R):
            if factors(k, p)[1] is not None:
                fetch(k, p).start()

    def fetch_left(which):
        return pltpu.make_async_copy((eb, n2, n1, c)[which], stage, lsem)

    def turn_left(which):
        fetch_left(which).wait()
        for a in range(0, D, 128):
            left[which % 2, a:a + 128, :] = stage[:, a:a + 128].T
        if which < 3:
            fetch_left(which + 1).start()

    def own(k):
        if k >= 2:
            for j in range(R // 2):
                give(0, k - 2, j).wait_send()
        if chunks[k][1] == 0:
            turn_left(chunks[k][0])
            if chunks[k][0] == 2:
                turn_left(3)
        size = chunks[k][2]
        runs = []
        for p in range(R):
            slot, source = factors(k, p)
            if source is None:
                continue
            fetch(k, p).wait()
            if runs and runs[-1][0] == slot:
                runs[-1][2] = p + 1
            else:
                runs.append([slot, p, p + 1])
        for slot, first, end in runs:
            def body(i, carry):
                at = pl.ds(pl.multiple_of(i * 288, 16), 288)
                X[k % 2, at, first * size:end * size] = mul(
                    left[slot, at, :], right[:, first * size:end * size]).astype(X.dtype)
                return carry
            lax.fori_loop(0, full // 288, body, 0)
        if k + 1 < K:
            fetch_all(k + 1)
        for j in range(R // 2):
            give(0, k, j).start()

    def store(level, k, j):
        return held[level].at[j, :, pl.ds(kind[k] if level == L - 1 else every[k], chunks[k][2])]

    def give(level, k, j):
        if level == 0:
            source = X.at[k % 2, :, part_lanes(k, ((r ^ 1) & 1) | (j << 1))]
        else:
            source = store(level - 1, k, 2 * j + (((r >> level) & 1) ^ 1))
        return pltpu.make_async_remote_copy(
            src_ref=source, dst_ref=store(level, k, j), send_sem=send_sem.at[level, k, j],
            recv_sem=recv_sem.at[level, k, j], device_id={"replica": r ^ bits[level]}, device_id_type=MESH)

    STEP = 96

    def merge(level, k):
        for j in range(R >> (level + 1)):
            give(level, k, j).wait_recv()
            mine = store(level, k, j)
            other = X.at[k % 2, :, part_lanes(k, kept(0, j))] if level == 0 else store(level - 1, k, 2 * j + ((r >> level) & 1))

            def body(i, carry):
                at = pl.ds(pl.multiple_of(i * STEP, 16), STEP)
                mine[at, :] = (mine[at, :].astype(F32) + other[at, :].astype(F32)).astype(mine.dtype)
                return carry
            lax.fori_loop(0, full // STEP, body, 0)
        if level + 1 < last(k):
            for j in range(R >> (level + 2)):
                give(level + 1, k, j).start()

    def last(k):
        return L - 1 if ahead_of_pairs(k, L) else L

    def lanes(k):
        return range(2) if ahead_of_pairs(k, L) else range(1)

    def total(k, j):
        return store(L - 2, k, j) if ahead_of_pairs(k, L) else store(L - 1, k, 0)

    def moving(k, side, t, j):
        place = t - 1 if side == 0 else t
        at = pl.ds(kind[k], chunks[k][2])
        return flow_two.at[side, place, j, :, at] if ahead_of_pairs(k, L) else flow.at[side, place, :, at]

    def pass_on(k, t, side, j, source):
        return pltpu.make_async_remote_copy(
            src_ref=source, dst_ref=moving(k, side, t, j), send_sem=zsend.at[k, side, t, j], recv_sem=zrecv.at[k, side, t, j],
            device_id={"fsdp": z + 1 if side == 0 else z - 1}, device_id_type=MESH)

    def launch(k):
        @pl.when(z == 0)
        def _():
            for t in range(n - 1, 0, -1):
                for j in lanes(k):
                    pass_on(k, t, 0, j, total(k, j).at[block(t), :]).start()
        @pl.when(z == n - 1)
        def _():
            for t in range(n - 1):
                for j in lanes(k):
                    pass_on(k, t, 1, j, total(k, j).at[block(t), :]).start()

    RSTEP = 96 if rows % 96 == 0 else 16

    def add_block(target, other, at_other):
        def body(i, carry):
            at = pl.ds(pl.multiple_of(i * RSTEP, 16), RSTEP)
            there = pl.ds(pl.multiple_of(at_other + i * RSTEP, 16), RSTEP)
            target[at, :] = (target[at, :].astype(F32) + other[there, :].astype(F32)).astype(target.dtype)
            return carry
        lax.fori_loop(0, rows // RSTEP, body, 0)

    def flows(k, hop):
        @pl.when(z == hop)
        def _():
            for t in range(n - 1, hop - 1, -1):
                for j in lanes(k):
                    here = moving(k, 0, t, j)
                    pass_on(k, t, 0, j, here).wait_recv()
                    add_block(here, total(k, j), t * rows)
                    if t > hop:
                        pass_on(k, t, 0, j, here).start()
        @pl.when(z == n - 1 - hop)
        def _():
            for t in range(n - hop):
                for j in lanes(k):
                    here = moving(k, 1, t, j)
                    pass_on(k, t, 1, j, here).wait_recv()
                    if t < n - 1 - hop or hop == n - 1:
                        add_block(here, total(k, j), t * rows)
                    if t < n - 1 - hop:
                        pass_on(k, t, 1, j, here).start()
        if hop == n - 1:
            for j in lanes(k):
                @pl.when((z > 0) & (z < n - 1))
                def _():
                    add_block(moving(k, 1, z, j), moving(k, 0, z, j), 0)

    def both_ends(act):
        @pl.when(z < n - 1)
        def _():
            act(1)
        @pl.when(z == n - 1)
        def _():
            act(0)

    def bit(k):
        return (r >> (L - 1)) & 1

    def trade(k, side):
        return pltpu.make_async_remote_copy(
            src_ref=moving(k, side, z, 1 - bit(k)), dst_ref=pair.at[:, pl.ds(kind[k], chunks[k][2])], send_sem=psend.at[k],
            recv_sem=precv.at[k], device_id={"replica": r ^ bits[L - 1]}, device_id_type=MESH)

    def complete(k):
        def act(side):
            trade(k, side).wait_recv()
            add_block(moving(k, side, z, bit(k)), pair.at[:, pl.ds(kind[k], chunks[k][2])], 0)
        both_ends(act)

    def finished(k, p):
        return F.at[group(k), :, columns(k, p)]

    def share(k, p, level, source=None):
        return pltpu.make_async_remote_copy(
            src_ref=finished(k, p) if source is None else source, dst_ref=finished(k, p),
            send_sem=fsend.at[k, p, level], recv_sem=frecv.at[k, p], device_id={"replica": r ^ bits[level]}, device_id_type=MESH)

    def done(k, side):
        return moving(k, side, z, bit(k) if ahead_of_pairs(k, L) else 0)

    def keep(k, side):
        return pltpu.make_async_copy(done(k, side), finished(k, r), fkeep.at[k])

    def publish(k):
        def act(side):
            for level in reversed(range(L)):
                share(k, r, level, done(k, side)).start()
            keep(k, side).start()
        both_ends(act)

    def masks(level):
        found = [0]
        for upper in range(level + 1, L):
            found = found + [m | bits[upper] for m in found]
        return [m | bits[level] for m in found]

    def collect(level, k):
        for mask in masks(level):
            p = r ^ mask
            share(k, p, level).wait_recv()
            for lower in reversed(range(level)):
                share(k, p, lower).start()

    def small_to_z(t):
        return pltpu.make_async_remote_copy(
            src_ref=small_in.at[t], dst_ref=small_z.at[z], send_sem=ss_z.at[t], recv_sem=sr_z.at[z],
            device_id={"fsdp": t}, device_id_type=MESH)

    def small_to_r(p):
        return pltpu.make_async_remote_copy(
            src_ref=small_sum, dst_ref=small_r.at[r], send_sem=ss_r.at[p], recv_sem=sr_r.at[r],
            device_id={"replica": p}, device_id_type=MESH)

    fetch_left(0).start()
    fetch_all(0)
    pl.semaphore_wait(barrier, n - 1 + R - 1)
    own_small = pltpu.make_async_copy(small_in.at[z], small_z.at[z], ss_l)
    own_small.start()
    own(0)
    for hop in range(1, n):
        small_to_z(lax.rem(z + hop, n)).start()
    stages = L + n + L
    for turn in range(K + stages - 1):
        for stage_index in [1, 0] + list(range(2, stages)):
            k = turn - stage_index
            if k < 0 or k >= K:
                continue
            hop = stage_index - last(k)
            if stage_index == 0:
                if k > 0:
                    own(k)
            elif stage_index <= last(k):
                merge(stage_index - 1, k)
                if stage_index == last(k):
                    launch(k)
            elif hop < n:
                flows(k, hop)
                if hop == n - 1:
                    if ahead_of_pairs(k, L):
                        both_ends(lambda side: trade(k, side).start())
                    else:
                        publish(k)
            elif stage_index == L + n - 1:
                complete(k)
                publish(k)
            else:
                collect(L - 1 - (stage_index - L - n), k)
        if turn == 1:
            own_small.wait()
            for hop in range(1, n):
                source = lax.rem(z + hop, n)
                pltpu.make_async_remote_copy(
                    src_ref=small_in.at[source], dst_ref=small_z.at[source], send_sem=ss_z.at[source],
                    recv_sem=sr_z.at[source], device_id={"fsdp": source}, device_id_type=MESH).wait_recv()
            together = small_z[0]
            for t in range(1, n):
                together = together + small_z[t]
            small_sum[...] = together
            small_r[r] = together
            for hop in range(1, R):
                small_to_r(lax.rem(r + hop, R)).start()
    for hop in range(1, R):
        p = lax.rem(r + hop, R)
        pltpu.make_async_remote_copy(
            src_ref=small_sum, dst_ref=small_r.at[p], send_sem=ss_r.at[p], recv_sem=sr_r.at[p],
            device_id={"replica": p}, device_id_type=MESH).wait_recv()
    together = small_r[0]
    for p in range(1, R):
        together = together + small_r[p]
    small_out[...] = together
    for hop in range(1, R):
        small_to_r(lax.rem(r + hop, R)).wait_send()
    for hop in range(1, n):
        small_to_z(lax.rem(z + hop, n)).wait_send()
    for k in range(K):
        for level in range(last(k)):
            if level == 0 and k < K - 2:
                continue
            for j in range(R >> (level + 1)):
                give(level, k, j).wait_send()
        for t in range(n):
            for j in lanes(k):
                if t > 0:
                    @pl.when(t > z)
                    def _():
                        pass_on(k, t, 0, j, moving(k, 0, t, j)).wait_send()
                if t < n - 1:
                    @pl.when(t < z)
                    def _():
                        pass_on(k, t, 1, j, moving(k, 1, t, j)).wait_send()
        if ahead_of_pairs(k, L):
            both_ends(lambda side: trade(k, side).wait_send())
        both_ends(lambda side: keep(k, side).wait())
        for level in range(L):
            share(k, r, level).wait_send()
            for mask in masks(level):
                for lower in range(level):
                    share(k, r ^ mask, lower).wait_send()


def reduce_grads(n, R, wide, small, n1, c, n2, eb, dqkv, low, du, g):
    tokens, D = n1.shape
    rows = D // n
    part = wide // R
    chunks = plan(R, part, D)
    K = len(chunks)
    most = max(size for _, _, size in chunks)
    L = R.bit_length() - 1
    one, two, both = places(chunks, L)[2]
    two = max(two, 128)
    dma = pltpu.SemaphoreType.DMA
    return pl.pallas_call(
        functools.partial(reduce_kernel, n, R, chunks),
        out_shape=(jax.ShapeDtypeStruct((3, rows, wide), HALF),
                   jax.ShapeDtypeStruct(small.shape[1:], small.dtype)),
        in_specs=[pl.BlockSpec(memory_space=pltpu.VMEM)] + [ANY] * 8,
        out_specs=(ANY, pl.BlockSpec(memory_space=pltpu.VMEM)),
        scratch_shapes=[pltpu.VMEM((R >> (level + 1), D, one if level == L - 1 else both), HALF) for level in range(L)] + [
            pltpu.VMEM((2, D, R * most), HALF),
            pltpu.VMEM((2, D, tokens), HALF),
            pltpu.VMEM((tokens, D), HALF),
            pltpu.VMEM((tokens, R * most), HALF),
            pltpu.VMEM((2, n - 1, rows, one), HALF),
            pltpu.VMEM((2, n - 1, 2, rows, two), HALF),
            pltpu.VMEM((rows, two), HALF),
            pltpu.VMEM((n,) + small.shape[1:], small.dtype),
            pltpu.VMEM((R,) + small.shape[1:], small.dtype),
            pltpu.VMEM(small.shape[1:], small.dtype),
            dma((R,)), dma(()),
            dma((L, K, R // 2)), dma((L, K, R // 2)),
            dma((K, 2, n, 2)), dma((K, 2, n, 2)),
            dma((K,)), dma((K,)),
            dma((K, R, L)), dma((K, R)), dma((K,)),
            dma((n,)), dma((n,)), dma((R,)), dma((R,)), dma(()),
        ],
        compiler_params=pltpu.CompilerParams(collective_id=1, has_side_effects=True, vmem_limit_bytes=62 * 1024 * 1024),
    )(small, n1, c, n2, eb, dqkv, low, du, g)


def shifted(value, axis, steps):
    count = lax.axis_size(axis)
    first, last = (max(0, -steps), min(count, count - steps))
    return lax.ppermute(value, axis, [(source, source + steps) for source in range(first, last)])


def pad_columns(value, wide):
    return jnp.pad(value, ((0, 0), (0, wide - value.shape[1])))


def on_device(ends, first_gain, first_shift, qkv_weight, qv_bias, out_weight, out_bias, second_gain, second_shift,
              up_weight, up_bias, down_weight, down_bias):
    n, R = lax.axis_size("fsdp"), lax.axis_size("replica")
    section = lax.axis_index("section")
    at_first = section == 0
    _, images, tok, D = ends.shape
    hidden = up_weight.shape[2]
    piece = D // n
    unit = 128 * R
    filled = -(-hidden // LANES) * LANES
    wide = max(-(-4 * D // unit), -(-filled // unit)) * unit

    vector = jnp.concatenate([first_gain[0], first_shift[0], qv_bias[0, 0], qv_bias[0, 1], out_bias[0], second_gain[0],
                              second_shift[0], down_bias[0], up_bias[0]])
    lanes = -(-vector.shape[0] // (16 * 128)) * 128
    small = jnp.pad(vector, (0, 16 * lanes - vector.shape[0])).reshape(16, lanes)
    G, S = gather_weights(n, R, qkv_weight[0], out_weight[0], pad_columns(up_weight[0], wide),
                          pad_columns(down_weight[0].T, wide), small)
    S = S.reshape(n, -1).astype(F32)
    vec = S[:, : 8 * piece].reshape(n, 8, piece).transpose(1, 0, 2).reshape(8, D)
    ub = pad_columns(S[:, 8 * piece : 8 * piece + hidden // n].reshape(1, hidden), filled)
    qb = jnp.concatenate([vec[2], jnp.zeros_like(vec[2]), vec[3]])[None]

    rows = ends[0].reshape(images * tok, D)
    T = images // MICRO * tok
    total = MICRO * T
    parts = [rows[m * T : (m + 1) * T] for m in range(MICRO)]
    here = section.astype(jnp.int32)

    def turn(micro, where):
        return jnp.stack([jnp.int32(micro), (here == where).astype(jnp.int32)])

    kept = (None,) * 9
    sent = []
    for micro in range(MICRO):
        *kept, y = f_layer(turn(micro, 0), total, wide, parts[micro], vec, qb, ub, G, tok, kept)
        sent.append(shifted(y, "section", 1))
    for micro in range(MICRO):
        *kept, y = f_layer(turn(micro, 1), total, wide, sent[micro], vec, qb, ub, G, tok, kept)
    n1, qkv, probs, c, r1, n2, g, gp, result = kept

    kept = (None, None, None, result)
    back = []
    stats, sums = [], []
    for where in (1, 0):
        for micro in range(MICRO):
            e, x = (parts[micro], sent[micro]) if where else (back[micro], parts[micro])
            *kept, dx, stat, part = d_layer(turn(micro, where), total, wide, where == 0, e, x, vec, G, gp, r1, qkv, probs, tok, kept)
            stats.append(stat)
            sums.append(part)
            if where:
                back.append(shifted(dx, "section", -1))
    du, low, dqkv, result = kept
    stats = sum(jnp.where(at_first, below, above) for above, below in zip(stats[:MICRO], stats[MICRO:]))
    sums = sum(jnp.where(at_first, below, above) for above, below in zip(sums[:MICRO], sums[MICRO:]))
    eb = jnp.where(at_first, jnp.concatenate(back), rows)

    stats = stats.sum(axis=1)
    vectors = jnp.stack([stats[4], stats[5], stats[6], stats[7], stats[2], stats[0], stats[1], stats[3]])
    vectors = vectors.reshape(8, n, piece).transpose(1, 0, 2).reshape(n, 8 * piece)
    vectors = jnp.concatenate([vectors, sums[0, :hidden].reshape(n, hidden // n)], axis=1)
    lanes = -(-vectors.shape[1] // (16 * 128)) * 128
    small = jnp.pad(vectors, ((0, 0), (0, 16 * lanes - vectors.shape[1]))).reshape(n, 16, lanes)
    F, s = reduce_grads(n, R, wide, small, n1, c, n2, eb, dqkv, low, du, g)
    s = s.reshape(-1)
    v = s[: 8 * piece].reshape(8, piece)
    return (
        result.reshape(1, images, tok, D),
        v[0][None],
        v[1][None],
        F[0, :, : 3 * D].astype(F32)[None],
        v[2:4][None],
        F[0, :, 3 * D : 4 * D].astype(F32)[None],
        v[4][None],
        v[5][None],
        v[6][None],
        F[1, :, :hidden].astype(F32)[None],
        s[8 * piece : 8 * piece + hidden // n][None],
        F[2, :, :hidden].T.astype(F32)[None],
        v[7][None],
    )


def solution(mesh):
    placed = (
        P("section", ("fsdp", "replica"), None, None),
        P("section", "fsdp"),
        P("section", "fsdp"),
        P("section", "fsdp", None),
        P("section", None, "fsdp"),
        P("section", "fsdp", None),
        P("section", "fsdp"),
        P("section", "fsdp"),
        P("section", "fsdp"),
        P("section", "fsdp", None),
        P("section", "fsdp"),
        P("section", None, "fsdp"),
        P("section", "fsdp"),
    )
    return jax.shard_map(on_device, mesh=mesh, in_specs=placed, out_specs=placed, check_vma=False)
```

time: 1340 us -> 709 us (0.53)
  matrix products: 444 us -> 0 us
  local copies, waits for them, and re-layouts: 243 us -> 16.6 us
  Pallas kernels: 417 us -> 607 us
  other arithmetic: 169 us -> 24.4 us
    dot_general x57 -> x0, matrix products: 444 us -> none  [the longest x3 48.6 us: layer_backward(): jnp.einsum('bsd,fd->bsf', grad_branch, weight_down, preferred_element_typ...]
    pallas_call x1 -> x13, Pallas kernels: 262 us -> 451 us  [the longest x1 222 us: reduce_grads(): pl.pallas_call(functools.partial(reduce_kernel, n, R, chunks), out_shape=...]
    reshape x34 -> x7, local copies, waits for them, and re-layouts: 84.3 us -> 1.88 us  [the longest x2 0.79 us: on_device(): vec = S[:, :8 * piece].reshape(n, 8, piece).transpose(1, 0, 2).reshape(8, D)]
    another operation x14 -> x6, other arithmetic: 64.3 us -> 2.96 us  [the longest x5 2.93 us: turn(): return jnp.stack([jnp.int32(micro), (here == where).astype(jnp.int32)])]
    reduce_sum x27 -> x1, other arithmetic: 47.5 us -> 1.29 us  [on_device(): stats = stats.sum(axis=1)]
    add x9 -> x0, local copies, waits for them, and re-layouts: 43.7 us -> none  [on_device(): left + right]
    convert_element_type x14 -> x2, other arithmetic: 39.7 us -> 6.47 us  [the longest x1 3.75 us: on_device(): F[0, :, :3 * D].astype(F32)[None]]
    squeeze x2, local copies, waits for them, and re-layouts: 28.8 us -> 0.15 us  [on_device(): qb = jnp.concatenate([vec[2], jnp.zeros_like(vec[2]), vec[3]])[None]]
  transfers between devices with their start and end apart: 4 -> 6, of which waited for: 2 -> 2; matrix products, arithmetic and copies ran while one was open for 12% -> 0% of each run, Pallas kernels for 0% -> 22%
where the time goes in v2:
time: 709 us; the launch traced here: 705 us
  Pallas kernels  607 us (86%)
  waiting for transfers between devices  48.5 us (7%)
  other arithmetic  24.4 us (3%)
  local copies, waits for them, and re-layouts  16.6 us (2%)
  starting transfers between devices  7.88 us (1%)
    pallas_call x1, Pallas kernels, reduce_grads(): pl.pallas_call(functools.partial(reduce_kernel, n, R, chunks), out_shape=...  222 us
    pallas_call x1, Pallas kernels, gather_weights(): pl.pallas_call(functools.partial(gather_kernel, n, R), out_shape=(jax.Sha...  155 us
    pallas_call x6, Pallas kernels, d_layer(): pl.pallas_call(kernel, out_shape=(shape(total, wide, HALF), shape(total,...  137 us
    pallas_call x6, Pallas kernels, f_layer(): pl.pallas_call(kernel, out_shape=(shape(total, D, HALF), shape(total, 3 *...  92.7 us
    ppermute x6, waiting for transfers between devices, shifted(): lax.ppermute(value, axis, [(source, source + steps) for source in range(f...  48.5 us
  transfers between devices with their start and end apart: 6, of which 2 were waited for; matrix products, arithmetic and copies ran while one was open for 0% of the time, Pallas kernels for 22%

profile of v2, /device:TPU:1, one launch (start us, length us, event | category | flops | bytes accessed | tf_op | source)
XLA Modules:
  0.0 705.4 jit_solution(3586699530077727412)
XLA Ops:
  6.5 2.0 pad.19.up
  9.7 155.0 %shard_map.228 = (bf16[3,1152,4608]{2,1,0:T(8,128)(2,1)}, bf16[4,16,256]{2,1,0:T(8,128)(2,1)S(1)}) custom-call(bf16[288,3456]{1,0:T(8,128)(2,1)S(1)} %bitcast.35, bf16[288,1152]{1,0:T(8,128)(2,1)S(1)} %bitcast.36, bf16[288,4608]{1,0:T(8,128)(2,1)S(1)} %pad.19.up, bf16[288,4608]{1,0:T(8,128)(2,1)S(1)} %pad.20.down, bf16[16,256]{1,0:T(8,128)(2,1)S(1)} %reshape.70.small), custom_call_target="tpu_custom_call" | custom-call | tf_op jit(solution)/shard_map/pallas_call | solution.py:543
  165.0 1.4 fusion.3
  169.2 26.7 %shard_map.229 = (bf16[960,1152]{1,0:T(8,128)(2,1)}, bf16[960,3456]{1,0:T(8,128)(2,1)}, bf16[6,16,160,160]{3,2,1,0:T(8,128)(2,1)}, bf16[960,1152]{1,0:T(8,128)(2...) custom-call(s32[2]{0:T(128)} %pad_add_fusion.5.slot, ...), custom_call_target="tpu_custom_call" | custom-call | flops 368640 | bytes 368640 | tf_op jit(solution)/shard_map/pallas_call | solution.py:244
  195.9 1.3 collective-permute-start.2
  197.9 26.8 %shard_map.230 = (bf16[960,1152]{1,0:T(8,128)(2,1)}, bf16[960,3456]{1,0:T(8,128)(2,1)}, bf16[6,16,160,160]{3,2,1,0:T(8,128)(2,1)}, bf16[960,1152]{1,0:T(8,128)(2...) custom-call(s32[2]{0:T(128)} %get-tuple-element.231.slot, ...), custom_call_target="tpu_custom_call", output_to_operand_aliasing={{0}: (6, {}), {1}: (7, {}), {2}: (8, {}), {3}: (9, {}), {4}... | custom-call | flops 368640 | bytes 368640 | tf_op jit(solution)/shard_map/pallas_call | solution.py:244
  224.6 1.3 collective-permute-start.1
  226.0 27.0 %shard_map.231 = (bf16[960,1152]{1,0:T(8,128)(2,1)}, bf16[960,3456]{1,0:T(8,128)(2,1)}, bf16[6,16,160,160]{3,2,1,0:T(8,128)(2,1)}, bf16[960,1152]{1,0:T(8,128)(2...) custom-call(s32[2]{0:T(128)} %get-tuple-element.230.slot, ...), custom_call_target="tpu_custom_call", output_to_operand_aliasing={{0}: (6, {}), {1}: (7, {}), {2}: (8, {}), {3}: (9, {}), {4}... | custom-call | flops 368640 | bytes 368640 | tf_op jit(solution)/shard_map/pallas_call | solution.py:244
  256.9 3.0 shard_map.232
  260.8 6.2 shard_map.233
  267.0 3.6 collective-permute-done.refs_0_.refs_1_
  271.4 3.1 shard_map.234
  274.5 10.1 %shard_map.235 = (bf16[960,4608]{1,0:T(8,128)(2,1)}, bf16[960,1152]{1,0:T(8,128)(2,1)}, bf16[960,3456]{1,0:T(8,128)(2,1)}, f32[960,1152]{1,0:T(8,128)}, bf16[320...) custom-call(s32[2]{0:T(128)} %pad_add_fusion.4.slot, ...), custom_call_target="tpu_custom_call", output_to_operand_aliasing={{3}: (9, {})} | custom-call | flops 368640 | bytes 368640 | tf_op jit(solution)/shard_map/pallas_call | solution.py:384
  286.0 9.6 %shard_map.236 = (bf16[960,4608]{1,0:T(8,128)(2,1)}, bf16[960,1152]{1,0:T(8,128)(2,1)}, bf16[960,3456]{1,0:T(8,128)(2,1)}, f32[960,1152]{1,0:T(8,128)}, bf16[320...) custom-call(s32[2]{0:T(128)} %pad_add_fusion.2.slot, ...), custom_call_target="tpu_custom_call", output_to_operand_aliasing={{0}: (9, {}), {1}: (10, {}), {2}: (11, {}), {3}: (12, {})} | custom-call | flops 368640 | bytes 368640 | tf_op jit(solution)/shard_map/pallas_call | solution.py:384
  296.9 9.8 %shard_map.237 = (bf16[960,4608]{1,0:T(8,128)(2,1)}, bf16[960,1152]{1,0:T(8,128)(2,1)}, bf16[960,3456]{1,0:T(8,128)(2,1)}, f32[960,1152]{1,0:T(8,128)}, bf16[320...) custom-call(s32[2]{0:T(128)} %pad_add_fusion.slot, ...), custom_call_target="tpu_custom_call", output_to_operand_aliasing={{0}: (9, {}), {1}: (10, {}), {2}: (11, {}), {3}: (12, {})} | custom-call | flops 368640 | bytes 368640 | tf_op jit(solution)/shard_map/pallas_call | solution.py:384
  308.0 45.0 %collective-permute-done.5.refs_0_ = bf16[320,1152]{1,0:T(8,128)(2,1)S(1)} collective-permute-done((bf16[320,1152]{1,0:T(8,128)(2,1)}, bf16[320,1152]{1,0:T(8,128)(2,1)S(1)}, u32[]{:S(2)}, u32[]{:S(2)}) %collective-permute-start.5) | collective-permute-done | bytes 737312 | tf_op jit(solution)/shard_map/ppermute | solution.py:990
  353.9 35.5 %shard_map.238 = (bf16[960,4608]{1,0:T(8,128)(2,1)}, bf16[960,1152]{1,0:T(8,128)(2,1)}, bf16[960,3456]{1,0:T(8,128)(2,1)}, f32[960,1152]{1,0:T(8,128)}, bf16[320...) custom-call(s32[2]{0:T(128)} %pad_add_fusion.5.slot, ...), custom_call_target="tpu_custom_call", output_to_operand_aliasing={{0}: (9, {}), {1}: (10, {}), {2}: (11, {}), {3}: (12, {})} | custom-call | flops 368640 | bytes 368640 | tf_op jit(solution)/shard_map/pallas_call | solution.py:384
  390.2 35.8 %shard_map.239 = (bf16[960,4608]{1,0:T(8,128)(2,1)}, bf16[960,1152]{1,0:T(8,128)(2,1)}, bf16[960,3456]{1,0:T(8,128)(2,1)}, f32[960,1152]{1,0:T(8,128)}, bf16[320...) custom-call(s32[2]{0:T(128)} %get-tuple-element.231.slot, ...), custom_call_target="tpu_custom_call", output_to_operand_aliasing={{0}: (9, {}), {1}: (10, {}), {2}: (11, {}), {3}: (12, {})} | custom-call | flops 368640 | bytes 368640 | tf_op jit(solution)/shard_map/pallas_call | solution.py:384
  427.0 36.0 %shard_map.240 = (bf16[960,4608]{1,0:T(8,128)(2,1)}, bf16[960,1152]{1,0:T(8,128)(2,1)}, bf16[960,3456]{1,0:T(8,128)(2,1)}, f32[960,1152]{1,0:T(8,128)}, bf16[320...) custom-call(s32[2]{0:T(128)} %get-tuple-element.230.slot, ...), custom_call_target="tpu_custom_call", output_to_operand_aliasing={{0}: (9, {}), {1}: (10, {}), {2}: (11, {}), {3}: (12, {})} | custom-call | flops 368640 | bytes 368640 | tf_op jit(solution)/shard_map/pallas_call | solution.py:384
  466.3 3.2 maximum_select_fusion.eb
  469.5 221.9 %shard_map.241 = (bf16[3,288,4608]{2,1,0:T(8,128)(2,1)}, f32[16,256]{1,0:T(8,128)}) custom-call(f32[4,16,256]{2,1,0:T(8,128)} %bitcast.49, bf16[960,1152]{1,0:T(8,128)(2,1)} %get-tuple-element.204.n1, bf16[960,1152]{1,0:T(8,128)(2,1)} %get-tuple-element.205.c, bf16[960,1152]{1,0:T(8,128)(2,1)} %get-tuple-element.206.n2, ...), custom_call_target="tpu_custom_call" | custom-call | tf_op jit(solution)/shard_map/pallas_call | solution.py:959
  693.3 2.7 slice_convert_fusion.2
  696.0 3.7 slice_convert_fusion.1
  699.8 4.7 convert_bitcast_fusion
  (102 shorter events, 28.4 us)
Async XLA Ops:
  6.5 2.5 copy-start.12
  6.5 3.1 copy-start
  6.5 3.2 copy-start.1
  9.1 155.9 %copy-start.2 = (bf16[1,6,160,1152]{3,2,1,0:T(8,128)(2,1)S(1)}, bf16[1,6,160,1152]{3,2,1,0:T(8,128)(2,1)}, u32[]{:S(2)}) copy-start(bf16[1,6,160,1152]{3,2,1,0:T(8,128)(2,1)} %param.13) | copy-start | bytes 6635524
  195.9 60.1 %collective-permute-start.2 = (bf16[320,1152]{1,0:T(8,128)(2,1)}, bf16[320,1152]{1,0:T(8,128)(2,1)S(1)}, u32[]{:S(2)}, u32[]{:S(2)}) collective-permute-start(bf16[320,1152]{1,0:T(8,128)(2,1)} %get-tuple-element.135), channel_id=1, source_target_pairs={{0,16},{1,17},{2,18},{3,19},{4,20},{5,21},{6,22},{7,23},{8,24},{9,... | collective-permute-start | bytes 2211848 | tf_op jit(solution)/shard_map/ppermute | solution.py:990
  224.6 35.3 %collective-permute-start.1 = (bf16[320,1152]{1,0:T(8,128)(2,1)}, bf16[320,1152]{1,0:T(8,128)(2,1)S(1)}, u32[]{:S(2)}, u32[]{:S(2)}) collective-permute-start(bf16[320,1152]{1,0:T(8,128)(2,1)} %get-tuple-element.134), channel_id=1, source_target_pairs={{0,16},{1,17},{2,18},{3,19},{4,20},{5,21},{6,22},{7,23},{8,24},{9,... | collective-permute-start | bytes 2211848 | tf_op jit(solution)/shard_map/ppermute | solution.py:990
  252.9 17.7 %collective-permute-start = (bf16[320,1152]{1,0:T(8,128)(2,1)}, bf16[320,1152]{1,0:T(8,128)(2,1)S(1)}, u32[]{:S(2)}, u32[]{:S(2)}) collective-permute-start(bf16[320,1152]{1,0:T(8,128)(2,1)} %get-tuple-element.133), channel_id=1, source_target_pairs={{0,16},{1,17},{2,18},{3,19},{4,20},{5,21},{6,22},{7,23},{8,24},{9,... | collective-permute-start | bytes 2211848 | tf_op jit(solution)/shard_map/ppermute | solution.py:990
  259.9 0.9 copy-start.6
  284.7 68.3 %collective-permute-start.5 = (bf16[320,1152]{1,0:T(8,128)(2,1)}, bf16[320,1152]{1,0:T(8,128)(2,1)S(1)}, u32[]{:S(2)}, u32[]{:S(2)}) collective-permute-start(bf16[320,1152]{1,0:T(8,128)(2,1)} %get-tuple-element.178), channel_id=1, source_target_pairs={{16,0},{17,1},{18,2},{19,3},{20,4},{21,5},{22,6},{23,7},{24,8},{25... | collective-permute-start | bytes 2211848 | tf_op jit(solution)/shard_map/ppermute | solution.py:990
  295.6 93.8 %collective-permute-start.4 = (bf16[320,1152]{1,0:T(8,128)(2,1)}, bf16[320,1152]{1,0:T(8,128)(2,1)S(1)}, u32[]{:S(2)}, u32[]{:S(2)}) collective-permute-start(bf16[320,1152]{1,0:T(8,128)(2,1)} %get-tuple-element.177), channel_id=1, source_target_pairs={{16,0},{17,1},{18,2},{19,3},{20,4},{21,5},{22,6},{23,7},{24,8},{25... | collective-permute-start | bytes 2211848 | tf_op jit(solution)/shard_map/ppermute | solution.py:990
  306.7 119.3 %collective-permute-start.3 = (bf16[320,1152]{1,0:T(8,128)(2,1)}, bf16[320,1152]{1,0:T(8,128)(2,1)S(1)}, u32[]{:S(2)}, u32[]{:S(2)}) collective-permute-start(bf16[320,1152]{1,0:T(8,128)(2,1)} %get-tuple-element.176), channel_id=1, source_target_pairs={{16,0},{17,1},{18,2},{19,3},{20,4},{21,5},{22,6},{23,7},{24,8},{25... | collective-permute-start | bytes 2211848 | tf_op jit(solution)/shard_map/ppermute | solution.py:990
  353.0 0.9 copy-start.8
  426.9 36.1 %copy-start.13 = (f32[8,8,1152]{2,1,0:T(8,128)S(1)}, f32[8,8,1152]{2,1,0:T(8,128)}, u32[]{:S(2)}) copy-start(f32[8,8,1152]{2,1,0:T(8,128)} %get-tuple-element.193) | copy-start | bytes 884740
  426.9 36.1 %copy-start.14 = (f32[8,8,1152]{2,1,0:T(8,128)S(1)}, f32[8,8,1152]{2,1,0:T(8,128)}, u32[]{:S(2)}) copy-start(f32[8,8,1152]{2,1,0:T(8,128)} %get-tuple-element.195) | copy-start | bytes 884740
  426.9 36.1 %copy-start.15 = (f32[8,8,1152]{2,1,0:T(8,128)S(1)}, f32[8,8,1152]{2,1,0:T(8,128)}, u32[]{:S(2)}) copy-start(f32[8,8,1152]{2,1,0:T(8,128)} %get-tuple-element.197) | copy-start | bytes 884740
  426.9 37.5 %copy-start.17 = (f32[1,4352]{1,0:T(1,128)S(1)}, f32[1,4352]{1,0:T(1,128)}, u32[]{:S(2)}) copy-start(f32[1,4352]{1,0:T(1,128)} %get-tuple-element.199) | copy-start | bytes 52228
  426.9 37.5 %copy-start.18 = (f32[1,4352]{1,0:T(1,128)S(1)}, f32[1,4352]{1,0:T(1,128)}, u32[]{:S(2)}) copy-start(f32[1,4352]{1,0:T(1,128)} %get-tuple-element.201) | copy-start | bytes 52228
  427.0 37.5 %copy-start.19 = (f32[1,4352]{1,0:T(1,128)S(1)}, f32[1,4352]{1,0:T(1,128)}, u32[]{:S(2)}) copy-start(f32[1,4352]{1,0:T(1,128)} %get-tuple-element.203) | copy-start | bytes 52228
  427.0 37.5 %copy-start.20 = (f32[1,4352]{1,0:T(1,128)S(1)}, f32[1,4352]{1,0:T(1,128)}, u32[]{:S(2)}) copy-start(f32[1,4352]{1,0:T(1,128)} %get-tuple-element.198) | copy-start | bytes 52228
  427.0 37.5 %copy-start.21 = (f32[1,4352]{1,0:T(1,128)S(1)}, f32[1,4352]{1,0:T(1,128)}, u32[]{:S(2)}) copy-start(f32[1,4352]{1,0:T(1,128)} %get-tuple-element.200) | copy-start | bytes 52228
  427.0 39.3 %copy-start.3 = (bf16[1,6,160,1152]{3,2,1,0:T(8,128)(2,1)S(1)}, bf16[1,6,160,1152]{3,2,1,0:T(8,128)(2,1)}, u32[]{:S(2)}) copy-start(bf16[1,6,160,1152]{3,2,1,0:T(8,128)(2,1)} %param.13) | copy-start | bytes 6635524
  427.0 39.3 %copy-start.9 = (bf16[320,1152]{1,0:T(8,128)(2,1)S(1)}, bf16[320,1152]{1,0:T(8,128)(2,1)}, u32[]{:S(2)}) copy-start(bf16[320,1152]{1,0:T(8,128)(2,1)} %copy-done.8) | copy-start | bytes 2211844
  692.1 7.6 %copy-start.4 = (bf16[3,288,4608]{2,1,0:T(8,128)(2,1)S(1)}, bf16[3,288,4608]{2,1,0:T(8,128)(2,1)}, u32[]{:S(2)}) copy-start(bf16[3,288,4608]{2,1,0:T(8,128)(2,1)} %get-tuple-element.212) | copy-start | bytes 23887876
  699.8 4.7 copy-start.16
  (4 other events, 3.5 us)

commit v3 on v2

--- a/solution.py
+++ b/solution.py
@@ -19,6 +19,7 @@
 NN = (((1,), (0,)), ((), ()))
 NT = (((1,), (1,)), ((), ()))
 TN = (((0,), (0,)), ((), ()))
+FOLD = 8
 
 
 def mul(left, right, dims=NN):
@@ -68,43 +69,48 @@
     lane = lax.broadcasted_iota(jnp.int32, (rows, hi - lo), 1) + lo
     return (lane >= a) & (lane < b)
 
+FOLD = 8
+
+
 def attn_image(qkv, P, c, D, tok, factor):
-    for h in range(HEADS):
-        a, b, lo, hi = spans(h)
-        mask = head_mask(h, tok)
-        q = jnp.where(mask, qkv[:, lo:hi], 0)
-        k = qkv[:, D + lo:D + hi]
-        v = qkv[:, 2 * D + lo:2 * D + hi]
-        s = mul(k, q, NT)
-        e = jnp.exp2((s - jnp.max(s, axis=0, keepdims=True)) * factor)
-        p = (e * (1.0 / jnp.sum(e, axis=0, keepdims=True))).astype(HALF)
-        P[h] = p
-        o = mul(p, v, TN).astype(HALF)
-        if a > lo:
-            c[:, lo:hi] = jnp.where(mask, o, c[:, lo:hi])
-        else:
-            c[:, lo:hi] = o
+    for first in range(0, HEADS, FOLD):
+        heads = range(first, first + FOLD)
+        held = []
+        for h in heads:
+            a, b, lo, hi = spans(h)
+            held.append(mul(qkv[:, D + lo:D + hi], jnp.where(head_mask(h, tok), qkv[:, lo:hi], 0), NT))
+        probs = []
+        for h, s in zip(heads, held):
+            e = jnp.exp2((s - jnp.max(s, axis=0, keepdims=True)) * factor)
+            p = (e * (1.0 / jnp.sum(e, axis=0, keepdims=True))).astype(HALF)
+            P[h] = p
+            probs.append(p)
+        for h, p in zip(heads, probs):
+            a, b, lo, hi = spans(h)
+            o = mul(p, qkv[:, 2 * D + lo:2 * D + hi], TN).astype(HALF)
+            c[:, lo:hi] = jnp.where(head_mask(h, tok), o, c[:, lo:hi]) if a > lo else o
+
 
 def attn_back_image(qkv, P, dc, out, D, tok, factor):
-    for h in range(HEADS):
-        a, b, lo, hi = spans(h)
-        mask = head_mask(h, tok)
-        q = qkv[:, lo:hi]
-        k = qkv[:, D + lo:D + hi]
-        v = qkv[:, 2 * D + lo:2 * D + hi]
-        d = dc[:, lo:hi]
-        p = P[h]
-        dv = mul(p, d).astype(HALF)
-        wide = p.astype(F32)
-        dp = mul(v, jnp.where(mask, d, 0), NT)
-        ds = (wide * (dp - jnp.sum(wide * dp, axis=0, keepdims=True))).astype(HALF)
-        dk = (mul(ds, q) * factor).astype(HALF)
-        dq = (mul(ds, k, TN) * factor).astype(HALF)
-        for base, value in ((0, dq), (D, dk), (2 * D, dv)):
-            if a > lo:
-                out[:, base + lo:base + hi] = jnp.where(mask, value, out[:, base + lo:base + hi])
-            else:
-                out[:, base + lo:base + hi] = value
+    for first in range(0, HEADS, FOLD):
+        heads = range(first, first + FOLD)
+        held = []
+        for h in heads:
+            a, b, lo, hi = spans(h)
+            held.append(mul(qkv[:, 2 * D + lo:2 * D + hi], jnp.where(head_mask(h, tok), dc[:, lo:hi], 0), NT))
+        grads = []
+        for h, dp in zip(heads, held):
+            wide = P[h].astype(F32)
+            grads.append((wide * (dp - jnp.sum(wide * dp, axis=0, keepdims=True)) * factor).astype(HALF))
+        for h, ds in zip(heads, grads):
+            a, b, lo, hi = spans(h)
+            mask = head_mask(h, tok)
+            dv = mul(P[h], dc[:, lo:hi]).astype(HALF)
+            dk = mul(ds, qkv[:, lo:hi]).astype(HALF)
+            dq = mul(ds, qkv[:, D + lo:D + hi], TN).astype(HALF)
+            for base, value in ((0, dq), (D, dk), (2 * D, dv)):
+                at = slice(base + lo, base + hi)
+                out[:, at] = jnp.where(mask, value, out[:, at]) if a > lo else value
 
 
 TILE = 512
@@ -125,7 +131,7 @@
         body(whole * step, width % step)
 
 
-def f_layer(slots, total, wide, x, vec, qb, ub, G, tok, kept):
+def f_layer(slots, total, wide, final, x, vec, qb, ub, G, tok, kept):
     T, D = x.shape
     hidden = ub.shape[1]
     images = T // tok
@@ -158,7 +164,9 @@
         def out(source, target, at, k):
             return pltpu.make_async_copy(source, target.at[at], osem.at[k])
         outs = [out(n1, n1o, save, 0), out(qkv, qkvo, save, 1), out(c, co, save, 2), out(r1, r1o, save, 3),
-                out(n2, n2o, save, 4), out(g, go, (save, pl.ds(0, hidden)), 5), out(res, reso, save, 6)]
+                out(n2, n2o, save, 4), out(g, go, (save, pl.ds(0, hidden)), 5)]
+        if final:
+            outs.append(out(res, reso, save, 6))
 
         def first(at):
             n1[at, :] = (normal(x[at, :].astype(F32))[0] * vec[0:1, :] + vec[1:2, :]).astype(HALF)
@@ -222,9 +230,11 @@
         for a, w in pieces(D, LANES):
             at = slice(a, a + w)
             value = mul(g[...], wa[a:a + w, 0:hidden], NT) + (r1[:, at] + vec[7:8, at])
-            res[:, at] = value
+            if final:
+                res[:, at] = value
             y[:, at] = value.astype(HALF)
-        outs[6].start()
+        if final:
+            outs[6].start()
         for copy in outs:
             copy.wait()
         for i in range(max(0, images - 2), images):
@@ -407,11 +417,14 @@
         bit //= 2
     return bits
 
-def gather_kernel(n, R, qkv, out, up, down, small, G, S, stage, stage_small, lsem, ssem, rsem, small_send, small_recv):
+def gather_kernel(n, R, halves, qkv, out, up, down, *refs):
+    (gain_one, shift_one, bias_qv, bias_out, gain_two, shift_two, bias_down, bias_up,
+     G, vec, qb, ub, stage, S, lsem, ssem, rsem, small_send, small_recv) = refs
     z = lax.axis_index("fsdp")
     r = lax.axis_index("replica")
     rows, wide = up.shape
     part = wide // R
+    some = rows // halves
     bits = powers(R)
     barrier = pltpu.get_barrier_semaphore()
     for hop in range(1, n):
@@ -425,42 +438,45 @@
         pltpu.make_async_copy(out, stage.at[0, :, pl.ds(first, out.shape[1])], lsem.at[1]),
         pltpu.make_async_copy(up, stage.at[1], lsem.at[2]),
         pltpu.make_async_copy(down, stage.at[2], lsem.at[3]),
-        pltpu.make_async_copy(small, stage_small, lsem.at[4]),
     ]
     for copy in local:
         copy.start()
-    keep = [pltpu.make_async_copy(stage.at[group], G.at[group, mine], lsem.at[5 + group]) for group in range(3)]
-    keep.append(pltpu.make_async_copy(stage_small, S.at[z], lsem.at[8]))
+    keep = [pltpu.make_async_copy(stage.at[group], G.at[group, mine], lsem.at[4 + group]) for group in range(3)]
+
+    for row, value in enumerate((gain_one, shift_one, None, None, bias_out, gain_two, shift_two, bias_down, bias_up)):
+        value = bias_qv[row - 2:row - 1, :] if value is None else value[...]
+        S[z, row:row + 1, 0:value.shape[1]] = value.astype(F32)
     pl.semaphore_wait(barrier, n - 1 + len(bits))
 
-    def piece(group, source, column):
-        return G.at[group, pl.ds(pl.multiple_of(source * rows, 16), rows),
+    def piece(unit, source, column):
+        group, half = unit // halves, unit % halves
+        return G.at[group, pl.ds(pl.multiple_of(source * rows + half * some, 16), some),
                     pl.ds(pl.multiple_of(column * part, 128), part)]
 
-    def send(group, source, column, kind, target, origin=None):
+    def send(unit, source, column, kind, target, origin=None):
         return pltpu.make_async_remote_copy(
-            src_ref=piece(group, source, column) if origin is None else origin, dst_ref=piece(group, source, column),
-            send_sem=ssem.at[group, source, column, kind], recv_sem=rsem.at[group, source, column],
+            src_ref=piece(unit, source, column) if origin is None else origin, dst_ref=piece(unit, source, column),
+            send_sem=ssem.at[unit, source, column, kind], recv_sem=rsem.at[unit, source, column],
             device_id=target, device_id_type=MESH)
 
-    def to_right(group, source, origin=None):
-        return send(group, source, r, 0, {"fsdp": z + 1}, origin)
-
-    def to_left(group, source, origin=None):
-        return send(group, source, r, 1, {"fsdp": z - 1}, origin)
-
-    def own(group):
-        return stage.at[group, :, pl.ds(pl.multiple_of(r * part, 128), part)]
-
-    def share(group, source, column, level):
-        return send(group, source, column, 2 + level, {"replica": r ^ bits[level]})
-
-    def arrived(group, source, column):
-        send(group, source, column, 0, {"replica": r ^ bits[0]}).wait_recv()
+    def to_right(unit, source, origin=None):
+        return send(unit, source, r, 0, {"fsdp": z + 1}, origin)
+
+    def to_left(unit, source, origin=None):
+        return send(unit, source, r, 1, {"fsdp": z - 1}, origin)
+
+    def own(unit):
+        return stage.at[unit // halves, pl.ds(unit % halves * some, some), pl.ds(pl.multiple_of(r * part, 128), part)]
+
+    def share(unit, source, column, level):
+        return send(unit, source, column, 2 + level, {"replica": r ^ bits[level]})
+
+    def arrived(unit, source, column):
+        send(unit, source, column, 0, {"replica": r ^ bits[0]}).wait_recv()
 
     def small_to(hop):
         return pltpu.make_async_remote_copy(
-            src_ref=small, dst_ref=S.at[z], send_sem=small_send.at[hop],
+            src_ref=S.at[z], dst_ref=S.at[z], send_sem=small_send.at[hop],
             recv_sem=small_recv.at[z], device_id={"fsdp": lax.rem(z + hop, n)}, device_id_type=MESH)
     for hop in range(1, n):
         small_to(hop).start()
@@ -470,96 +486,113 @@
             local[1].wait()
         else:
             local[1 + group].wait()
-        @pl.when(z + 1 < n)
-        def _():
-            to_right(group, z, own(group)).start()
-        @pl.when(z > 0)
-        def _():
-            to_left(group, z, own(group)).start()
+        for unit in range(group * halves, (group + 1) * halves):
+            @pl.when(z + 1 < n)
+            def _():
+                to_right(unit, z, own(unit)).start()
+            @pl.when(z > 0)
+            def _():
+                to_left(unit, z, own(unit)).start()
         keep[group].start()
-    local[4].wait()
-    keep[3].start()
     columns = {}
     for level, bit in enumerate(bits):
         masks = [0]
         for upper in bits[:level]:
             masks = masks + [m | upper for m in masks]
         columns[level] = [bit | m for m in masks]
-    steps = [(hop, group) for hop in range(1, n) for group in range(3)]
+    units = 3 * halves
+    steps = [(hop, unit) for hop in range(1, n) for unit in range(units)]
     for turn in range(len(steps) + len(bits)):
         for level in range(-1, len(bits)):
             place = turn - 1 - level
             if place < 0 or place >= len(steps):
                 continue
-            hop, group = steps[place]
+            hop, unit = steps[place]
             for sign in (-1, 1):
                 source = z + sign * hop
                 @pl.when((source >= 0) & (source < n))
                 def _():
                     if level < 0:
-                        arrived(group, source, r)
+                        arrived(unit, source, r)
                         for lower in range(len(bits)):
-                            share(group, source, r, lower).start()
+                            share(unit, source, r, lower).start()
                         if sign < 0:
                             @pl.when(z + 1 < n)
                             def _():
-                                to_right(group, source).start()
+                                to_right(unit, source).start()
                         else:
                             @pl.when(z > 0)
                             def _():
-                                to_left(group, source).start()
+                                to_left(unit, source).start()
                     else:
                         for mask in columns[level]:
-                            arrived(group, source, r ^ mask)
+                            arrived(unit, source, r ^ mask)
                             for lower in range(level + 1, len(bits)):
-                                share(group, source, r ^ mask, lower).start()
+                                share(unit, source, r ^ mask, lower).start()
     for copy in keep:
         copy.wait()
     for hop in range(1, n):
+        source = lax.rem(z + hop, n)
         pltpu.make_async_remote_copy(
-            src_ref=small, dst_ref=S.at[lax.rem(z + hop, n)], send_sem=small_send.at[hop],
-            recv_sem=small_recv.at[lax.rem(z + hop, n)], device_id={"fsdp": lax.rem(z + hop, n)}, device_id_type=MESH).wait_recv()
+            src_ref=S.at[source], dst_ref=S.at[source], send_sem=small_send.at[hop],
+            recv_sem=small_recv.at[source], device_id={"fsdp": source}, device_id_type=MESH).wait_recv()
         small_to(hop).wait_send()
-    for group in range(3):
+    D = vec.shape[1]
+    few = bias_up.shape[1]
+    ub[...] = jnp.zeros_like(ub)
+    for source in range(n):
+        vec[:, source * rows:(source + 1) * rows] = S[source, 0:8, 0:rows]
+        ub[:, source * few:(source + 1) * few] = S[source, 8:9, 0:few]
+    qb[:, 0:D] = vec[2:3, :]
+    qb[:, D:2 * D] = jnp.zeros((1, D), F32)
+    qb[:, 2 * D:3 * D] = vec[3:4, :]
+    for unit in range(units):
         for source in range(n):
             @pl.when((source <= z) & (z + 1 < n))
             def _():
-                to_right(group, source).wait_send()
+                to_right(unit, source).wait_send()
             @pl.when((source >= z) & (z > 0))
             def _():
-                to_left(group, source).wait_send()
+                to_left(unit, source).wait_send()
             @pl.when(source != z)
             def _():
                 for level in range(len(bits)):
-                    share(group, source, r, level).wait_send()
+                    share(unit, source, r, level).wait_send()
                 for level in range(len(bits)):
                     for mask in columns[level]:
                         for lower in range(level + 1, len(bits)):
-                            share(group, source, r ^ mask, lower).wait_send()
-
-def gather_weights(n, R, qkv, out, up, down, small):
+                            share(unit, source, r ^ mask, lower).wait_send()
+
+
+def gather_weights(n, R, filled, qkv, out, up, down, vectors):
     rows, wide = up.shape
     kinds = 2 + len(powers(R))
+    halves = 2 if rows % 32 == 0 else 1
+    lanes = -(-max(v.shape[1] for v in vectors) // 128) * 128
+    dma = pltpu.SemaphoreType.DMA
+    whole = pl.BlockSpec(memory_space=pltpu.VMEM)
+    D = n * rows
     return pl.pallas_call(
-        functools.partial(gather_kernel, n, R),
-        out_shape=(jax.ShapeDtypeStruct((3, n * rows, wide), qkv.dtype),
-                   jax.ShapeDtypeStruct((n,) + small.shape, small.dtype)),
-        in_specs=[pl.BlockSpec(memory_space=pl.ANY)] * 5,
-        out_specs=(pl.BlockSpec(memory_space=pl.ANY),) * 2,
+        functools.partial(gather_kernel, n, R, halves),
+        out_shape=(jax.ShapeDtypeStruct((3, D, wide), qkv.dtype), shape(8, D, F32), shape(1, 3 * D, F32),
+                   shape(1, filled, F32)),
+        in_specs=[ANY] * 4 + [whole] * len(vectors),
+        out_specs=(ANY,) + (whole,) * 3,
         scratch_shapes=[
             pltpu.VMEM((3, rows, wide), qkv.dtype),
-            pltpu.VMEM(small.shape, small.dtype),
-            pltpu.SemaphoreType.DMA((9,)),
-            pltpu.SemaphoreType.DMA((3, n, R, kinds)),
-            pltpu.SemaphoreType.DMA((3, n, R)),
-            pltpu.SemaphoreType.DMA((n,)),
-            pltpu.SemaphoreType.DMA((n,)),
+            pltpu.VMEM((n, 16, lanes), F32),
+            dma((7,)),
+            dma((3 * halves, n, R, kinds)),
+            dma((3 * halves, n, R)),
+            dma((n,)),
+            dma((n,)),
         ],
         compiler_params=pltpu.CompilerParams(collective_id=0, has_side_effects=True, vmem_limit_bytes=32 * 1024 * 1024),
-    )(qkv, out, up, down, small)
+    )(qkv, out, up, down, *vectors)
 
 
 ORDER = (2, 1, 0)
+SCRATCH = 26
 
 
 def plan(R, part, D):
@@ -599,7 +632,9 @@
     return every, kind, counts
 
 
-def reduce_kernel(n, R, chunks, small_in, n1, c, n2, eb, dqkv, low, du, g, F, small_out, *scratch):
+def reduce_kernel(n, R, chunks, small_in, n1, c, n2, rows_in, dqkv, low, du, g, *refs):
+    back = refs[:-2 - SCRATCH - (R.bit_length() - 1)]
+    F, small_out, *scratch = refs[len(back):]
     L = R.bit_length() - 1
     bits = [1 << level for level in range(L)]
     held = scratch[:L]
@@ -656,10 +691,26 @@
                 fetch(k, p).start()
 
     def fetch_left(which):
-        return pltpu.make_async_copy((eb, n2, n1, c)[which], stage, lsem)
+        return pltpu.make_async_copy((rows_in, n2, n1, c)[which], stage, lsem.at[0])
+
+    def fetch_back(m):
+        some = tokens // len(back)
+        return pltpu.make_async_copy(back[m], stage.at[pl.ds(m * some, some), :], lsem.at[m])
+
+    def first_left(act):
+        @pl.when(lax.axis_index("section") == 0)
+        def _():
+            for m in range(len(back)):
+                act(fetch_back(m))
+        @pl.when(lax.axis_index("section") != 0)
+        def _():
+            act(fetch_left(0))
 
     def turn_left(which):
-        fetch_left(which).wait()
+        if which == 0:
+            first_left(lambda copy: copy.wait())
+        else:
+            fetch_left(which).wait()
         for a in range(0, D, 128):
             left[which % 2, a:a + 128, :] = stage[:, a:a + 128].T
         if which < 3:
@@ -858,7 +909,7 @@
             src_ref=small_sum, dst_ref=small_r.at[r], send_sem=ss_r.at[p], recv_sem=sr_r.at[r],
             device_id={"replica": p}, device_id_type=MESH)
 
-    fetch_left(0).start()
+    first_left(lambda copy: copy.start())
     fetch_all(0)
     pl.semaphore_wait(barrier, n - 1 + R - 1)
     own_small = pltpu.make_async_copy(small_in.at[z], small_z.at[z], ss_l)
@@ -945,7 +996,7 @@
                     share(k, r ^ mask, lower).wait_send()
 
 
-def reduce_grads(n, R, wide, small, n1, c, n2, eb, dqkv, low, du, g):
+def reduce_grads(n, R, wide, small, n1, c, n2, rows_in, dqkv, low, du, g, back):
     tokens, D = n1.shape
     rows = D // n
     part = wide // R
@@ -960,7 +1011,7 @@
         functools.partial(reduce_kernel, n, R, chunks),
         out_shape=(jax.ShapeDtypeStruct((3, rows, wide), HALF),
                    jax.ShapeDtypeStruct(small.shape[1:], small.dtype)),
-        in_specs=[pl.BlockSpec(memory_space=pltpu.VMEM)] + [ANY] * 8,
+        in_specs=[pl.BlockSpec(memory_space=pltpu.VMEM)] + [ANY] * (8 + len(back)),
         out_specs=(ANY, pl.BlockSpec(memory_space=pltpu.VMEM)),
         scratch_shapes=[pltpu.VMEM((R >> (level + 1), D, one if level == L - 1 else both), HALF) for level in range(L)] + [
             pltpu.VMEM((2, D, R * most), HALF),
@@ -973,7 +1024,7 @@
             pltpu.VMEM((n,) + small.shape[1:], small.dtype),
             pltpu.VMEM((R,) + small.shape[1:], small.dtype),
             pltpu.VMEM(small.shape[1:], small.dtype),
-            dma((R,)), dma(()),
+            dma((R,)), dma((len(back),)),
             dma((L, K, R // 2)), dma((L, K, R // 2)),
             dma((K, 2, n, 2)), dma((K, 2, n, 2)),
             dma((K,)), dma((K,)),
@@ -981,7 +1032,7 @@
             dma((n,)), dma((n,)), dma((R,)), dma((R,)), dma(()),
         ],
         compiler_params=pltpu.CompilerParams(collective_id=1, has_side_effects=True, vmem_limit_bytes=62 * 1024 * 1024),
-    )(small, n1, c, n2, eb, dqkv, low, du, g)
+    )(small, n1, c, n2, rows_in, dqkv, low, du, g, *back)
 
 
 def shifted(value, axis, steps):
@@ -1006,16 +1057,9 @@
     filled = -(-hidden // LANES) * LANES
     wide = max(-(-4 * D // unit), -(-filled // unit)) * unit
 
-    vector = jnp.concatenate([first_gain[0], first_shift[0], qv_bias[0, 0], qv_bias[0, 1], out_bias[0], second_gain[0],
-                              second_shift[0], down_bias[0], up_bias[0]])
-    lanes = -(-vector.shape[0] // (16 * 128)) * 128
-    small = jnp.pad(vector, (0, 16 * lanes - vector.shape[0])).reshape(16, lanes)
-    G, S = gather_weights(n, R, qkv_weight[0], out_weight[0], pad_columns(up_weight[0], wide),
-                          pad_columns(down_weight[0].T, wide), small)
-    S = S.reshape(n, -1).astype(F32)
-    vec = S[:, : 8 * piece].reshape(n, 8, piece).transpose(1, 0, 2).reshape(8, D)
-    ub = pad_columns(S[:, 8 * piece : 8 * piece + hidden // n].reshape(1, hidden), filled)
-    qb = jnp.concatenate([vec[2], jnp.zeros_like(vec[2]), vec[3]])[None]
+    G, vec, qb, ub = gather_weights(
+        n, R, filled, qkv_weight[0], out_weight[0], pad_columns(up_weight[0], wide), pad_columns(down_weight[0].T, wide),
+        (first_gain, first_shift, qv_bias[0], out_bias, second_gain, second_shift, down_bias, up_bias))
 
     rows = ends[0].reshape(images * tok, D)
     T = images // MICRO * tok
@@ -1029,10 +1073,10 @@
     kept = (None,) * 9
     sent = []
     for micro in range(MICRO):
-        *kept, y = f_layer(turn(micro, 0), total, wide, parts[micro], vec, qb, ub, G, tok, kept)
+        *kept, y = f_layer(turn(micro, 0), total, wide, False, parts[micro], vec, qb, ub, G, tok, kept)
         sent.append(shifted(y, "section", 1))
     for micro in range(MICRO):
-        *kept, y = f_layer(turn(micro, 1), total, wide, sent[micro], vec, qb, ub, G, tok, kept)
+        *kept, y = f_layer(turn(micro, 1), total, wide, True, sent[micro], vec, qb, ub, G, tok, kept)
     n1, qkv, probs, c, r1, n2, g, gp, result = kept
 
     kept = (None, None, None, result)
@@ -1049,7 +1093,6 @@
     du, low, dqkv, result = kept
     stats = sum(jnp.where(at_first, below, above) for above, below in zip(stats[:MICRO], stats[MICRO:]))
     sums = sum(jnp.where(at_first, below, above) for above, below in zip(sums[:MICRO], sums[MICRO:]))
-    eb = jnp.where(at_first, jnp.concatenate(back), rows)
 
     stats = stats.sum(axis=1)
     vectors = jnp.stack([stats[4], stats[5], stats[6], stats[7], stats[2], stats[0], stats[1], stats[3]])
@@ -1057,7 +1100,7 @@
     vectors = jnp.concatenate([vectors, sums[0, :hidden].reshape(n, hidden // n)], axis=1)
     lanes = -(-vectors.shape[1] // (16 * 128)) * 128
     small = jnp.pad(vectors, ((0, 0), (0, 16 * lanes - vectors.shape[1]))).reshape(n, 16, lanes)
-    F, s = reduce_grads(n, R, wide, small, n1, c, n2, eb, dqkv, low, du, g)
+    F, s = reduce_grads(n, R, wide, small, n1, c, n2, rows, dqkv, low, du, g, back)
     s = s.reshape(-1)
     v = s[: 8 * piece].reshape(8, piece)
     return (

time: 709 us -> 678 us (0.956)
  Pallas kernels: 607 us -> 587 us
  other arithmetic: 24.4 us -> 16.1 us
    pallas_call x6, Pallas kernels: 137 us -> 118 us  [d_layer(): pl.pallas_call(kernel, out_shape=(shape(total, wide, HALF), shape(total,...]
  transfers between devices with their start and end apart: 6 -> 6, of which waited for: 2 -> 2; matrix products, arithmetic and copies ran while one was open for 0% -> 0% of each run, Pallas kernels for 22% -> 20%
where the time goes in v3:
time: 678 us; the launch traced here: 674 us
  Pallas kernels  587 us (87%)
  waiting for transfers between devices  46.3 us (7%)
  other arithmetic  16.1 us (2%)
  local copies, waits for them, and re-layouts  14.9 us (2%)
  starting transfers between devices  7.88 us (1%)
    pallas_call x1, Pallas kernels, reduce_grads(): pl.pallas_call(functools.partial(reduce_kernel, n, R, chunks), out_shape=...  223 us
    pallas_call x1, Pallas kernels, gather_weights(): pl.pallas_call(functools.partial(gather_kernel, n, R, halves), out_shape=...  158 us
    pallas_call x6, Pallas kernels, d_layer(): pl.pallas_call(kernel, out_shape=(shape(total, wide, HALF), shape(total,...  118 us
    pallas_call x6, Pallas kernels, f_layer(): pl.pallas_call(kernel, out_shape=(shape(total, D, HALF), shape(total, 3 *...  89.5 us
    ppermute x6, waiting for transfers between devices, shifted(): lax.ppermute(value, axis, [(source, source + steps) for source in range(f...  46.3 us
  transfers between devices with their start and end apart: 6, of which 2 were waited for; matrix products, arithmetic and copies ran while one was open for 0% of the time, Pallas kernels for 20%

profile of v3, /device:TPU:1, one launch (start us, length us, event | category | flops | bytes accessed | tf_op | source)
XLA Modules:
  0.0 674.0 jit_solution(9277551861809788640)
XLA Ops:
  0.7 3.1 fusion.3
  5.7 157.6 %shard_map.228 = (bf16[3,1152,4608]{2,1,0:T(8,128)(2,1)}, f32[8,1152]{1,0:T(8,128)S(1)}, f32[1,3456]{1,0:T(1,128)S(1)}, f32[1,4352]{1,0:T(1,128)S(1)}) custom-call(bf16[288,3456]{1,0:T(8,128)(2,1)S(1)} %bitcast.31, bf16[288,1152]{1,0:T(8,128)(2,1)S(1)} %bitcast.32, bf16[288,4608]{1,0:T(8,128)(2,1)S(1)} %pad.11.up, bf16[288,4608]{1,0:T(8,128)(2,1)S(1)} %pad.12.down, ...), custom_call_target="tpu_custom_call" | custom-call | tf_op jit(solution)/shard_map/pallas_call | solution.py:575
  165.2 25.9 %shard_map.229 = (bf16[960,1152]{1,0:T(8,128)(2,1)}, bf16[960,3456]{1,0:T(8,128)(2,1)}, bf16[6,16,160,160]{3,2,1,0:T(8,128)(2,1)}, bf16[960,1152]{1,0:T(8,128)(2...) custom-call(s32[2]{0:T(128)} %pad_add_fusion.5.slot, ...), custom_call_target="tpu_custom_call" | custom-call | flops 368640 | bytes 368640 | tf_op jit(solution)/shard_map/pallas_call | solution.py:254
  191.0 1.3 collective-permute-start.2
  193.0 25.5 %shard_map.230 = (bf16[960,1152]{1,0:T(8,128)(2,1)}, bf16[960,3456]{1,0:T(8,128)(2,1)}, bf16[6,16,160,160]{3,2,1,0:T(8,128)(2,1)}, bf16[960,1152]{1,0:T(8,128)(2...) custom-call(s32[2]{0:T(128)} %get-tuple-element.231.slot, ...), custom_call_target="tpu_custom_call", output_to_operand_aliasing={{0}: (6, {}), {1}: (7, {}), {2}: (8, {}), {3}: (9, {}), {4}... | custom-call | flops 368640 | bytes 368640 | tf_op jit(solution)/shard_map/pallas_call | solution.py:254
  218.5 1.3 collective-permute-start.1
  219.9 25.6 %shard_map.231 = (bf16[960,1152]{1,0:T(8,128)(2,1)}, bf16[960,3456]{1,0:T(8,128)(2,1)}, bf16[6,16,160,160]{3,2,1,0:T(8,128)(2,1)}, bf16[960,1152]{1,0:T(8,128)(2...) custom-call(s32[2]{0:T(128)} %get-tuple-element.230.slot, ...), custom_call_target="tpu_custom_call", output_to_operand_aliasing={{0}: (6, {}), {1}: (7, {}), {2}: (8, {}), {3}: (9, {}), {4}... | custom-call | flops 368640 | bytes 368640 | tf_op jit(solution)/shard_map/pallas_call | solution.py:254
  245.5 1.3 collective-permute-start
  249.5 3.2 shard_map.232
  253.6 6.2 shard_map.233
  259.8 3.5 collective-permute-done.refs_0_.refs_1_
  264.1 3.1 shard_map.234
  267.2 10.1 %shard_map.235 = (bf16[960,4608]{1,0:T(8,128)(2,1)}, bf16[960,1152]{1,0:T(8,128)(2,1)}, bf16[960,3456]{1,0:T(8,128)(2,1)}, f32[960,1152]{1,0:T(8,128)}, bf16[320...) custom-call(s32[2]{0:T(128)} %pad_add_fusion.4.slot, ...), custom_call_target="tpu_custom_call", output_to_operand_aliasing={{3}: (9, {})} | custom-call | flops 368640 | bytes 368640 | tf_op jit(solution)/shard_map/pallas_call | solution.py:394
  277.3 1.3 collective-permute-start.5
  278.6 8.4 %shard_map.236 = (bf16[960,4608]{1,0:T(8,128)(2,1)}, bf16[960,1152]{1,0:T(8,128)(2,1)}, bf16[960,3456]{1,0:T(8,128)(2,1)}, f32[960,1152]{1,0:T(8,128)}, bf16[320...) custom-call(s32[2]{0:T(128)} %pad_add_fusion.2.slot, ...), custom_call_target="tpu_custom_call", output_to_operand_aliasing={{0}: (9, {}), {1}: (10, {}), {2}: (11, {}), {3}: (12, {})} | custom-call | flops 368640 | bytes 368640 | tf_op jit(solution)/shard_map/pallas_call | solution.py:394
  288.4 8.4 %shard_map.237 = (bf16[960,4608]{1,0:T(8,128)(2,1)}, bf16[960,1152]{1,0:T(8,128)(2,1)}, bf16[960,3456]{1,0:T(8,128)(2,1)}, f32[960,1152]{1,0:T(8,128)}, bf16[320...) custom-call(s32[2]{0:T(128)} %pad_add_fusion.slot, ...), custom_call_target="tpu_custom_call", output_to_operand_aliasing={{0}: (9, {}), {1}: (10, {}), {2}: (11, {}), {3}: (12, {})} | custom-call | flops 368640 | bytes 368640 | tf_op jit(solution)/shard_map/pallas_call | solution.py:394
  298.1 42.8 %collective-permute-done.5.refs_0_ = bf16[320,1152]{1,0:T(8,128)(2,1)S(1)} collective-permute-done((bf16[320,1152]{1,0:T(8,128)(2,1)}, bf16[320,1152]{1,0:T(8,128)(2,1)S(1)}, u32[]{:S(2)}, u32[]{:S(2)}) %collective-permute-start.5) | collective-permute-done | bytes 737312 | tf_op jit(solution)/shard_map/ppermute | solution.py:1041
  341.8 30.3 %shard_map.238 = (bf16[960,4608]{1,0:T(8,128)(2,1)}, bf16[960,1152]{1,0:T(8,128)(2,1)}, bf16[960,3456]{1,0:T(8,128)(2,1)}, f32[960,1152]{1,0:T(8,128)}, bf16[320...) custom-call(s32[2]{0:T(128)} %pad_add_fusion.5.slot, ...), custom_call_target="tpu_custom_call", output_to_operand_aliasing={{0}: (9, {}), {1}: (10, {}), {2}: (11, {}), {3}: (12, {})} | custom-call | flops 368640 | bytes 368640 | tf_op jit(solution)/shard_map/pallas_call | solution.py:394
  373.0 30.1 %shard_map.239 = (bf16[960,4608]{1,0:T(8,128)(2,1)}, bf16[960,1152]{1,0:T(8,128)(2,1)}, bf16[960,3456]{1,0:T(8,128)(2,1)}, f32[960,1152]{1,0:T(8,128)}, bf16[320...) custom-call(s32[2]{0:T(128)} %get-tuple-element.231.slot, ...), custom_call_target="tpu_custom_call", output_to_operand_aliasing={{0}: (9, {}), {1}: (10, {}), {2}: (11, {}), {3}: (12, {})} | custom-call | flops 368640 | bytes 368640 | tf_op jit(solution)/shard_map/pallas_call | solution.py:394
  404.0 30.4 %shard_map.240 = (bf16[960,4608]{1,0:T(8,128)(2,1)}, bf16[960,1152]{1,0:T(8,128)(2,1)}, bf16[960,3456]{1,0:T(8,128)(2,1)}, f32[960,1152]{1,0:T(8,128)}, bf16[320...) custom-call(s32[2]{0:T(128)} %get-tuple-element.230.slot, ...), custom_call_target="tpu_custom_call", output_to_operand_aliasing={{0}: (9, {}), {1}: (10, {}), {2}: (11, {}), {3}: (12, {})} | custom-call | flops 368640 | bytes 368640 | tf_op jit(solution)/shard_map/pallas_call | solution.py:394
  437.5 222.6 %shard_map.241 = (bf16[3,288,4608]{2,1,0:T(8,128)(2,1)}, f32[16,256]{1,0:T(8,128)}) custom-call(f32[4,16,256]{2,1,0:T(8,128)} %bitcast.47, bf16[960,1152]{1,0:T(8,128)(2,1)} %get-tuple-element.208.n1, bf16[960,1152]{1,0:T(8,128)(2,1)} %get-tuple-element.209.c, bf16[960,1152]{1,0:T(8,128)(2,1)} %get-tuple-element.210.n2, bf16[960,1152]{1,0:T(8,128)(2,1)} %bitcast.44, ...), custom_call_target="tpu_custom_call" | custom-call | tf_op jit(solution)/shard_map/pallas_call | solution.py:1010
  662.0 2.7 slice_convert_fusion.2
  664.7 3.7 slice_convert_fusion.1
  668.5 4.7 convert_bitcast_fusion
  (97 shorter events, 19.3 us)
Async XLA Ops:
  0.6 3.2 copy-start.20
  0.7 3.9 copy-start.21
  3.8 1.9 copy-start.2
  3.8 1.9 copy-start.5
  3.8 1.9 copy-start.6
  3.8 1.9 copy-start.7
  191.0 57.5 %collective-permute-start.2 = (bf16[320,1152]{1,0:T(8,128)(2,1)}, bf16[320,1152]{1,0:T(8,128)(2,1)S(1)}, u32[]{:S(2)}, u32[]{:S(2)}) collective-permute-start(bf16[320,1152]{1,0:T(8,128)(2,1)} %get-tuple-element.139), channel_id=1, source_target_pairs={{0,16},{1,17},{2,18},{3,19},{4,20},{5,21},{6,22},{7,23},{8,24},{9,... | collective-permute-start | bytes 2211848 | tf_op jit(solution)/shard_map/ppermute | solution.py:1041
  218.5 34.2 %collective-permute-start.1 = (bf16[320,1152]{1,0:T(8,128)(2,1)}, bf16[320,1152]{1,0:T(8,128)(2,1)S(1)}, u32[]{:S(2)}, u32[]{:S(2)}) collective-permute-start(bf16[320,1152]{1,0:T(8,128)(2,1)} %get-tuple-element.138), channel_id=1, source_target_pairs={{0,16},{1,17},{2,18},{3,19},{4,20},{5,21},{6,22},{7,23},{8,24},{9,... | collective-permute-start | bytes 2211848 | tf_op jit(solution)/shard_map/ppermute | solution.py:1041
  245.5 17.8 %collective-permute-start = (bf16[320,1152]{1,0:T(8,128)(2,1)}, bf16[320,1152]{1,0:T(8,128)(2,1)S(1)}, u32[]{:S(2)}, u32[]{:S(2)}) collective-permute-start(bf16[320,1152]{1,0:T(8,128)(2,1)} %get-tuple-element.137), channel_id=1, source_target_pairs={{0,16},{1,17},{2,18},{3,19},{4,20},{5,21},{6,22},{7,23},{8,24},{9,... | collective-permute-start | bytes 2211848 | tf_op jit(solution)/shard_map/ppermute | solution.py:1041
  277.3 63.6 %collective-permute-start.5 = (bf16[320,1152]{1,0:T(8,128)(2,1)}, bf16[320,1152]{1,0:T(8,128)(2,1)S(1)}, u32[]{:S(2)}, u32[]{:S(2)}) collective-permute-start(bf16[320,1152]{1,0:T(8,128)(2,1)} %get-tuple-element.182), channel_id=1, source_target_pairs={{16,0},{17,1},{18,2},{19,3},{20,4},{21,5},{22,6},{23,7},{24,8},{25... | collective-permute-start | bytes 2211848 | tf_op jit(solution)/shard_map/ppermute | solution.py:1041
  287.1 85.0 %collective-permute-start.4 = (bf16[320,1152]{1,0:T(8,128)(2,1)}, bf16[320,1152]{1,0:T(8,128)(2,1)S(1)}, u32[]{:S(2)}, u32[]{:S(2)}) collective-permute-start(bf16[320,1152]{1,0:T(8,128)(2,1)} %get-tuple-element.181), channel_id=1, source_target_pairs={{16,0},{17,1},{18,2},{19,3},{20,4},{21,5},{22,6},{23,7},{24,8},{25... | collective-permute-start | bytes 2211848 | tf_op jit(solution)/shard_map/ppermute | solution.py:1041
  296.8 106.2 %collective-permute-start.3 = (bf16[320,1152]{1,0:T(8,128)(2,1)}, bf16[320,1152]{1,0:T(8,128)(2,1)S(1)}, u32[]{:S(2)}, u32[]{:S(2)}) collective-permute-start(bf16[320,1152]{1,0:T(8,128)(2,1)} %get-tuple-element.180), channel_id=1, source_target_pairs={{16,0},{17,1},{18,2},{19,3},{20,4},{21,5},{22,6},{23,7},{24,8},{25... | collective-permute-start | bytes 2211848 | tf_op jit(solution)/shard_map/ppermute | solution.py:1041
  403.9 30.5 %copy-start.22 = (f32[8,8,1152]{2,1,0:T(8,128)S(1)}, f32[8,8,1152]{2,1,0:T(8,128)}, u32[]{:S(2)}) copy-start(f32[8,8,1152]{2,1,0:T(8,128)} %get-tuple-element.197) | copy-start | bytes 884740
  403.9 30.5 %copy-start.23 = (f32[8,8,1152]{2,1,0:T(8,128)S(1)}, f32[8,8,1152]{2,1,0:T(8,128)}, u32[]{:S(2)}) copy-start(f32[8,8,1152]{2,1,0:T(8,128)} %get-tuple-element.199) | copy-start | bytes 884740
  403.9 30.5 %copy-start.24 = (f32[8,8,1152]{2,1,0:T(8,128)S(1)}, f32[8,8,1152]{2,1,0:T(8,128)}, u32[]{:S(2)}) copy-start(f32[8,8,1152]{2,1,0:T(8,128)} %get-tuple-element.201) | copy-start | bytes 884740
  403.9 30.5 %copy-start.25 = (f32[8,8,1152]{2,1,0:T(8,128)S(1)}, f32[8,8,1152]{2,1,0:T(8,128)}, u32[]{:S(2)}) copy-start(f32[8,8,1152]{2,1,0:T(8,128)} %get-tuple-element.196) | copy-start | bytes 884740
  403.9 30.5 %copy-start.26 = (f32[8,8,1152]{2,1,0:T(8,128)S(1)}, f32[8,8,1152]{2,1,0:T(8,128)}, u32[]{:S(2)}) copy-start(f32[8,8,1152]{2,1,0:T(8,128)} %get-tuple-element.198) | copy-start | bytes 884740
  403.9 31.7 %copy-start.28 = (f32[1,4352]{1,0:T(1,128)S(1)}, f32[1,4352]{1,0:T(1,128)}, u32[]{:S(2)}) copy-start(f32[1,4352]{1,0:T(1,128)} %get-tuple-element.203) | copy-start | bytes 52228
  404.0 31.7 %copy-start.29 = (f32[1,4352]{1,0:T(1,128)S(1)}, f32[1,4352]{1,0:T(1,128)}, u32[]{:S(2)}) copy-start(f32[1,4352]{1,0:T(1,128)} %get-tuple-element.205) | copy-start | bytes 52228
  404.0 31.7 %copy-start.30 = (f32[1,4352]{1,0:T(1,128)S(1)}, f32[1,4352]{1,0:T(1,128)}, u32[]{:S(2)}) copy-start(f32[1,4352]{1,0:T(1,128)} %get-tuple-element.207) | copy-start | bytes 52228
  404.0 31.7 %copy-start.31 = (f32[1,4352]{1,0:T(1,128)S(1)}, f32[1,4352]{1,0:T(1,128)}, u32[]{:S(2)}) copy-start(f32[1,4352]{1,0:T(1,128)} %get-tuple-element.202) | copy-start | bytes 52228
  404.0 31.7 %copy-start.32 = (f32[1,4352]{1,0:T(1,128)S(1)}, f32[1,4352]{1,0:T(1,128)}, u32[]{:S(2)}) copy-start(f32[1,4352]{1,0:T(1,128)} %get-tuple-element.204) | copy-start | bytes 52228
  660.8 7.6 %copy-start.13 = (bf16[3,288,4608]{2,1,0:T(8,128)(2,1)S(1)}, bf16[3,288,4608]{2,1,0:T(8,128)(2,1)}, u32[]{:S(2)}) copy-start(bf16[3,288,4608]{2,1,0:T(8,128)(2,1)} %get-tuple-element.216) | copy-start | bytes 23887876
  668.5 4.7 copy-start.27
  (15 other events, 18.0 us)

commit v4 on v3

--- a/solution.py
+++ b/solution.py
@@ -131,7 +131,7 @@
         body(whole * step, width % step)
 
 
-def f_layer(slots, total, wide, final, x, vec, qb, ub, G, tok, kept):
+def f_layer(slots, total, final, x, vec, qb, ub, G, base, tok, kept):
     T, D = x.shape
     hidden = ub.shape[1]
     images = T // tok
@@ -147,16 +147,18 @@
             work(slot, *refs)
 
     def work(slot, *refs):
-        x, vec, qb, ub, G = refs[:plain]
+        x_in, vec, qb, ub, G = refs[:plain]
         (n1o, qkvo, Po, co, r1o, n2o, go, gpo, reso, y,
-         wa, wb, n1, qkv, P, c, r1, n2, g, gp, res, wsem, psem, gsem, osem) = refs[plain + spare:]
+         x, wa, wb, n1, qkv, P, c, r1, n2, g, gp, res, wsem, psem, gsem, osem) = refs[plain + spare:]
         save = pl.ds(pl.multiple_of(slot[0] * T, 16), T)
 
         def weight(j):
             a, w = cut[j]
-            return pltpu.make_async_copy(G.at[0, :, pl.ds(a, w)], wa.at[:, pl.ds(a, w)], wsem.at[j])
-        up = pltpu.make_async_copy(G.at[1, :, pl.ds(0, hidden)], wb, wsem.at[len(cut)])
-        down = pltpu.make_async_copy(G.at[2, :, pl.ds(0, hidden)], wa.at[:, pl.ds(0, hidden)], wsem.at[len(cut) + 1])
+            return pltpu.make_async_copy(G.at[:, pl.ds(a, w)], wa.at[:, pl.ds(a, w)], wsem.at[j])
+        up = pltpu.make_async_copy(G.at[:, pl.ds(base, hidden)], wb, wsem.at[len(cut)])
+        down = pltpu.make_async_copy(G.at[:, pl.ds(base + hidden, hidden)], wa.at[:, pl.ds(0, hidden)], wsem.at[len(cut) + 1])
+        tokens = pltpu.make_async_copy(x_in, x, wsem.at[len(cut) + 2])
+        tokens.start()
         for j in range(len(cut)):
             weight(j).start()
         up.start()
@@ -164,12 +166,13 @@
         def out(source, target, at, k):
             return pltpu.make_async_copy(source, target.at[at], osem.at[k])
         outs = [out(n1, n1o, save, 0), out(qkv, qkvo, save, 1), out(c, co, save, 2), out(r1, r1o, save, 3),
-                out(n2, n2o, save, 4), out(g, go, (save, pl.ds(0, hidden)), 5)]
+                out(n2, n2o, save, 4), out(g, go, save, 5)]
         if final:
             outs.append(out(res, reso, save, 6))
 
         def first(at):
             n1[at, :] = (normal(x[at, :].astype(F32))[0] * vec[0:1, :] + vec[1:2, :]).astype(HALF)
+        tokens.wait()
         row_loop(T, tok, first)
         outs[0].start()
         for j, (a, w) in enumerate(cut):
@@ -255,23 +258,23 @@
         kernel,
         out_shape=(shape(total, D, HALF), shape(total, 3 * D, HALF),
                    jax.ShapeDtypeStruct((total // tok, HEADS, tok, tok), HALF), shape(total, D, HALF), shape(total, D, F32),
-                   shape(total, D, HALF), shape(total, wide, HALF), shape(total, hidden, HALF), shape(total, D, F32),
+                   shape(total, D, HALF), shape(total, hidden, HALF), shape(total, hidden, HALF), shape(total, D, F32),
                    shape(T, D, HALF)),
         grid_spec=pltpu.PrefetchScalarGridSpec(
-            num_scalar_prefetch=1, grid=(1,), in_specs=[whole] * 4 + [ANY] * (1 + spare), out_specs=(ANY,) * 9 + (whole,),
+            num_scalar_prefetch=1, grid=(1,), in_specs=[ANY] + [whole] * 3 + [ANY] + [ANY] * spare, out_specs=(ANY,) * 9 + (whole,),
             scratch_shapes=[
-                pltpu.VMEM((D, 4 * D), HALF), pltpu.VMEM((D, hidden), HALF), pltpu.VMEM((T, D), HALF),
+                pltpu.VMEM((T, D), HALF), pltpu.VMEM((D, 4 * D), HALF), pltpu.VMEM((D, hidden), HALF), pltpu.VMEM((T, D), HALF),
                 pltpu.VMEM((T, 3 * D), HALF), pltpu.VMEM((2, HEADS, tok, tok), HALF), pltpu.VMEM((T, D), HALF),
                 pltpu.VMEM((T, D), F32), pltpu.VMEM((T, D), HALF), pltpu.VMEM((T, hidden), HALF),
                 pltpu.VMEM((2, T, TILE), HALF), pltpu.VMEM((T, D), F32),
-                dma((len(cut) + 2,)), dma((2,)), dma((2,)), dma((7,))]),
+                dma((len(cut) + 3,)), dma((2,)), dma((2,)), dma((7,))]),
         input_output_aliases=aliases,
         compiler_params=params(60),
         cost_estimate=pl.CostEstimate(flops=T * D, bytes_accessed=T * D, transcendentals=0),
     )(slots, *ins)
 
 
-def d_layer(slots, total, wide, final, e, x, vec, G, GP, R1, QKV, PP, tok, kept):
+def d_layer(slots, total, final, e, x, vec, G, base, GP, R1, QKV, PP, tok, kept):
     T, D = x.shape
     hidden = GP.shape[1]
     images = T // tok
@@ -285,26 +288,31 @@
             work(slot, *refs)
 
     def work(slot, *refs):
-        e, x, vec, G, GP, R1, QKV, PP = refs[:plain]
+        e_in, x_in, vec, G, GP, R1, QKV, PP = refs[:plain]
         (duo, lowo, dqkvo, reso, dx, stats, sums,
-         wa, wb, gp, r1, qkv, P, du, grad, dr1, low, dc, dqkv, wsem, psem, isem, osem) = refs[plain + spare:]
+         e, x, wa, wb, gp, r1, qkv, P, du, grad, dr1, low, dc, dqkv, wsem, psem, isem, osem) = refs[plain + spare:]
         save = pl.ds(pl.multiple_of(slot[0] * T, 16), T)
         cuts = pieces(hidden, 2 * TILE)
-        down = [pltpu.make_async_copy(G.at[2, :, pl.ds(a, w)], wa.at[:, pl.ds(a, w)], wsem.at[2 + j]) for j, (a, w) in enumerate(cuts)]
+        down = [pltpu.make_async_copy(G.at[:, pl.ds(base + hidden + a, w)], wa.at[:, pl.ds(a, w)], wsem.at[2 + j]) for j, (a, w) in enumerate(cuts)]
         slope = [pltpu.make_async_copy(GP.at[save, pl.ds(a, w)], gp.at[:, pl.ds(a, w)], isem.at[2 + j]) for j, (a, w) in enumerate(cuts)]
-        up = pltpu.make_async_copy(G.at[1, :, pl.ds(0, hidden)], wb, wsem.at[0])
-        rest = pltpu.make_async_copy(G.at[0, :, pl.ds(0, 4 * D)], wa, wsem.at[1])
+        up = pltpu.make_async_copy(G.at[:, pl.ds(base, hidden)], wb, wsem.at[0])
+        rest = pltpu.make_async_copy(G.at[:, pl.ds(0, 4 * D)], wa, wsem.at[1])
         loads = [pltpu.make_async_copy(R1.at[save], r1, isem.at[0]), pltpu.make_async_copy(QKV.at[save], qkv, isem.at[1])]
+        count = len(cuts)
+        cotangent = pltpu.make_async_copy(e_in, e, isem.at[2 + count])
+        tokens = pltpu.make_async_copy(x_in, x, isem.at[3 + count])
+        cotangent.start()
         for weight, factor in zip(down, slope):
             weight.start()
             factor.start()
         up.start()
+        tokens.start()
         for copy in loads:
             copy.start()
 
         def out(source, target, at, k):
             return pltpu.make_async_copy(source, target.at[at], osem.at[k])
-        outs = [out(du, duo, (save, pl.ds(0, hidden)), 0), out(low, lowo, save, 1), out(dqkv, dqkvo, save, 2)]
+        outs = [out(du, duo, save, 0), out(low, lowo, save, 1), out(dqkv, dqkvo, save, 2)]
         if final:
             outs.append(out(dr1, reso, save, 3))
 
@@ -323,6 +331,7 @@
                 part = jnp.sum(d.astype(F32), axis=0, keepdims=True)
                 total = part if total is None else total + part
             sums[:, at] = total
+        cotangent.wait()
         for j, (a, w) in enumerate(cuts):
             down[j].wait()
             slope[j].wait()
@@ -364,6 +373,7 @@
             return carry
         lax.fori_loop(0, images, image, 0)
         outs[2].start()
+        tokens.wait()
         for a, w in pieces(D, LANES):
             grad[:, a:a + w] = mul(dqkv[...], wa[a:a + w, 0:3 * D], NT)
 
@@ -393,16 +403,17 @@
     whole = pl.BlockSpec(memory_space=pltpu.VMEM)
     return pl.pallas_call(
         kernel,
-        out_shape=(shape(total, wide, HALF), shape(total, D, HALF), shape(total, 3 * D, HALF), shape(total, D, F32),
+        out_shape=(shape(total, hidden, HALF), shape(total, D, HALF), shape(total, 3 * D, HALF), shape(total, D, F32),
                    shape(T, D, HALF), jax.ShapeDtypeStruct((8, 8, D), F32), shape(1, hidden, F32)),
         grid_spec=pltpu.PrefetchScalarGridSpec(
-            num_scalar_prefetch=1, grid=(1,), in_specs=[whole] * 3 + [ANY] * (5 + spare), out_specs=(ANY,) * 4 + (whole,) * 3,
+            num_scalar_prefetch=1, grid=(1,), in_specs=[ANY] * 2 + [whole] + [ANY] + [ANY] * (4 + spare), out_specs=(ANY,) * 4 + (whole,) * 3,
             scratch_shapes=[
+                pltpu.VMEM((T, D), HALF), pltpu.VMEM((T, D), HALF),
                 pltpu.VMEM((D, 4 * D), HALF), pltpu.VMEM((D, hidden), HALF), pltpu.VMEM((T, hidden), HALF),
                 pltpu.VMEM((T, D), F32), pltpu.VMEM((T, 3 * D), HALF), pltpu.VMEM((2, HEADS, tok, tok), HALF),
                 pltpu.VMEM((T, hidden), HALF), pltpu.VMEM((T, D), F32), pltpu.VMEM((T, D), F32), pltpu.VMEM((T, D), HALF),
                 pltpu.VMEM((T, D), HALF), pltpu.VMEM((T, 3 * D), HALF),
-                dma((2 + len(pieces(hidden, 2 * TILE)),)), dma((2,)), dma((2 + len(pieces(hidden, 2 * TILE)),)), dma((4,))]),
+                dma((2 + len(pieces(hidden, 2 * TILE)),)), dma((2,)), dma((4 + len(pieces(hidden, 2 * TILE)),)), dma((4,))]),
         input_output_aliases=aliases,
         compiler_params=params(60),
         cost_estimate=pl.CostEstimate(flops=T * D, bytes_accessed=T * D, transcendentals=0),
@@ -419,11 +430,13 @@
 
 def gather_kernel(n, R, halves, qkv, out, up, down, *refs):
     (gain_one, shift_one, bias_qv, bias_out, gain_two, shift_two, bias_down, bias_up,
-     G, vec, qb, ub, stage, S, lsem, ssem, rsem, small_send, small_recv) = refs
+     G, vec, qb, ub, stage_a, stage_b, S, lsem, ssem, rsem, small_send, small_recv) = refs
     z = lax.axis_index("fsdp")
     r = lax.axis_index("replica")
-    rows, wide = up.shape
-    part = wide // R
+    rows, filled = up.shape
+    stage = (stage_a, stage_b)
+    part = [ref.shape[1] // R for ref in stage]
+    base = (0, stage_a.shape[1])
     some = rows // halves
     bits = powers(R)
     barrier = pltpu.get_barrier_semaphore()
@@ -434,14 +447,14 @@
     mine = pl.ds(pl.multiple_of(z * rows, 16), rows)
     first = qkv.shape[1]
     local = [
-        pltpu.make_async_copy(qkv, stage.at[0, :, pl.ds(0, first)], lsem.at[0]),
-        pltpu.make_async_copy(out, stage.at[0, :, pl.ds(first, out.shape[1])], lsem.at[1]),
-        pltpu.make_async_copy(up, stage.at[1], lsem.at[2]),
-        pltpu.make_async_copy(down, stage.at[2], lsem.at[3]),
+        pltpu.make_async_copy(qkv, stage_a.at[:, pl.ds(0, first)], lsem.at[0]),
+        pltpu.make_async_copy(out, stage_a.at[:, pl.ds(first, out.shape[1])], lsem.at[1]),
+        pltpu.make_async_copy(up, stage_b.at[:, pl.ds(0, filled)], lsem.at[2]),
+        pltpu.make_async_copy(down, stage_b.at[:, pl.ds(filled, filled)], lsem.at[3]),
     ]
     for copy in local:
         copy.start()
-    keep = [pltpu.make_async_copy(stage.at[group], G.at[group, mine], lsem.at[4 + group]) for group in range(3)]
+    keep = [pltpu.make_async_copy(stage[group], G.at[mine, pl.ds(base[group], stage[group].shape[1])], lsem.at[4 + group]) for group in range(2)]
 
     for row, value in enumerate((gain_one, shift_one, None, None, bias_out, gain_two, shift_two, bias_down, bias_up)):
         value = bias_qv[row - 2:row - 1, :] if value is None else value[...]
@@ -450,8 +463,8 @@
 
     def piece(unit, source, column):
         group, half = unit // halves, unit % halves
-        return G.at[group, pl.ds(pl.multiple_of(source * rows + half * some, 16), some),
-                    pl.ds(pl.multiple_of(column * part, 128), part)]
+        return G.at[pl.ds(pl.multiple_of(source * rows + half * some, 16), some),
+                    pl.ds(pl.multiple_of(base[group] + column * part[group], 128), part[group])]
 
     def send(unit, source, column, kind, target, origin=None):
         return pltpu.make_async_remote_copy(
@@ -466,7 +479,8 @@
         return send(unit, source, r, 1, {"fsdp": z - 1}, origin)
 
     def own(unit):
-        return stage.at[unit // halves, pl.ds(unit % halves * some, some), pl.ds(pl.multiple_of(r * part, 128), part)]
+        wide = part[unit // halves]
+        return stage[unit // halves].at[pl.ds(unit % halves * some, some), pl.ds(pl.multiple_of(r * wide, 128), wide)]
 
     def share(unit, source, column, level):
         return send(unit, source, column, 2 + level, {"replica": r ^ bits[level]})
@@ -480,28 +494,27 @@
             recv_sem=small_recv.at[z], device_id={"fsdp": lax.rem(z + hop, n)}, device_id_type=MESH)
     for hop in range(1, n):
         small_to(hop).start()
-    for group in range(3):
-        if group == 0:
-            local[0].wait()
-            local[1].wait()
-        else:
-            local[1 + group].wait()
-        for unit in range(group * halves, (group + 1) * halves):
-            @pl.when(z + 1 < n)
-            def _():
-                to_right(unit, z, own(unit)).start()
-            @pl.when(z > 0)
-            def _():
-                to_left(unit, z, own(unit)).start()
-        keep[group].start()
+    order = [0] + list(range(halves, 2 * halves)) + list(range(1, halves))
+    for unit in order:
+        group = unit // halves
+        if unit % halves == 0:
+            local[2 * group].wait()
+            local[2 * group + 1].wait()
+            keep[group].start()
+        @pl.when(z + 1 < n)
+        def _():
+            to_right(unit, z, own(unit)).start()
+        @pl.when(z > 0)
+        def _():
+            to_left(unit, z, own(unit)).start()
     columns = {}
     for level, bit in enumerate(bits):
         masks = [0]
         for upper in bits[:level]:
             masks = masks + [m | upper for m in masks]
         columns[level] = [bit | m for m in masks]
-    units = 3 * halves
-    steps = [(hop, unit) for hop in range(1, n) for unit in range(units)]
+    units = 2 * halves
+    steps = [(hop, unit) for hop in range(1, n) for unit in order]
     for turn in range(len(steps) + len(bits)):
         for level in range(-1, len(bits)):
             place = turn - 1 - level
@@ -564,26 +577,27 @@
                             share(unit, source, r ^ mask, lower).wait_send()
 
 
-def gather_weights(n, R, filled, qkv, out, up, down, vectors):
-    rows, wide = up.shape
+def gather_weights(n, R, wide, filled, qkv, out, up, down, vectors):
+    rows = up.shape[0]
     kinds = 2 + len(powers(R))
-    halves = 2 if rows % 32 == 0 else 1
+    halves = 3 if rows % 48 == 0 else 1
     lanes = -(-max(v.shape[1] for v in vectors) // 128) * 128
     dma = pltpu.SemaphoreType.DMA
     whole = pl.BlockSpec(memory_space=pltpu.VMEM)
     D = n * rows
     return pl.pallas_call(
         functools.partial(gather_kernel, n, R, halves),
-        out_shape=(jax.ShapeDtypeStruct((3, D, wide), qkv.dtype), shape(8, D, F32), shape(1, 3 * D, F32),
+        out_shape=(shape(D, sum(wide), HALF), shape(8, D, F32), shape(1, 3 * D, F32),
                    shape(1, filled, F32)),
         in_specs=[ANY] * 4 + [whole] * len(vectors),
         out_specs=(ANY,) + (whole,) * 3,
         scratch_shapes=[
-            pltpu.VMEM((3, rows, wide), qkv.dtype),
+            pltpu.VMEM((rows, wide[0]), HALF),
+            pltpu.VMEM((rows, wide[1]), HALF),
             pltpu.VMEM((n, 16, lanes), F32),
-            dma((7,)),
-            dma((3 * halves, n, R, kinds)),
-            dma((3 * halves, n, R)),
+            dma((6,)),
+            dma((2 * halves, n, R, kinds)),
+            dma((2 * halves, n, R)),
             dma((n,)),
             dma((n,)),
         ],
@@ -591,14 +605,15 @@
     )(qkv, out, up, down, *vectors)
 
 
-ORDER = (2, 1, 0)
+ORDER = (1, 0)
 SCRATCH = 26
 
 
-def plan(R, part, D):
+def plan(R, parts, D, filled):
     found = []
-    for place in range(3):
-        edges = (3 * D, 4 * D) if ORDER[place] == 0 else ()
+    for place, group in enumerate(ORDER):
+        edges = (filled, 2 * filled) if group else (3 * D, 4 * D)
+        part = parts[group]
         sizes, at = [], 0
         while at < part:
             size = min(max(12 // R, 1) * 128, part - at)
@@ -608,7 +623,7 @@
             at += size
         if place == 0 and sizes[0] == 384:
             sizes[:1] = [128, 256]
-        if place == 2 and sizes[-1] > 128:
+        if place == 1 and sizes[-1] > 128:
             sizes[-1:] = [sizes[-1] - 128, 128]
         at = 0
         for size in sizes:
@@ -633,8 +648,9 @@
 
 
 def reduce_kernel(n, R, chunks, small_in, n1, c, n2, rows_in, dqkv, low, du, g, *refs):
-    back = refs[:-2 - SCRATCH - (R.bit_length() - 1)]
-    F, small_out, *scratch = refs[len(back):]
+    back = refs[:-3 - SCRATCH - (R.bit_length() - 1)]
+    F_a, F_b, small_out, *scratch = refs[len(back):]
+    F = (F_a, F_b)
     L = R.bit_length() - 1
     bits = [1 << level for level in range(L)]
     held = scratch[:L]
@@ -645,8 +661,8 @@
     tokens, D = n1.shape
     full = D
     rows = full // n
-    wide = F.shape[2]
-    part = wide // R
+    filled = g.shape[1]
+    part = [ref.shape[1] // R for ref in F]
     K = len(chunks)
     every, kind, _ = places(chunks, L)
     barrier = pltpu.get_barrier_semaphore()
@@ -659,7 +675,7 @@
         return ORDER[chunks[k][0]]
 
     def columns(k, p):
-        return pl.ds(pl.multiple_of(p * part + chunks[k][1], 128), chunks[k][2])
+        return pl.ds(pl.multiple_of(p * part[group(k)] + chunks[k][1], 128), chunks[k][2])
 
     def part_lanes(k, p):
         return pl.ds(pl.multiple_of(p * chunks[k][2], 128), chunks[k][2])
@@ -671,11 +687,13 @@
         return (r & ((2 << level) - 1)) | (j << (level + 1))
 
     def factors(k, p):
-        a, sub = p * part + chunks[k][1], chunks[k][2]
-        if group(k) == 2:
-            return 0, g.at[:, pl.ds(a, sub)]
+        a, sub = p * part[group(k)] + chunks[k][1], chunks[k][2]
         if group(k) == 1:
-            return 1, du.at[:, pl.ds(a, sub)]
+            if a < filled:
+                return 1, du.at[:, pl.ds(a, sub)]
+            if a < 2 * filled:
+                return 0, g.at[:, pl.ds(a - filled, sub)]
+            return None, None
         if a < 3 * D:
             return 0, dqkv.at[:, pl.ds(a, sub)]
         if a < 4 * D:
@@ -691,11 +709,11 @@
                 fetch(k, p).start()
 
     def fetch_left(which):
-        return pltpu.make_async_copy((rows_in, n2, n1, c)[which], stage, lsem.at[0])
+        return pltpu.make_async_copy((rows_in, n2, n1, c)[which], stage.at[which % 2], lsem.at[which])
 
     def fetch_back(m):
         some = tokens // len(back)
-        return pltpu.make_async_copy(back[m], stage.at[pl.ds(m * some, some), :], lsem.at[m])
+        return pltpu.make_async_copy(back[m], stage.at[0, pl.ds(m * some, some), :], lsem.at[4 + m])
 
     def first_left(act):
         @pl.when(lax.axis_index("section") == 0)
@@ -712,18 +730,17 @@
         else:
             fetch_left(which).wait()
         for a in range(0, D, 128):
-            left[which % 2, a:a + 128, :] = stage[:, a:a + 128].T
-        if which < 3:
-            fetch_left(which + 1).start()
+            left[which % 2, a:a + 128, :] = stage[which % 2, :, a:a + 128].T
+        if which < 2:
+            fetch_left(which + 2).start()
 
     def own(k):
         if k >= 2:
             for j in range(R // 2):
                 give(0, k - 2, j).wait_send()
         if chunks[k][1] == 0:
-            turn_left(chunks[k][0])
-            if chunks[k][0] == 2:
-                turn_left(3)
+            turn_left(2 * chunks[k][0])
+            turn_left(2 * chunks[k][0] + 1)
         size = chunks[k][2]
         runs = []
         for p in range(R):
@@ -866,7 +883,7 @@
         both_ends(act)
 
     def finished(k, p):
-        return F.at[group(k), :, columns(k, p)]
+        return F[group(k)].at[:, columns(k, p)]
 
     def share(k, p, level, source=None):
         return pltpu.make_async_remote_copy(
@@ -910,6 +927,7 @@
             device_id={"replica": p}, device_id_type=MESH)
 
     first_left(lambda copy: copy.start())
+    fetch_left(1).start()
     fetch_all(0)
     pl.semaphore_wait(barrier, n - 1 + R - 1)
     own_small = pltpu.make_async_copy(small_in.at[z], small_z.at[z], ss_l)
@@ -999,8 +1017,7 @@
 def reduce_grads(n, R, wide, small, n1, c, n2, rows_in, dqkv, low, du, g, back):
     tokens, D = n1.shape
     rows = D // n
-    part = wide // R
-    chunks = plan(R, part, D)
+    chunks = plan(R, [w // R for w in wide], D, g.shape[1])
     K = len(chunks)
     most = max(size for _, _, size in chunks)
     L = R.bit_length() - 1
@@ -1009,14 +1026,14 @@
     dma = pltpu.SemaphoreType.DMA
     return pl.pallas_call(
         functools.partial(reduce_kernel, n, R, chunks),
-        out_shape=(jax.ShapeDtypeStruct((3, rows, wide), HALF),
+        out_shape=(shape(rows, wide[0], HALF), shape(rows, wide[1], HALF),
                    jax.ShapeDtypeStruct(small.shape[1:], small.dtype)),
         in_specs=[pl.BlockSpec(memory_space=pltpu.VMEM)] + [ANY] * (8 + len(back)),
-        out_specs=(ANY, pl.BlockSpec(memory_space=pltpu.VMEM)),
+        out_specs=(ANY, ANY, pl.BlockSpec(memory_space=pltpu.VMEM)),
         scratch_shapes=[pltpu.VMEM((R >> (level + 1), D, one if level == L - 1 else both), HALF) for level in range(L)] + [
             pltpu.VMEM((2, D, R * most), HALF),
             pltpu.VMEM((2, D, tokens), HALF),
-            pltpu.VMEM((tokens, D), HALF),
+            pltpu.VMEM((2, tokens, D), HALF),
             pltpu.VMEM((tokens, R * most), HALF),
             pltpu.VMEM((2, n - 1, rows, one), HALF),
             pltpu.VMEM((2, n - 1, 2, rows, two), HALF),
@@ -1024,7 +1041,7 @@
             pltpu.VMEM((n,) + small.shape[1:], small.dtype),
             pltpu.VMEM((R,) + small.shape[1:], small.dtype),
             pltpu.VMEM(small.shape[1:], small.dtype),
-            dma((R,)), dma((len(back),)),
+            dma((R,)), dma((4 + len(back),)),
             dma((L, K, R // 2)), dma((L, K, R // 2)),
             dma((K, 2, n, 2)), dma((K, 2, n, 2)),
             dma((K,)), dma((K,)),
@@ -1055,10 +1072,10 @@
     piece = D // n
     unit = 128 * R
     filled = -(-hidden // LANES) * LANES
-    wide = max(-(-4 * D // unit), -(-filled // unit)) * unit
+    wide = [-(-columns // unit) * unit for columns in (4 * D, 2 * filled)]
 
     G, vec, qb, ub = gather_weights(
-        n, R, filled, qkv_weight[0], out_weight[0], pad_columns(up_weight[0], wide), pad_columns(down_weight[0].T, wide),
+        n, R, wide, filled, qkv_weight[0], out_weight[0], pad_columns(up_weight[0], filled), pad_columns(down_weight[0].T, filled),
         (first_gain, first_shift, qv_bias[0], out_bias, second_gain, second_shift, down_bias, up_bias))
 
     rows = ends[0].reshape(images * tok, D)
@@ -1073,10 +1090,10 @@
     kept = (None,) * 9
     sent = []
     for micro in range(MICRO):
-        *kept, y = f_layer(turn(micro, 0), total, wide, False, parts[micro], vec, qb, ub, G, tok, kept)
+        *kept, y = f_layer(turn(micro, 0), total, False, parts[micro], vec, qb, ub, G, wide[0], tok, kept)
         sent.append(shifted(y, "section", 1))
     for micro in range(MICRO):
-        *kept, y = f_layer(turn(micro, 1), total, wide, True, sent[micro], vec, qb, ub, G, tok, kept)
+        *kept, y = f_layer(turn(micro, 1), total, True, sent[micro], vec, qb, ub, G, wide[0], tok, kept)
     n1, qkv, probs, c, r1, n2, g, gp, result = kept
 
     kept = (None, None, None, result)
@@ -1085,7 +1102,7 @@
     for where in (1, 0):
         for micro in range(MICRO):
             e, x = (parts[micro], sent[micro]) if where else (back[micro], parts[micro])
-            *kept, dx, stat, part = d_layer(turn(micro, where), total, wide, where == 0, e, x, vec, G, gp, r1, qkv, probs, tok, kept)
+            *kept, dx, stat, part = d_layer(turn(micro, where), total, where == 0, e, x, vec, G, wide[0], gp, r1, qkv, probs, tok, kept)
             stats.append(stat)
             sums.append(part)
             if where:
@@ -1100,22 +1117,22 @@
     vectors = jnp.concatenate([vectors, sums[0, :hidden].reshape(n, hidden // n)], axis=1)
     lanes = -(-vectors.shape[1] // (16 * 128)) * 128
     small = jnp.pad(vectors, ((0, 0), (0, 16 * lanes - vectors.shape[1]))).reshape(n, 16, lanes)
-    F, s = reduce_grads(n, R, wide, small, n1, c, n2, rows, dqkv, low, du, g, back)
+    F_a, F_b, s = reduce_grads(n, R, wide, small, n1, c, n2, rows, dqkv, low, du, g, back)
     s = s.reshape(-1)
     v = s[: 8 * piece].reshape(8, piece)
     return (
         result.reshape(1, images, tok, D),
         v[0][None],
         v[1][None],
-        F[0, :, : 3 * D].astype(F32)[None],
+        F_a[:, : 3 * D].astype(F32)[None],
         v[2:4][None],
-        F[0, :, 3 * D : 4 * D].astype(F32)[None],
+        F_a[:, 3 * D : 4 * D].astype(F32)[None],
         v[4][None],
         v[5][None],
         v[6][None],
-        F[1, :, :hidden].astype(F32)[None],
+        F_b[:, :hidden].astype(F32)[None],
         s[8 * piece : 8 * piece + hidden // n][None],
-        F[2, :, :hidden].T.astype(F32)[None],
+        F_b[:, filled : filled + hidden].T.astype(F32)[None],
         v[7][None],
     )
 

time: 678 us -> 671 us (0.990)
  Pallas kernels: 587 us -> 579 us
  transfers between devices with their start and end apart: 6 -> 6, of which waited for: 2 -> 2; matrix products, arithmetic and copies ran while one was open for 0% -> 0% of each run, Pallas kernels for 20% -> 21%
where the time goes in v4:
time: 671 us; the launch traced here: 666 us
  Pallas kernels  579 us (86%)
  waiting for transfers between devices  46.8 us (7%)
  other arithmetic  15.9 us (2%)
  local copies, waits for them, and re-layouts  15 us (2%)
  starting transfers between devices  7.88 us (1%)
    pallas_call x1, Pallas kernels, reduce_grads(): pl.pallas_call(functools.partial(reduce_kernel, n, R, chunks), out_shape=...  219 us
    pallas_call x1, Pallas kernels, gather_weights(): pl.pallas_call(functools.partial(gather_kernel, n, R, halves), out_shape=...  153 us
    pallas_call x6, Pallas kernels, d_layer(): pl.pallas_call(kernel, out_shape=(shape(total, hidden, HALF), shape(total...  118 us
    pallas_call x6, Pallas kernels, f_layer(): pl.pallas_call(kernel, out_shape=(shape(total, D, HALF), shape(total, 3 *...  88.4 us
    ppermute x6, waiting for transfers between devices, shifted(): lax.ppermute(value, axis, [(source, source + steps) for source in range(f...  46.8 us
  transfers between devices with their start and end apart: 6, of which 2 were waited for; matrix products, arithmetic and copies ran while one was open for 0% of the time, Pallas kernels for 21%

profile of v4, /device:TPU:1, one launch (start us, length us, event | category | flops | bytes accessed | tf_op | source)
XLA Modules:
  0.0 665.7 jit_solution(1961912855566135473)
XLA Ops:
  0.7 3.1 fusion.3
  5.7 153.3 %shard_map.228 = (bf16[1152,13312]{1,0:T(8,128)(2,1)}, f32[8,1152]{1,0:T(8,128)S(1)}, f32[1,3456]{1,0:T(1,128)S(1)}, f32[1,4352]{1,0:T(1,128)S(1)}) custom-call(bf16[288,3456]{1,0:T(8,128)(2,1)S(1)} %bitcast.37, bf16[288,1152]{1,0:T(8,128)(2,1)S(1)} %bitcast.38, bf16[288,4352]{1,0:T(8,128)(2,1)S(1)} %pad.11.up, bf16[288,4352]{1,0:T(8,128)(2,1)S(1)} %pad.12.down, ...), custom_call_target="tpu_custom_call" | custom-call | tf_op jit(solution)/shard_map/pallas_call | solution.py:588
  160.8 25.8 %shard_map.229 = (bf16[960,1152]{1,0:T(8,128)(2,1)}, bf16[960,3456]{1,0:T(8,128)(2,1)}, bf16[6,16,160,160]{3,2,1,0:T(8,128)(2,1)}, bf16[960,1152]{1,0:T(8,128)(2...) custom-call(s32[2]{0:T(128)} %pad_add_fusion.5.slot, ...), custom_call_target="tpu_custom_call" | custom-call | flops 368640 | bytes 368640 | tf_op jit(solution)/shard_map/pallas_call | solution.py:257
  186.6 1.3 collective-permute-start.2
  188.5 25.4 %shard_map.230 = (bf16[960,1152]{1,0:T(8,128)(2,1)}, bf16[960,3456]{1,0:T(8,128)(2,1)}, bf16[6,16,160,160]{3,2,1,0:T(8,128)(2,1)}, bf16[960,1152]{1,0:T(8,128)(2...) custom-call(s32[2]{0:T(128)} %get-tuple-element.233.slot, ...), custom_call_target="tpu_custom_call", output_to_operand_aliasing={{0}: (6, {}), {1}: (7, {}), {2}: (8, {}), {3}: (9, {}), {4}... | custom-call | flops 368640 | bytes 368640 | tf_op jit(solution)/shard_map/pallas_call | solution.py:257
  214.0 1.3 collective-permute-start.1
  215.3 25.5 %shard_map.231 = (bf16[960,1152]{1,0:T(8,128)(2,1)}, bf16[960,3456]{1,0:T(8,128)(2,1)}, bf16[6,16,160,160]{3,2,1,0:T(8,128)(2,1)}, bf16[960,1152]{1,0:T(8,128)(2...) custom-call(s32[2]{0:T(128)} %get-tuple-element.232.slot, ...), custom_call_target="tpu_custom_call", output_to_operand_aliasing={{0}: (6, {}), {1}: (7, {}), {2}: (8, {}), {3}: (9, {}), {4}... | custom-call | flops 368640 | bytes 368640 | tf_op jit(solution)/shard_map/pallas_call | solution.py:257
  240.8 1.3 collective-permute-start
  244.8 2.9 shard_map.232
  248.6 6.2 shard_map.233
  254.7 3.8 collective-permute-done.refs_0_.refs_1_
  259.4 2.7 shard_map.234
  262.1 10.2 %shard_map.235 = (bf16[960,4352]{1,0:T(8,128)(2,1)}, bf16[960,1152]{1,0:T(8,128)(2,1)}, bf16[960,3456]{1,0:T(8,128)(2,1)}, f32[960,1152]{1,0:T(8,128)}, bf16[320...) custom-call(s32[2]{0:T(128)} %pad_add_fusion.4.slot, ...), custom_call_target="tpu_custom_call", output_to_operand_aliasing={{3}: (9, {})} | custom-call | flops 368640 | bytes 368640 | tf_op jit(solution)/shard_map/pallas_call | solution.py:404
  273.6 8.4 %shard_map.236 = (bf16[960,4352]{1,0:T(8,128)(2,1)}, bf16[960,1152]{1,0:T(8,128)(2,1)}, bf16[960,3456]{1,0:T(8,128)(2,1)}, f32[960,1152]{1,0:T(8,128)}, bf16[320...) custom-call(s32[2]{0:T(128)} %pad_add_fusion.2.slot, ...), custom_call_target="tpu_custom_call", output_to_operand_aliasing={{0}: (9, {}), {1}: (10, {}), {2}: (11, {}), {3}: (12, {})} | custom-call | flops 368640 | bytes 368640 | tf_op jit(solution)/shard_map/pallas_call | solution.py:404
  283.3 8.5 %shard_map.237 = (bf16[960,4352]{1,0:T(8,128)(2,1)}, bf16[960,1152]{1,0:T(8,128)(2,1)}, bf16[960,3456]{1,0:T(8,128)(2,1)}, f32[960,1152]{1,0:T(8,128)}, bf16[320...) custom-call(s32[2]{0:T(128)} %pad_add_fusion.slot, ...), custom_call_target="tpu_custom_call", output_to_operand_aliasing={{0}: (9, {}), {1}: (10, {}), {2}: (11, {}), {3}: (12, {})} | custom-call | flops 368640 | bytes 368640 | tf_op jit(solution)/shard_map/pallas_call | solution.py:404
  291.9 1.3 collective-permute-start.3
  293.2 42.9 %collective-permute-done.5.refs_0_ = bf16[320,1152]{1,0:T(8,128)(2,1)S(1)} collective-permute-done((bf16[320,1152]{1,0:T(8,128)(2,1)}, bf16[320,1152]{1,0:T(8,128)(2,1)S(1)}, u32[]{:S(2)}, u32[]{:S(2)}) %collective-permute-start.5) | collective-permute-done | bytes 737312 | tf_op jit(solution)/shard_map/ppermute | solution.py:1058
  337.0 30.4 %shard_map.238 = (bf16[960,4352]{1,0:T(8,128)(2,1)}, bf16[960,1152]{1,0:T(8,128)(2,1)}, bf16[960,3456]{1,0:T(8,128)(2,1)}, f32[960,1152]{1,0:T(8,128)}, bf16[320...) custom-call(s32[2]{0:T(128)} %pad_add_fusion.5.slot, ...), custom_call_target="tpu_custom_call", output_to_operand_aliasing={{0}: (9, {}), {1}: (10, {}), {2}: (11, {}), {3}: (12, {})} | custom-call | flops 368640 | bytes 368640 | tf_op jit(solution)/shard_map/pallas_call | solution.py:404
  368.2 30.1 %shard_map.239 = (bf16[960,4352]{1,0:T(8,128)(2,1)}, bf16[960,1152]{1,0:T(8,128)(2,1)}, bf16[960,3456]{1,0:T(8,128)(2,1)}, f32[960,1152]{1,0:T(8,128)}, bf16[320...) custom-call(s32[2]{0:T(128)} %get-tuple-element.233.slot, ...), custom_call_target="tpu_custom_call", output_to_operand_aliasing={{0}: (9, {}), {1}: (10, {}), {2}: (11, {}), {3}: (12, {})} | custom-call | flops 368640 | bytes 368640 | tf_op jit(solution)/shard_map/pallas_call | solution.py:404
  399.3 30.5 %shard_map.240 = (bf16[960,4352]{1,0:T(8,128)(2,1)}, bf16[960,1152]{1,0:T(8,128)(2,1)}, bf16[960,3456]{1,0:T(8,128)(2,1)}, f32[960,1152]{1,0:T(8,128)}, bf16[320...) custom-call(s32[2]{0:T(128)} %get-tuple-element.232.slot, ...), custom_call_target="tpu_custom_call", output_to_operand_aliasing={{0}: (9, {}), {1}: (10, {}), {2}: (11, {}), {3}: (12, {})} | custom-call | flops 368640 | bytes 368640 | tf_op jit(solution)/shard_map/pallas_call | solution.py:404
  432.8 219.0 %shard_map.241 = (bf16[288,4608]{1,0:T(8,128)(2,1)}, bf16[288,8704]{1,0:T(8,128)(2,1)}, f32[16,256]{1,0:T(8,128)}) custom-call(f32[4,16,256]{2,1,0:T(8,128)} %bitcast.53, bf16[960,1152]{1,0:T(8,128)(2,1)} %get-tuple-element.209.n1, bf16[960,1152]{1,0:T(8,128)(2,1)} %get-tuple-element.210.c, bf16[960,1152]{1,0:T(8,128)(2,1)} %get-tuple-element.211.n2, ...), custom_call_target="tpu_custom_call" | custom-call | tf_op jit(solution)/shard_map/pallas_call | solution.py:1027
  653.9 2.6 bitcast_convert_fusion.2
  656.4 3.7 bitcast_convert_fusion.1
  660.8 4.7 convert_bitcast_fusion
  (97 shorter events, 19.3 us)
Async XLA Ops:
  0.6 3.2 copy-start.20
  0.7 3.9 copy-start.21
  3.8 1.9 copy-start.2
  3.8 1.9 copy-start.5
  3.8 1.9 copy-start.6
  3.8 1.9 copy-start.7
  186.6 57.3 %collective-permute-start.2 = (bf16[320,1152]{1,0:T(8,128)(2,1)}, bf16[320,1152]{1,0:T(8,128)(2,1)S(1)}, u32[]{:S(2)}, u32[]{:S(2)}) collective-permute-start(bf16[320,1152]{1,0:T(8,128)(2,1)} %get-tuple-element.140), channel_id=1, source_target_pairs={{0,16},{1,17},{2,18},{3,19},{4,20},{5,21},{6,22},{7,23},{8,24},{9,... | collective-permute-start | bytes 2211848 | tf_op jit(solution)/shard_map/ppermute | solution.py:1058
  214.0 33.7 %collective-permute-start.1 = (bf16[320,1152]{1,0:T(8,128)(2,1)}, bf16[320,1152]{1,0:T(8,128)(2,1)S(1)}, u32[]{:S(2)}, u32[]{:S(2)}) collective-permute-start(bf16[320,1152]{1,0:T(8,128)(2,1)} %get-tuple-element.139), channel_id=1, source_target_pairs={{0,16},{1,17},{2,18},{3,19},{4,20},{5,21},{6,22},{7,23},{8,24},{9,... | collective-permute-start | bytes 2211848 | tf_op jit(solution)/shard_map/ppermute | solution.py:1058
  240.8 17.7 %collective-permute-start = (bf16[320,1152]{1,0:T(8,128)(2,1)}, bf16[320,1152]{1,0:T(8,128)(2,1)S(1)}, u32[]{:S(2)}, u32[]{:S(2)}) collective-permute-start(bf16[320,1152]{1,0:T(8,128)(2,1)} %get-tuple-element.138), channel_id=1, source_target_pairs={{0,16},{1,17},{2,18},{3,19},{4,20},{5,21},{6,22},{7,23},{8,24},{9,... | collective-permute-start | bytes 2211848 | tf_op jit(solution)/shard_map/ppermute | solution.py:1058
  272.3 63.8 %collective-permute-start.5 = (bf16[320,1152]{1,0:T(8,128)(2,1)}, bf16[320,1152]{1,0:T(8,128)(2,1)S(1)}, u32[]{:S(2)}, u32[]{:S(2)}) collective-permute-start(bf16[320,1152]{1,0:T(8,128)(2,1)} %get-tuple-element.183), channel_id=1, source_target_pairs={{16,0},{17,1},{18,2},{19,3},{20,4},{21,5},{22,6},{23,7},{24,8},{25... | collective-permute-start | bytes 2211848 | tf_op jit(solution)/shard_map/ppermute | solution.py:1058
  282.0 85.3 %collective-permute-start.4 = (bf16[320,1152]{1,0:T(8,128)(2,1)}, bf16[320,1152]{1,0:T(8,128)(2,1)S(1)}, u32[]{:S(2)}, u32[]{:S(2)}) collective-permute-start(bf16[320,1152]{1,0:T(8,128)(2,1)} %get-tuple-element.182), channel_id=1, source_target_pairs={{16,0},{17,1},{18,2},{19,3},{20,4},{21,5},{22,6},{23,7},{24,8},{25... | collective-permute-start | bytes 2211848 | tf_op jit(solution)/shard_map/ppermute | solution.py:1058
  291.9 106.5 %collective-permute-start.3 = (bf16[320,1152]{1,0:T(8,128)(2,1)}, bf16[320,1152]{1,0:T(8,128)(2,1)S(1)}, u32[]{:S(2)}, u32[]{:S(2)}) collective-permute-start(bf16[320,1152]{1,0:T(8,128)(2,1)} %get-tuple-element.181), channel_id=1, source_target_pairs={{16,0},{17,1},{18,2},{19,3},{20,4},{21,5},{22,6},{23,7},{24,8},{25... | collective-permute-start | bytes 2211848 | tf_op jit(solution)/shard_map/ppermute | solution.py:1058
  399.2 30.5 %copy-start.22 = (f32[8,8,1152]{2,1,0:T(8,128)S(1)}, f32[8,8,1152]{2,1,0:T(8,128)}, u32[]{:S(2)}) copy-start(f32[8,8,1152]{2,1,0:T(8,128)} %get-tuple-element.198) | copy-start | bytes 884740
  399.2 30.5 %copy-start.23 = (f32[8,8,1152]{2,1,0:T(8,128)S(1)}, f32[8,8,1152]{2,1,0:T(8,128)}, u32[]{:S(2)}) copy-start(f32[8,8,1152]{2,1,0:T(8,128)} %get-tuple-element.200) | copy-start | bytes 884740
  399.2 30.6 %copy-start.24 = (f32[8,8,1152]{2,1,0:T(8,128)S(1)}, f32[8,8,1152]{2,1,0:T(8,128)}, u32[]{:S(2)}) copy-start(f32[8,8,1152]{2,1,0:T(8,128)} %get-tuple-element.202) | copy-start | bytes 884740
  399.2 30.6 %copy-start.25 = (f32[8,8,1152]{2,1,0:T(8,128)S(1)}, f32[8,8,1152]{2,1,0:T(8,128)}, u32[]{:S(2)}) copy-start(f32[8,8,1152]{2,1,0:T(8,128)} %get-tuple-element.197) | copy-start | bytes 884740
  399.2 30.6 %copy-start.26 = (f32[8,8,1152]{2,1,0:T(8,128)S(1)}, f32[8,8,1152]{2,1,0:T(8,128)}, u32[]{:S(2)}) copy-start(f32[8,8,1152]{2,1,0:T(8,128)} %get-tuple-element.199) | copy-start | bytes 884740
  399.2 31.7 %copy-start.28 = (f32[1,4352]{1,0:T(1,128)S(1)}, f32[1,4352]{1,0:T(1,128)}, u32[]{:S(2)}) copy-start(f32[1,4352]{1,0:T(1,128)} %get-tuple-element.204) | copy-start | bytes 52228
  399.2 31.7 %copy-start.29 = (f32[1,4352]{1,0:T(1,128)S(1)}, f32[1,4352]{1,0:T(1,128)}, u32[]{:S(2)}) copy-start(f32[1,4352]{1,0:T(1,128)} %get-tuple-element.206) | copy-start | bytes 52228
  399.3 31.7 %copy-start.30 = (f32[1,4352]{1,0:T(1,128)S(1)}, f32[1,4352]{1,0:T(1,128)}, u32[]{:S(2)}) copy-start(f32[1,4352]{1,0:T(1,128)} %get-tuple-element.208) | copy-start | bytes 52228
  399.3 31.7 %copy-start.31 = (f32[1,4352]{1,0:T(1,128)S(1)}, f32[1,4352]{1,0:T(1,128)}, u32[]{:S(2)}) copy-start(f32[1,4352]{1,0:T(1,128)} %get-tuple-element.203) | copy-start | bytes 52228
  399.3 31.7 %copy-start.32 = (f32[1,4352]{1,0:T(1,128)S(1)}, f32[1,4352]{1,0:T(1,128)}, u32[]{:S(2)}) copy-start(f32[1,4352]{1,0:T(1,128)} %get-tuple-element.205) | copy-start | bytes 52228
  651.8 8.4 %copy-start.27 = (f32[16,256]{1,0:T(8,128)S(1)}, f32[16,256]{1,0:T(8,128)}, u32[]{:S(2)}) copy-start(f32[16,256]{1,0:T(8,128)} %get-tuple-element.216) | copy-start | bytes 49156
  652.7 8.1 %copy-start.13 = (bf16[288,8704]{1,0:T(8,128)(2,1)S(1)}, bf16[288,8704]{1,0:T(8,128)(2,1)}, u32[]{:S(2)}) copy-start(bf16[288,8704]{1,0:T(8,128)(2,1)} %get-tuple-element.218) | copy-start | bytes 15040516
  (15 other events, 17.9 us)

commit v5 on v4

--- a/solution.py
+++ b/solution.py
@@ -167,8 +167,6 @@
             return pltpu.make_async_copy(source, target.at[at], osem.at[k])
         outs = [out(n1, n1o, save, 0), out(qkv, qkvo, save, 1), out(c, co, save, 2), out(r1, r1o, save, 3),
                 out(n2, n2o, save, 4), out(g, go, save, 5)]
-        if final:
-            outs.append(out(res, reso, save, 6))
 
         def first(at):
             n1[at, :] = (normal(x[at, :].astype(F32))[0] * vec[0:1, :] + vec[1:2, :]).astype(HALF)
@@ -235,9 +233,9 @@
             value = mul(g[...], wa[a:a + w, 0:hidden], NT) + (r1[:, at] + vec[7:8, at])
             if final:
                 res[:, at] = value
+                outs.append(out(res.at[:, pl.ds(a, w)], reso, (save, pl.ds(a, w)), 6 + a // LANES))
+                outs[-1].start()
             y[:, at] = value.astype(HALF)
-        if final:
-            outs[6].start()
         for copy in outs:
             copy.wait()
         for i in range(max(0, images - 2), images):
@@ -267,9 +265,9 @@
                 pltpu.VMEM((T, 3 * D), HALF), pltpu.VMEM((2, HEADS, tok, tok), HALF), pltpu.VMEM((T, D), HALF),
                 pltpu.VMEM((T, D), F32), pltpu.VMEM((T, D), HALF), pltpu.VMEM((T, hidden), HALF),
                 pltpu.VMEM((2, T, TILE), HALF), pltpu.VMEM((T, D), F32),
-                dma((len(cut) + 3,)), dma((2,)), dma((2,)), dma((7,))]),
+                dma((len(cut) + 3,)), dma((2,)), dma((2,)), dma((6 + len(pieces(D, LANES)),))]),
         input_output_aliases=aliases,
-        compiler_params=params(60),
+        compiler_params=params(64),
         cost_estimate=pl.CostEstimate(flops=T * D, bytes_accessed=T * D, transcendentals=0),
     )(slots, *ins)
 
@@ -313,8 +311,6 @@
         def out(source, target, at, k):
             return pltpu.make_async_copy(source, target.at[at], osem.at[k])
         outs = [out(du, duo, save, 0), out(low, lowo, save, 1), out(dqkv, dqkvo, save, 2)]
-        if final:
-            outs.append(out(dr1, reso, save, 3))
 
         def probs(i):
             return pltpu.make_async_copy(PP.at[slot[0] * images + i], P.at[i % 2], psem.at[i % 2])
@@ -387,9 +383,12 @@
             stats[5] += fold(g)
             stats[6] += fold(dqkv[at, 0:D].astype(F32))
             stats[7] += fold(dqkv[at, 2 * D:3 * D].astype(F32))
-        row_loop(T, tok, first)
-        if final:
-            outs[3].start()
+        for i in range(images):
+            at = pl.ds(i * tok, tok)
+            first(at)
+            if final:
+                outs.append(out(dr1.at[at], reso, pl.ds(pl.multiple_of(slot[0] * T + i * tok, 16), tok), 3 + i))
+                outs[-1].start()
         for copy in outs:
             copy.wait()
 
@@ -413,9 +412,9 @@
                 pltpu.VMEM((T, D), F32), pltpu.VMEM((T, 3 * D), HALF), pltpu.VMEM((2, HEADS, tok, tok), HALF),
                 pltpu.VMEM((T, hidden), HALF), pltpu.VMEM((T, D), F32), pltpu.VMEM((T, D), F32), pltpu.VMEM((T, D), HALF),
                 pltpu.VMEM((T, D), HALF), pltpu.VMEM((T, 3 * D), HALF),
-                dma((2 + len(pieces(hidden, 2 * TILE)),)), dma((2,)), dma((4 + len(pieces(hidden, 2 * TILE)),)), dma((4,))]),
+                dma((2 + len(pieces(hidden, 2 * TILE)),)), dma((2,)), dma((4 + len(pieces(hidden, 2 * TILE)),)), dma((3 + images,))]),
         input_output_aliases=aliases,
-        compiler_params=params(60),
+        compiler_params=params(64),
         cost_estimate=pl.CostEstimate(flops=T * D, bytes_accessed=T * D, transcendentals=0),
     )(slots, *ins)
 

time: 671 us -> 667 us (level)
  transfers between devices with their start and end apart: 6 -> 6, of which waited for: 2 -> 4; matrix products, arithmetic and copies ran while one was open for 0% -> 0% of each run, Pallas kernels for 21% -> 21%
where the time goes in v5:
time: 667 us; the launch traced here: 662 us
  Pallas kernels  578 us (87%)
  waiting for transfers between devices  46.9 us (7%)
  other arithmetic  16.1 us (2%)
  starting transfers between devices  10.4 us (2%)
  local copies, waits for them, and re-layouts  9.73 us (1%)
    pallas_call x1, Pallas kernels, reduce_grads(): pl.pallas_call(functools.partial(reduce_kernel, n, R, chunks), out_shape=...  219 us
    pallas_call x1, Pallas kernels, gather_weights(): pl.pallas_call(functools.partial(gather_kernel, n, R, halves), out_shape=...  153 us
    pallas_call x6, Pallas kernels, d_layer(): pl.pallas_call(kernel, out_shape=(shape(total, hidden, HALF), shape(total...  115 us
    pallas_call x6, Pallas kernels, f_layer(): pl.pallas_call(kernel, out_shape=(shape(total, D, HALF), shape(total, 3 *...  90.1 us
    ppermute x6, waiting for transfers between devices, shifted(): lax.ppermute(value, axis, [(source, source + steps) for source in range(f...  46.9 us
  transfers between devices with their start and end apart: 6, of which 4 were waited for; matrix products, arithmetic and copies ran while one was open for 0% of the time, Pallas kernels for 21%

profile of v5, /device:TPU:1, one launch (start us, length us, event | category | flops | bytes accessed | tf_op | source)
XLA Modules:
  0.0 661.9 jit_solution(14934662160666770955)
XLA Ops:
  0.7 3.1 fusion.3
  5.7 153.3 %shard_map.228 = (bf16[1152,13312]{1,0:T(8,128)(2,1)}, f32[8,1152]{1,0:T(8,128)S(1)}, f32[1,3456]{1,0:T(1,128)S(1)}, f32[1,4352]{1,0:T(1,128)S(1)}) custom-call(bf16[288,3456]{1,0:T(8,128)(2,1)S(1)} %bitcast.37, bf16[288,1152]{1,0:T(8,128)(2,1)S(1)} %bitcast.38, bf16[288,4352]{1,0:T(8,128)(2,1)S(1)} %pad.11.up, bf16[288,4352]{1,0:T(8,128)(2,1)S(1)} %pad.12.down, ...), custom_call_target="tpu_custom_call" | custom-call | tf_op jit(solution)/shard_map/pallas_call | solution.py:587
  160.8 25.8 %shard_map.229 = (bf16[960,1152]{1,0:T(8,128)(2,1)}, bf16[960,3456]{1,0:T(8,128)(2,1)}, bf16[6,16,160,160]{3,2,1,0:T(8,128)(2,1)}, bf16[960,1152]{1,0:T(8,128)(2...) custom-call(s32[2]{0:T(128)} %pad_add_fusion.5.slot, ...), custom_call_target="tpu_custom_call" | custom-call | flops 368640 | bytes 368640 | tf_op jit(solution)/shard_map/pallas_call | solution.py:255
  186.6 2.2 collective-permute-start.2
  189.4 25.5 %shard_map.230 = (bf16[960,1152]{1,0:T(8,128)(2,1)}, bf16[960,3456]{1,0:T(8,128)(2,1)}, bf16[6,16,160,160]{3,2,1,0:T(8,128)(2,1)}, bf16[960,1152]{1,0:T(8,128)(2...) custom-call(s32[2]{0:T(128)} %get-tuple-element.233.slot, ...), custom_call_target="tpu_custom_call", output_to_operand_aliasing={{0}: (6, {}), {1}: (7, {}), {2}: (8, {}), {3}: (9, {}), {4}... | custom-call | flops 368640 | bytes 368640 | tf_op jit(solution)/shard_map/pallas_call | solution.py:255
  214.9 2.2 collective-permute-start.1
  217.1 25.5 %shard_map.231 = (bf16[960,1152]{1,0:T(8,128)(2,1)}, bf16[960,3456]{1,0:T(8,128)(2,1)}, bf16[6,16,160,160]{3,2,1,0:T(8,128)(2,1)}, bf16[960,1152]{1,0:T(8,128)(2...) custom-call(s32[2]{0:T(128)} %get-tuple-element.232.slot, ...), custom_call_target="tpu_custom_call", output_to_operand_aliasing={{0}: (6, {}), {1}: (7, {}), {2}: (8, {}), {3}: (9, {}), {4}... | custom-call | flops 368640 | bytes 368640 | tf_op jit(solution)/shard_map/pallas_call | solution.py:255
  242.6 2.2 collective-permute-start
  246.5 3.0 shard_map.232
  249.5 7.0 %shard_map.233 = (bf16[960,1152]{1,0:T(8,128)(2,1)}, bf16[960,3456]{1,0:T(8,128)(2,1)}, bf16[6,16,160,160]{3,2,1,0:T(8,128)(2,1)}, bf16[960,1152]{1,0:T(8,128)(2...) custom-call(s32[2]{0:T(128)} %pad_add_fusion.2.slot, ...), custom_call_target="tpu_custom_call", output_to_operand_aliasing={{0}: (6, {}), {1}: (7, {}), {2}: (8, {}), {3}: (9, {}), {4}... | custom-call | flops 368640 | bytes 368640 | tf_op jit(solution)/shard_map/pallas_call | solution.py:255
  256.6 3.8 collective-permute-done.refs_0_.refs_1_
  260.4 3.3 shard_map.234
  263.7 10.1 %shard_map.235 = (bf16[960,4352]{1,0:T(8,128)(2,1)}, bf16[960,1152]{1,0:T(8,128)(2,1)}, bf16[960,3456]{1,0:T(8,128)(2,1)}, f32[960,1152]{1,0:T(8,128)}, bf16[320...) custom-call(s32[2]{0:T(128)} %pad_add_fusion.4.slot, ...), custom_call_target="tpu_custom_call", output_to_operand_aliasing={{3}: (9, {})} | custom-call | flops 368640 | bytes 368640 | tf_op jit(solution)/shard_map/pallas_call | solution.py:403
  275.0 8.6 %shard_map.236 = (bf16[960,4352]{1,0:T(8,128)(2,1)}, bf16[960,1152]{1,0:T(8,128)(2,1)}, bf16[960,3456]{1,0:T(8,128)(2,1)}, f32[960,1152]{1,0:T(8,128)}, bf16[320...) custom-call(s32[2]{0:T(128)} %pad_add_fusion.2.slot, ...), custom_call_target="tpu_custom_call", output_to_operand_aliasing={{0}: (9, {}), {1}: (10, {}), {2}: (11, {}), {3}: (12, {})} | custom-call | flops 368640 | bytes 368640 | tf_op jit(solution)/shard_map/pallas_call | solution.py:403
  285.0 8.7 %shard_map.237 = (bf16[960,4352]{1,0:T(8,128)(2,1)}, bf16[960,1152]{1,0:T(8,128)(2,1)}, bf16[960,3456]{1,0:T(8,128)(2,1)}, f32[960,1152]{1,0:T(8,128)}, bf16[320...) custom-call(s32[2]{0:T(128)} %pad_add_fusion.slot, ...), custom_call_target="tpu_custom_call", output_to_operand_aliasing={{0}: (9, {}), {1}: (10, {}), {2}: (11, {}), {3}: (12, {})} | custom-call | flops 368640 | bytes 368640 | tf_op jit(solution)/shard_map/pallas_call | solution.py:403
  294.9 40.4 %collective-permute-done.5.refs_0_ = bf16[320,1152]{1,0:T(8,128)(2,1)} collective-permute-done((bf16[320,1152]{1,0:T(8,128)(2,1)}, bf16[320,1152]{1,0:T(8,128)(2,1)}, u32[]{:S(2)}, u32[]{:S(2)}) %collective-permute-start.5) | collective-permute-done | bytes 737312 | tf_op jit(solution)/shard_map/ppermute | solution.py:1057
  335.3 29.4 %shard_map.238 = (bf16[960,4352]{1,0:T(8,128)(2,1)}, bf16[960,1152]{1,0:T(8,128)(2,1)}, bf16[960,3456]{1,0:T(8,128)(2,1)}, f32[960,1152]{1,0:T(8,128)}, bf16[320...) custom-call(s32[2]{0:T(128)} %pad_add_fusion.5.slot, ...), custom_call_target="tpu_custom_call", output_to_operand_aliasing={{0}: (9, {}), {1}: (10, {}), {2}: (11, {}), {3}: (12, {})} | custom-call | flops 368640 | bytes 368640 | tf_op jit(solution)/shard_map/pallas_call | solution.py:403
  365.8 29.1 %shard_map.239 = (bf16[960,4352]{1,0:T(8,128)(2,1)}, bf16[960,1152]{1,0:T(8,128)(2,1)}, bf16[960,3456]{1,0:T(8,128)(2,1)}, f32[960,1152]{1,0:T(8,128)}, bf16[320...) custom-call(s32[2]{0:T(128)} %get-tuple-element.233.slot, ...), custom_call_target="tpu_custom_call", output_to_operand_aliasing={{0}: (9, {}), {1}: (10, {}), {2}: (11, {}), {3}: (12, {})} | custom-call | flops 368640 | bytes 368640 | tf_op jit(solution)/shard_map/pallas_call | solution.py:403
  394.9 1.5 collective-permute-done.3.refs_0_.refs_2_
  396.5 29.3 %shard_map.240 = (bf16[960,4352]{1,0:T(8,128)(2,1)}, bf16[960,1152]{1,0:T(8,128)(2,1)}, bf16[960,3456]{1,0:T(8,128)(2,1)}, f32[960,1152]{1,0:T(8,128)}, bf16[320...) custom-call(s32[2]{0:T(128)} %get-tuple-element.232.slot, ...), custom_call_target="tpu_custom_call", output_to_operand_aliasing={{0}: (9, {}), {1}: (10, {}), {2}: (11, {}), {3}: (12, {})} | custom-call | flops 368640 | bytes 368640 | tf_op jit(solution)/shard_map/pallas_call | solution.py:403
  429.0 219.0 %shard_map.241 = (bf16[288,4608]{1,0:T(8,128)(2,1)}, bf16[288,8704]{1,0:T(8,128)(2,1)}, f32[16,256]{1,0:T(8,128)}) custom-call(f32[4,16,256]{2,1,0:T(8,128)} %bitcast.53, bf16[960,1152]{1,0:T(8,128)(2,1)} %get-tuple-element.209.n1, bf16[960,1152]{1,0:T(8,128)(2,1)} %get-tuple-element.210.c, bf16[960,1152]{1,0:T(8,128)(2,1)} %get-tuple-element.211.n2, ...), custom_call_target="tpu_custom_call" | custom-call | tf_op jit(solution)/shard_map/pallas_call | solution.py:1026
  650.1 2.6 bitcast_convert_fusion.2
  652.6 3.7 bitcast_convert_fusion.1
  657.0 4.7 convert_bitcast_fusion
  (65 shorter events, 16.8 us)
Async XLA Ops:
  0.6 3.2 copy-start.14
  0.7 3.9 copy-start.15
  3.8 1.7 copy-start.1
  3.8 1.9 copy-start.2
  3.8 1.9 copy-start.5
  3.8 1.9 copy-start.6
  3.8 1.9 copy-start.7
  3.8 1.8 copy-start.8
  3.9 1.8 copy-start.9
  3.9 1.8 copy-start.10
  3.9 1.8 copy-start.11
  3.9 1.8 copy-start.12
  159.0 0.6 copy-start
  159.6 0.6 copy-start.3
  160.2 0.6 copy-start.4
  186.6 59.9 %collective-permute-start.2 = (bf16[320,1152]{1,0:T(8,128)(2,1)}, bf16[320,1152]{1,0:T(8,128)(2,1)}, u32[]{:S(2)}, u32[]{:S(2)}) collective-permute-start(bf16[320,1152]{1,0:T(8,128)(2,1)} %get-tuple-element.140), channel_id=1, source_target_pairs={{0,16},{1,17},{2,18},{3,19},{4,20},{5,21},{6,22},{7,23},{8,24},{9,... | collective-permute-start | bytes 2211848 | tf_op jit(solution)/shard_map/ppermute | solution.py:1057
  214.9 34.6 %collective-permute-start.1 = (bf16[320,1152]{1,0:T(8,128)(2,1)}, bf16[320,1152]{1,0:T(8,128)(2,1)}, u32[]{:S(2)}, u32[]{:S(2)}) collective-permute-start(bf16[320,1152]{1,0:T(8,128)(2,1)} %get-tuple-element.139), channel_id=1, source_target_pairs={{0,16},{1,17},{2,18},{3,19},{4,20},{5,21},{6,22},{7,23},{8,24},{9,... | collective-permute-start | bytes 2211848 | tf_op jit(solution)/shard_map/ppermute | solution.py:1057
  242.6 17.8 %collective-permute-start = (bf16[320,1152]{1,0:T(8,128)(2,1)}, bf16[320,1152]{1,0:T(8,128)(2,1)}, u32[]{:S(2)}, u32[]{:S(2)}) collective-permute-start(bf16[320,1152]{1,0:T(8,128)(2,1)} %get-tuple-element.138), channel_id=1, source_target_pairs={{0,16},{1,17},{2,18},{3,19},{4,20},{5,21},{6,22},{7,23},{8,24},{9,... | collective-permute-start | bytes 2211848 | tf_op jit(solution)/shard_map/ppermute | solution.py:1057
  273.7 61.6 %collective-permute-start.5 = (bf16[320,1152]{1,0:T(8,128)(2,1)}, bf16[320,1152]{1,0:T(8,128)(2,1)}, u32[]{:S(2)}, u32[]{:S(2)}) collective-permute-start(bf16[320,1152]{1,0:T(8,128)(2,1)} %get-tuple-element.183), channel_id=1, source_target_pairs={{16,0},{17,1},{18,2},{19,3},{20,4},{21,5},{22,6},{23,7},{24,8},{25... | collective-permute-start | bytes 2211848 | tf_op jit(solution)/shard_map/ppermute | solution.py:1057
  283.7 82.2 %collective-permute-start.4 = (bf16[320,1152]{1,0:T(8,128)(2,1)}, bf16[320,1152]{1,0:T(8,128)(2,1)}, u32[]{:S(2)}, u32[]{:S(2)}) collective-permute-start(bf16[320,1152]{1,0:T(8,128)(2,1)} %get-tuple-element.182), channel_id=1, source_target_pairs={{16,0},{17,1},{18,2},{19,3},{20,4},{21,5},{22,6},{23,7},{24,8},{25... | collective-permute-start | bytes 2211848 | tf_op jit(solution)/shard_map/ppermute | solution.py:1057
  293.6 102.8 %collective-permute-start.3 = (bf16[320,1152]{1,0:T(8,128)(2,1)}, bf16[320,1152]{1,0:T(8,128)(2,1)}, u32[]{:S(2)}, u32[]{:S(2)}) collective-permute-start(bf16[320,1152]{1,0:T(8,128)(2,1)} %get-tuple-element.181), channel_id=1, source_target_pairs={{16,0},{17,1},{18,2},{19,3},{20,4},{21,5},{22,6},{23,7},{24,8},{25... | collective-permute-start | bytes 2211848 | tf_op jit(solution)/shard_map/ppermute | solution.py:1057
  648.0 8.4 %copy-start.16 = (f32[16,256]{1,0:T(8,128)S(1)}, f32[16,256]{1,0:T(8,128)}, u32[]{:S(2)}) copy-start(f32[16,256]{1,0:T(8,128)} %get-tuple-element.216) | copy-start | bytes 49156
  648.9 8.1 %copy-start.13 = (bf16[288,8704]{1,0:T(8,128)(2,1)S(1)}, bf16[288,8704]{1,0:T(8,128)(2,1)}, u32[]{:S(2)}) copy-start(bf16[288,8704]{1,0:T(8,128)(2,1)} %get-tuple-element.218) | copy-start | bytes 15040516
